TPU v7x, 256 devices: a whole 4x4x8 slice. The times are simulated.
256 devices in a mesh: dp: 8 (over x, core), row: 8 (over z), col: 4 (over y).
Axes of the slice: x: 4, y: 4, z: 8, core: 2. Of those that a mesh axis runs over, the one named last changes fastest.
Arguments:
- tokens: bfloat16 [2048, 8192], P('dp', 'row'), may hold values from -0.119628906 to 0.119628906
- upstream: bfloat16 [2048, 14848], P('dp', 'col'), may hold values from -6 to 6
- weight: bfloat16 [8192, 14848], P('row', 'col'), may hold values from -0.0625 to 0.0625
- factor_b: bfloat16 [8192, 32], P('row'), may hold values from -0.0625 to 0.0625
- factor_a: bfloat16 [32, 14848], P(None, 'col'), may hold values from -0.046875 to 0.046875
- magnitude: float32 [14848], P('col'), may hold values from 0.5 to 2
Outputs:
- grad_tokens: bfloat16 [2048, 8192], P('dp', ('row', 'col'))
- grad_magnitude: float32 [14848], P('col')
- grad_a: float32 [32, 14848], P(None, 'col')
- grad_b: float32 [8192, 32], P('row')
All inputs are finite; a program needn't handle non-finite values.
Results may differ from a plain program's by a relative error of at most 0.0049.
Values sent between devices are 32-bit elements; how exact they have to be, the bound alone decides.
No kernel may reach another device: no remote copies, remote signals or barrier semaphores. Data moves between devices by JAX's collectives and lax.ppermute only.
A program may use at most 128 MiB of HBM per device.

v0:
```python
import jax
import jax.numpy as jnp
from jax import lax
from jax.sharding import PartitionSpec as P

SCALE = 2.0
EPS = 1e-06


def shards(tokens, upstream, weight, factor_b, factor_a, magnitude):
    dp_count = lax.axis_size("dp")
    merged_raw = weight.astype(jnp.float32) + SCALE * jnp.dot(
        factor_b, factor_a, preferred_element_type=jnp.float32
    )
    normsq_part = jnp.sum(merged_raw * merged_raw, 0)
    outer = jnp.dot(tokens.T, upstream, preferred_element_type=jnp.float32)
    along_part = jnp.sum(outer * merged_raw, 0)
    normsq_sum = lax.psum(normsq_part, "row")
    along = lax.psum(along_part, ("dp", "row"))
    normsq = normsq_sum + EPS
    ratio = magnitude / jnp.sqrt(normsq)
    merged = (merged_raw * ratio).astype(jnp.bfloat16)
    grad_cols = lax.psum_scatter(
        lax.dot_general(
            merged, upstream, (((1,), (1,)), ((), ())), preferred_element_type=jnp.float32
        ),
        "col",
        scatter_dimension=0,
        tiled=True,
    )
    grad_tokens = grad_cols.T.astype(jnp.bfloat16)
    grad_magnitude = along / jnp.sqrt(normsq)
    grad_merged = (ratio * (outer - merged_raw * (along / (normsq * dp_count)))).astype(
        jnp.bfloat16
    )
    a_part = SCALE * jnp.dot(factor_b.T, grad_merged, preferred_element_type=jnp.float32)
    grad_a = lax.psum(a_part, ("dp", "row"))
    b_part = SCALE * jnp.dot(grad_merged, factor_a.T, preferred_element_type=jnp.float32)
    grad_b = lax.psum(b_part, ("dp", "col"))
    return (grad_tokens, grad_magnitude, grad_a, grad_b)


def solution(mesh):
    placed = (
        P("dp", "row"),
        P("dp", "col"),
        P("row", "col"),
        P("row", None),
        P(None, "col"),
        P("col"),
    )
    return jax.shard_map(
        shards,
        mesh=mesh,
        in_specs=placed,
        out_specs=(P("dp", ("row", "col")), P("col"), P(None, "col"), P("row", None)),
        check_vma=False,
    )
```

profile of v0, /device:TPU:1, one launch (start us, length us, event | category | flops | bytes accessed | tf_op | source)
XLA Modules:
  0.0 627.8 jit_solution(16673390379533651434)
XLA Ops:
  8.0 0.0 copy-start
  8.0 0.0 copy-start.3
  8.0 0.0 reduce-scatter.2.cloned.1.call-start
  8.1 5.6 multiply_add_fusion
  13.7 0.0 copy-done
  13.7 0.0 copy-done.3
  13.7 0.0 copy-start.1
  13.7 0.0 copy-start.6
  13.7 7.3 %multiply_reduce_fusion = (f32[3712]{0:T(1024)S(1)}, f32[3712]{0:T(1024)S(1)}, f32[1024,3712]{1,0:T(8,128)}) fusion(f32[1024,3712]{1,0:T(8,128)S(1)} %multiply_add_fusion, bf16[256,1024]{1,0:T(8,128)(2,1)S(1)} %copy-done.3, bf16[256,3712]{1,0:T(8,128)(2,1)S(1)} %copy-done), kind=kOutput, calls=%fused_computation.1 | convolution fusion | flops 1961353984 | bytes 32863232 | tf_op jit(solution)/shard_map/dot_general | solution.py:16
  21.1 2.5 copy-done.1
  23.6 246.1 %psum.29 = f32[3712]{0:T(1024)S(1)} all-reduce(f32[3712]{0:T(1024)S(1)} %get-tuple-element.8), channel_id=1, replica_groups=mesh['dp'=8,'row'=8,'col'=4] {'dp','row'}, use_global_device_ids=true, to_apply=%region_4.0 | all-reduce | flops 3712 | bytes 29696 | tf_op jit(solution)/shard_map/psum | solution.py:19
  269.7 20.2 %psum.28 = f32[3712]{0:T(1024)S(1)} all-reduce(f32[3712]{0:T(1024)S(1)} %get-tuple-element.9), channel_id=1, replica_groups=mesh['dp'=8,'row'=8,'col'=4] {'row'}, use_global_device_ids=true, to_apply=%region_1.0 | all-reduce | flops 3712 | bytes 29696 | tf_op jit(solution)/shard_map/psum | solution.py:18
  289.9 0.0 copy-done.6
  289.9 0.6 multiply_divide_fusion
  290.5 8.5 %fusion = f32[1024,256]{1,0:T(8,128)} fusion(bf16[256,3712]{1,0:T(8,128)(2,1)S(1)} %copy-done, f32[1024,3712]{1,0:T(8,128)} %copy-done.1, f32[3712]{0:T(1024)S(1)} %get-tuple-element.12), kind=kOutput, calls=%fused_computation.5 | convolution fusion | flops 1953759232 | bytes 18168320 | tf_op jit(solution)/shard_map/dot_general | solution.py:24
  299.1 0.0 reduce-scatter.2.cloned.1.call-update
  299.1 0.0 all-reduce.5.cloned.1.call-start
  299.1 0.0 copy-start.4
  299.2 0.0 copy-start.5
  299.2 10.5 %multiply_convert_fusion = bf16[1024,3712]{1,0:T(8,128)(2,1)S(1)} fusion(f32[1024,3712]{1,0:T(8,128)} %get-tuple-element.13, f32[1024,3712]{1,0:T(8,128)} %copy-done.1, f32[3712]{0:T(1024)S(1)} %get-tuple-element.10, f32[3712]{0:T(1024)S(1)} %get-tuple-element.12), kind=kLoop, calls=%fused_computation | loop fusion | flops 15204352 | bytes 38040576 | tf_op jit(solution)/shard_map/convert_element_type | solution.py:33
  309.7 0.0 copy-start.2
  309.7 3.0 copy-done.2
  312.7 0.0 copy-done.4
  312.7 3.0 convolution_multiply_fusion.1
  315.7 0.0 all-reduce.5.cloned.1.call-update
  315.7 0.0 all-reduce.3.cloned.1.call-start
  315.8 0.0 copy-done.5
  315.8 5.3 fusion.2
  321.2 0.0 all-reduce.3.cloned.1.call-update
  321.2 12.8 %reduce-scatter.2.cloned.1.call-done = f32[256,256]{1,0:T(8,128)} async-done(((f32[1024,256]{1,0:T(8,128)}), f32[256,256]{1,0:T(8,128)}) %reduce-scatter.2.cloned.1.call-update) | async-done | bytes 262160 | tf_op jit(solution)/shard_map/reduce_scatter | solution.py:23
  334.0 1.0 convert_bitcast_fusion
  335.0 0.8 copy.10
  335.7 99.9 %all-reduce.5.cloned.1.call-done = f32[1024,32]{0,1:T(8,128)} async-done(((f32[1024,32]{0,1:T(8,128)}), f32[1024,32]{0,1:T(8,128)}) %all-reduce.5.cloned.1.call-update) | async-done | bytes 131088 | tf_op jit(solution)/shard_map/psum | solution.py:39
  435.6 181.4 %all-reduce.3.cloned.1.call-done = f32[32,3712]{1,0:T(8,128)} async-done(((f32[32,3712]{1,0:T(8,128)}), f32[32,3712]{1,0:T(8,128)}) %all-reduce.3.cloned.1.call-update) | async-done | bytes 475152 | tf_op jit(solution)/shard_map/psum | solution.py:37
  617.0 1.8 copy.13
  618.8 1.6 copy.14
Async XLA Ops:
  8.0 5.7 copy-start
  8.0 5.7 copy-start.3
  8.0 326.0 %reduce-scatter.2.cloned.1.call-start = ((), (), s32[]{:S(2)}) async-start(), calls=%async_computation.1 | async-start | bytes 1310720 | tf_op jit(solution)/shard_map/reduce_scatter | solution.py:23
  13.7 9.9 %copy-start.1 = (f32[1024,3712]{1,0:T(8,128)}, f32[1024,3712]{1,0:T(8,128)S(1)}, u32[]{:S(2)}) copy-start(f32[1024,3712]{1,0:T(8,128)S(1)} %multiply_add_fusion) | copy-start | bytes 45613060
  13.7 276.2 %copy-start.6 = (f32[3712]{0:T(1024)S(1)}, f32[3712]{0:T(1024)}, u32[]{:S(2)}) copy-start(f32[3712]{0:T(1024)} %param.11) | copy-start | bytes 44548
  299.1 136.6 %all-reduce.5.cloned.1.call-start = ((), (), s32[]{:S(2)}) async-start(), calls=%async_computation.3 | async-start | bytes 262144 | tf_op jit(solution)/shard_map/psum | solution.py:39
  299.1 13.6 %copy-start.4 = (bf16[32,3712]{1,0:T(8,128)(2,1)S(1)}, bf16[32,3712]{1,0:T(8,128)(2,1)}, u32[]{:S(2)}) copy-start(bf16[32,3712]{1,0:T(8,128)(2,1)} %param.10) | copy-start | bytes 712708
  299.2 16.6 %copy-start.5 = (bf16[1024,32]{0,1:T(8,128)(2,1)S(1)}, bf16[1024,32]{0,1:T(8,128)(2,1)}, u32[]{:S(2)}) copy-start(bf16[1024,32]{0,1:T(8,128)(2,1)} %param.9) | copy-start | bytes 196612
  309.7 3.0 copy-start.2
  315.7 301.3 %all-reduce.3.cloned.1.call-start = ((), (), s32[]{:S(2)}) async-start(), calls=%async_computation.2 | async-start | bytes 950272 | tf_op jit(solution)/shard_map/psum | solution.py:37
Sparse Core Ops, SparseCore 0:
  299.2 34.7 reduce-scatter.1
Sparse Core Ops, SparseCore 1:
  315.8 119.8 all-reduce.4
  439.6 177.4 all-reduce.2
where the time goes:
time: 628 us
  waiting for transfers between devices  294 us (47%)
  blocking collectives  266 us (42%)
  matrix products  29.8 us (5%)
  between operations  15.6 us (2%)
  other arithmetic  12.1 us (2%)
  local copies, waits for them, and re-layouts  9.72 us (2%)
    psum x1, blocking collectives, shards(): along = lax.psum(along_part, ('dp', 'row'))  246 us
    psum x1, waiting for transfers between devices, shards(): grad_a = lax.psum(a_part, ('dp', 'row'))  181 us
    psum x1, waiting for transfers between devices, shards(): grad_b = lax.psum(b_part, ('dp', 'col'))  99.9 us
    psum x1, blocking collectives, shards(): normsq_sum = lax.psum(normsq_part, 'row')  20.2 us
    reduce_scatter x1, waiting for transfers between devices, shards(): lax.psum_scatter(lax.dot_general(merged, upstream, (((1,), (1,)), ((), ()...  12.8 us
  transfers between devices with their start and end apart: 3, of which 3 were waited for; matrix products, arithmetic and copies ran while one was open for 3% of the time, Pallas kernels for 0%

commit v1 on v0

v1 whole, which is shorter than its diff:
```python
import jax
import jax.numpy as jnp
from jax import lax
from jax.experimental import pallas as pl
from jax.experimental.pallas import tpu as pltpu
from jax.sharding import PartitionSpec as P

SCALE = 2.0
EPS = 1e-06

TOK, ROWS, COLS, RANK = 256, 1024, 3712, 32
CW = 512
NC = 8
WIDTHS = [min(CW, COLS - CW * c) for c in range(NC)]
PW = CW + 128
PH = 40
X_GROUPS = [[0, 2, 4, 6], [1, 3, 5, 7]]
CORE_FLIP = [(i, i ^ 1) for i in range(8)]
F32, BF16 = jnp.float32, jnp.bfloat16
NN = (((1,), (0,)), ((), ()))
NT = (((1,), (1,)), ((), ()))
TN = (((0,), (0,)), ((), ()))

VMEM = pl.BlockSpec(memory_space=pltpu.VMEM)
SMEM = pl.BlockSpec(memory_space=pltpu.SMEM)
HBM = pl.BlockSpec(memory_space=pl.ANY)


def mm(a, b, dims):
    return lax.dot_general(a, b, dims, preferred_element_type=F32)


def span(c):
    return pl.ds(CW * c, WIDTHS[c])


def fetch(w_hbm, u_hbm, w_v, u_v, sems):
    copies = []
    for c in range(NC):
        pair = (
            pltpu.make_async_copy(w_hbm.at[:, span(c)], w_v.at[:, span(c)], sems.at[0, c]),
            pltpu.make_async_copy(u_hbm.at[:, span(c)], u_v.at[:, span(c)], sems.at[1, c]),
        )
        for copy in pair:
            copy.start()
        copies.append(pair)
    return copies


def first_kernel(pos, tok_ref, bt_ref, a_ref, w_hbm, u_hbm, out, w_v, u_v, a_v, sems):
    copies = fetch(w_hbm, u_hbm, w_v, u_v, sems)
    w_v[:, COLS:] = jnp.zeros((ROWS, NC * CW - COLS), BF16)
    a_v[:, :COLS] = a_ref[...]
    a_v[:, COLS:] = jnp.zeros((RANK, NC * CW - COLS), BF16)
    out[NC - 1] = jnp.zeros((8, CW), F32)
    tok, bt = tok_ref[...], bt_ref[...]
    b2t = bt * BF16(SCALE)
    low = mm(bt, tok, NT)
    low2 = mm(tok, b2t, NT).astype(BF16)
    gram = mm(bt, b2t, NT).astype(BF16)
    for r in range(NC):
        for i in range(4):
            lane = TOK * (i % 2)
            out[r, 6 + i // 2 : 7 + i // 2, lane : lane + TOK] = low[4 * r + i : 4 * r + i + 1]
    for c in range(NC):
        for copy in copies[c]:
            copy.wait()
        n = WIDTHS[c]
        wc, ac = w_v[:, span(c)], a_v[:, span(c)]
        merged = wc.astype(F32) + mm(b2t, ac, TN)
        out[c, 0:1, :n] = jnp.sum(merged * merged, 0, keepdims=True)
        y = mm(tok, wc, NN) + mm(low2, ac, NN)
        out[c, 1:2, :n] = jnp.sum(u_v[:, span(c)].astype(F32) * y, 0, keepdims=True)
    mine = pl.ds(pl.multiple_of(pos[0] * CW, CW), CW)
    q = mm(bt, w_v[:, mine], NN) + mm(gram, a_v[:, mine], NN)
    for r in range(NC):
        out[r, 2:6, :] = q[4 * r : 4 * r + 4]


def second_kernel(
    pos, zz, mag, tok_ref, bt_ref, a_ref, w_hbm, u_hbm, keep, send, s_out, w_v, u_v, g_v, t_v, sems
):
    copies = fetch(w_hbm, u_hbm, w_v, u_v, sems)
    tok, bt = tok_ref[...], bt_ref[...]
    b2t = bt * BF16(SCALE)
    for r in range(NC):
        for i in range(4):
            lane = TOK * (i % 2)
            t_v[4 * r + i : 4 * r + i + 1, :] = zz[r, 6 + i // 2 : 7 + i // 2, lane : lane + TOK]
    low = t_v[...]
    high = low.astype(BF16)
    pair = jnp.concatenate([high, (low - high.astype(F32)).astype(BF16)], 0)
    s_sum = jnp.zeros((RANK, TOK), F32)
    va_sum = jnp.zeros((RANK, RANK), F32)
    vm_sum = jnp.zeros((RANK, ROWS), F32)
    g_v[NC - 1] = jnp.zeros((PH, PW), F32)
    for c in range(NC):
        for copy in copies[c]:
            copy.wait()
        n = WIDTHS[c]
        wc, uc, ac = w_v[:, span(c)], u_v[:, span(c)], a_ref[:, span(c)]
        normsq = zz[c, 0:1, :n] + EPS
        along = zz[c, 1:2, :n]
        ratio = mag[c : c + 1, :n] / jnp.sqrt(normsq)
        v = (ac.astype(F32) * (ratio * (along / normsq))).astype(BF16)
        scaled = (uc.astype(F32) * ratio).astype(BF16)
        s_sum = s_sum + mm(ac, scaled, NT)
        va_sum = va_sum + mm(v, ac, NT)
        vm_sum = vm_sum + mm(v, wc, NT)
        p = mm(pair, uc, NN)
        g_v[c, :RANK, :n] = (SCALE * ratio) * (p[:RANK] + p[RANK:])
        g_v[c, RANK : RANK + 1, :n] = along
        g_v[c, RANK + 1 :, :] = jnp.zeros((PH - RANK - 1, PW), F32)
        g_v[c, RANK : RANK + 1, CW:] = jnp.zeros((1, PW - CW), F32)
    s_out[...] = s_sum
    gb = mm(s_sum.astype(BF16), tok, NN) - vm_sum - mm(va_sum.astype(BF16), b2t, NN)
    gb = SCALE * gb
    for c in range(NC):
        g_v[c, :RANK, CW:] = gb[:, 128 * c : 128 * (c + 1)]
    core = pos[1]
    for x in range(4):
        keep[x] = g_v[2 * x + core]
        send[x] = g_v[2 * x + 1 - core]


def third_kernel(
    pos, zz, mag, s_ref, bt_ref, w_hbm, u_hbm, o0, o1, o2, o3, w_v, u_v, acc, sems
):
    copies = fetch(w_hbm, u_hbm, w_v, u_v, sems)
    b2t = bt_ref[...] * BF16(SCALE)
    acc[...] = mm(s_ref[...].astype(BF16), b2t, TN)
    for c in range(NC):
        for copy in copies[c]:
            copy.wait()
        n = WIDTHS[c]
        ratio = mag[c : c + 1, :n] / jnp.sqrt(zz[c, 0:1, :n] + EPS)
        scaled = (u_v[:, span(c)].astype(F32) * ratio).astype(BF16)
        acc[...] += mm(scaled, w_v[:, span(c)], NT)
    for d, o in enumerate((o0, o1, o2, o3)):
        part = lax.rem(pos[2] + d, 4)
        o[...] = acc[:, pl.ds(pl.multiple_of(part * 256, 256), 256)]


def combine_kernel(pos, y, zz, mag, pack, gb4):
    s = pos[0]
    total = (y[0] + y[1]) + (y[2] + y[3])
    mine = zz[s]
    normsq = mine[0:1] + EPS
    root = jnp.sqrt(normsq)
    ratio = mag[pl.ds(s, 1), :] / root
    along = total[RANK : RANK + 1, :CW]
    factor = (SCALE * ratio) * (along / normsq)
    for r in range(NC):
        rows = slice(4 * r, 4 * r + 4)
        pack[rows, :CW] = total[rows, :CW] - factor * zz[r, 2:6, :]
    pack[RANK : RANK + 1, :CW] = along / root
    pack[RANK + 1 :, :CW] = jnp.zeros((PH - RANK - 1, CW), F32)
    pack[:, CW:] = jnp.zeros((PH, PW - CW), F32)
    gb = total[:RANK, CW:]
    for i in range(4):
        gb4[i] = gb


def spread_kernel(pack, gb4, out):
    gb = (gb4[0] + gb4[1]) + (gb4[2] + gb4[3])
    for i in range(4):
        out[i] = pack[...]
        out[i, :RANK, CW:] = gb


def last_kernel(pos, own, other, ga, gm, gb, both):
    core = pos[1]
    for x in range(4):
        both[2 * x + core] = own[x]
        both[2 * x + 1 - core] = other[x]
    for c in range(NC):
        ga[:, span(c)] = both[c, :RANK, : WIDTHS[c]]
        gm[c : c + 1, :] = both[c, RANK : RANK + 1, :CW]
        gb[:, 128 * c : 128 * (c + 1)] = both[c, :RANK, CW:]


def call(kernel, name, ins, outs, scratch=(), cost=None, limit=48):
    shapes = [jax.ShapeDtypeStruct(shape, F32) for shape in outs]
    return pl.pallas_call(
        kernel,
        name=name,
        out_shape=shapes if len(shapes) > 1 else shapes[0],
        in_specs=ins,
        out_specs=[VMEM] * len(outs) if len(outs) > 1 else VMEM,
        scratch_shapes=list(scratch),
        cost_estimate=cost,
        compiler_params=pltpu.CompilerParams(vmem_limit_bytes=limit << 20),
    )


LOADED = (
    pltpu.VMEM((ROWS, COLS), BF16),
    pltpu.VMEM((TOK, COLS), BF16),
)
COST = pl.CostEstimate(
    flops=4 * TOK * ROWS * COLS, bytes_accessed=10_000_000, transcendentals=COLS
)


def shards(tokens, upstream, weight, factor_b, factor_a, magnitude):
    dp = lax.axis_index("dp")
    pos = jnp.stack([dp, lax.rem(dp, 2), lax.axis_index("col")]).astype(jnp.int32)
    bt = factor_b.T
    mag = jnp.pad(magnitude, (0, NC * CW - COLS)).reshape(NC, CW)
    part = call(
        first_kernel,
        "norms",
        [SMEM, VMEM, VMEM, VMEM, HBM, HBM],
        [(NC, 8, CW)],
        (
            pltpu.VMEM((ROWS, NC * CW), BF16),
            pltpu.VMEM((TOK, COLS), BF16),
            pltpu.VMEM((RANK, NC * CW), BF16),
            pltpu.SemaphoreType.DMA((2, NC)),
        ),
        COST,
    )(pos, tokens, bt, factor_a, weight, upstream)
    z = jnp.sum(lax.all_to_all(part, "row", 0, 0, tiled=True), 0)
    zz = lax.all_to_all(jnp.broadcast_to(z[None], part.shape), "row", 0, 0, tiled=True)

    keep, send, s_part = call(
        second_kernel,
        "factors",
        [SMEM, VMEM, VMEM, VMEM, VMEM, VMEM, HBM, HBM],
        [(4, PH, PW), (4, PH, PW), (RANK, TOK)],
        LOADED
        + (
            pltpu.VMEM((NC, PH, PW), F32),
            pltpu.VMEM((RANK, TOK), F32),
            pltpu.SemaphoreType.DMA((2, NC)),
        ),
        COST,
    )(pos, zz, mag, tokens, bt, factor_a, weight, upstream)
    halves = keep + lax.ppermute(send, "dp", CORE_FLIP)
    y = lax.all_to_all(halves, "dp", 0, 0, tiled=True, axis_index_groups=X_GROUPS)

    o0, o1, o2, o3 = call(
        third_kernel,
        "tokens_grad",
        [SMEM, VMEM, VMEM, VMEM, VMEM, HBM, HBM],
        [(TOK, 256)] * 4,
        LOADED + (pltpu.VMEM((TOK, ROWS), F32), pltpu.SemaphoreType.DMA((2, NC))),
        COST,
    )(pos, zz, mag, s_part, bt, weight, upstream)

    pack, gb4 = call(
        combine_kernel, "combine", [SMEM, VMEM, VMEM, VMEM], [(PH, PW), (4, RANK, 128)]
    )(pos, y, zz, mag)
    gb4 = lax.all_to_all(gb4, "col", 0, 0, tiled=True)
    gb4, o1, o2, o3 = lax.optimization_barrier((gb4, o1, o2, o3))
    arrived = [
        lax.ppermute(o, "col", [(i, (i + d) % 4) for i in range(4)])
        for d, o in ((1, o1), (2, o2), (3, o3))
    ]
    packs = call(spread_kernel, "spread", [VMEM, VMEM], [(4, PH, PW)])(pack, gb4)
    own = lax.all_to_all(packs, "dp", 0, 0, tiled=True, axis_index_groups=X_GROUPS)
    other = lax.ppermute(own, "dp", CORE_FLIP)
    grad_a, gm, gbt = call(
        last_kernel,
        "outputs",
        [SMEM, VMEM, VMEM],
        [(RANK, COLS), (NC, CW), (RANK, ROWS)],
        (pltpu.VMEM((NC, PH, PW), F32),),
    )(pos, own, other)
    grad_tokens = ((o0 + arrived[0]) + (arrived[1] + arrived[2])).astype(BF16)
    return grad_tokens, gm.reshape(-1)[:COLS], grad_a, gbt.T


def solution(mesh):
    placed = (
        P("dp", "row"),
        P("dp", "col"),
        P("row", "col"),
        P("row", None),
        P(None, "col"),
        P("col"),
    )
    return jax.shard_map(
        shards,
        mesh=mesh,
        in_specs=placed,
        out_specs=(P("dp", ("row", "col")), P("col"), P(None, "col"), P("row", None)),
        check_vma=False,
    )
```

time: 628 us -> 97.8 us (0.16)
  the two profiles are of different devices: /device:TPU:1 before, /device:TPU:2 now
where the time goes in v1:
time: 97.8 us; the launch traced here: 97.2 us
  blocking collectives  29.1 us (30%)
  Pallas kernels  22.7 us (23%)
  waiting for transfers between devices  19.9 us (20%)
  starting transfers between devices  18.2 us (19%)
  local copies, waits for them, and re-layouts  5.65 us (6%)
    all_to_all x1, blocking collectives, shards(): z = jnp.sum(lax.all_to_all(part, 'row', 0, 0, tiled=True), 0)  17.4 us
    all_to_all x1, blocking collectives, shards(): lax.all_to_all(halves, 'dp', 0, 0, tiled=True, axis_index_groups=X_GROUPS)  11.7 us
    all_to_all x1, waiting for transfers between devices, shards(): lax.all_to_all(jnp.broadcast_to(z[None], part.shape), 'row', 0, 0, tiled=...  8.95 us
    pallas_call x1, Pallas kernels, shards(): call(first_kernel, 'norms', [SMEM, VMEM, VMEM, VMEM, HBM, HBM], [(NC, 8,...  8.31 us
    ppermute x3, waiting for transfers between devices, shards(): lax.ppermute(o, 'col', [(i, (i + d) % 4) for i in range(4)])  7.86 us
    pallas_call x1, Pallas kernels, shards(): call(second_kernel, 'factors', [SMEM, VMEM, VMEM, VMEM, VMEM, VMEM, HBM,...  6.16 us
    ppermute x3, starting transfers between devices, shards(): lax.ppermute(o, 'col', [(i, (i + d) % 4) for i in range(4)])  5.39 us
    unnamed x19, local copies, waits for them, and re-layouts  4.97 us
  transfers between devices with their start and end apart: 8, of which 6 were waited for; matrix products, arithmetic and copies ran while one was open for 1% of the time, Pallas kernels for 5%

profile of v1, /device:TPU:2, one launch (start us, length us, event | category | flops | bytes accessed | tf_op | source)
XLA Modules:
  0.0 97.2 jit_solution(13655149790964327974)
XLA Ops:
  0.6 0.1 pad_add_fusion.pos
  0.7 0.0 copy-start
  0.7 1.5 %copy-done = bf16[256,3712]{1,0:T(8,128)(2,1)S(1)} copy-done((bf16[256,3712]{1,0:T(8,128)(2,1)S(1)}, bf16[256,3712]{1,0:T(8,128)(2,1)}, u32[]{:S(2)}) %copy-start) | copy-done | bytes 1900568
  2.2 0.0 copy-start.2
  2.2 1.0 %copy-done.2 = bf16[256,1024]{1,0:T(8,128)(2,1)S(1)} copy-done((bf16[256,1024]{1,0:T(8,128)(2,1)S(1)}, bf16[256,1024]{1,0:T(8,128)(2,1)}, u32[]{:S(2)}) %copy-start.2) | copy-done | bytes 524312
  3.3 0.0 copy-start.4
  3.3 0.9 copy-done.4
  4.2 0.0 copy-start.6
  4.2 0.8 copy-done.6
  5.1 0.0 copy-start.8
  5.1 0.0 copy-start.1
  5.1 0.0 copy-start.3
  5.1 0.0 copy-start.5
  5.1 0.0 copy-start.7
  5.1 8.3 %norms.1 = f32[8,8,512]{2,1,0:T(8,128)S(1)} custom-call(s32[3]{0:T(128)S(1)} %pad_add_fusion.pos, bf16[256,1024]{1,0:T(8,128)(2,1)S(1)} %copy-done.2, bf16[32,1024]{1,0:T(8,128)(2,1)S(1)} %bitcast.9, bf16[32,3712]{1,0:T(8,128)(2,1)S(1)} %copy-done.4, bf16[1024,3712]{1,0:T(8,128)(2,1)} %w_hbm.5, bf16[256,3712]{1,0:T(8,128)(2,1)S(1)} %copy-done), custom_call_target="tpu_custom_call" | custom-call | flops 3892314112 | bytes 10000000 | tf_op jit(solution)/shard_map/norms/pallas_call | solution.py:210
  13.4 17.4 %all_to_all.25 = f32[8,8,512]{2,1,0:T(8,128)S(1)} all-to-all(f32[8,8,512]{2,1,0:T(8,128)S(1)} %norms.1), channel_id=1, replica_groups=mesh['dp'=8,'row'=8,'col'=4] {'row'}, dimensions={0} | all-to-all | bytes 262144 | tf_op jit(solution)/shard_map/all_to_all | solution.py:223
  30.8 0.7 broadcast_in_dim.2
  31.5 3.4 %all-to-all-start.1 = ((f32[8,8,512]{2,1,0:T(8,128)}), f32[8,8,512]{2,1,0:T(8,128)S(1)}, u32[]{:S(2)}, u32[]{:S(2)}) async-start(f32[8,8,512]{2,1,0:T(8,128)} %broadcast_in_dim.2), calls=%async_computation.1 | async-start | bytes 262144 | tf_op jit(solution)/shard_map/all_to_all | solution.py:224
  34.8 0.0 copy-done.8
  34.9 8.9 %all-to-all-done.1.zz = f32[8,8,512]{2,1,0:T(8,128)S(1)} async-done(((f32[8,8,512]{2,1,0:T(8,128)}), f32[8,8,512]{2,1,0:T(8,128)S(1)}, u32[]{:S(2)}, u32[]{:S(2)}) %all-to-all-start.1) | async-done | bytes 131104 | tf_op jit(solution)/shard_map/all_to_all | solution.py:224
  43.8 0.0 copy-done.1
  43.8 0.0 copy-done.3
  43.8 0.0 copy-done.5
  43.8 0.0 copy-done.7
  43.9 6.2 %factors.1 = (f32[4,40,640]{2,1,0:T(8,128)S(1)}, f32[4,40,640]{2,1,0:T(8,128)S(1)}, f32[32,256]{1,0:T(8,128)S(1)}) custom-call(s32[3]{0:T(128)S(1)} %pad_add_fusion.pos, f32[8,8,512]{2,1,0:T(8,128)S(1)} %all-to-all-done.1.zz, f32[8,512]{1,0:T(8,128)S(1)} %reshape.15.mag, bf16[256,1024]{1,0:T(8,128)(2,1)S(1)} %copy-done.3, bf16[32,1024]{1,0:T(8,128)(2,1)S(1)} %bitcast.10, ...), custom_call_target="tpu_custom_call" | custom-call | flops 3892314112 | bytes 10000000 | tf_op jit(solution)/shard_map/factors/pallas_call | solution.py:226
  50.0 0.1 collective-permute-start
  50.1 1.7 %collective-permute-done = f32[4,40,640]{2,1,0:T(8,128)S(1)} collective-permute-done((f32[4,40,640]{2,1,0:T(8,128)S(1)}, f32[4,40,640]{2,1,0:T(8,128)S(1)}, u32[]{:S(2)}, u32[]{:S(2)}) %collective-permute-start) | collective-permute-done | bytes 409632 | tf_op jit(solution)/shard_map/ppermute | solution.py:239
  51.9 11.7 %all_to_all.26.y = f32[4,40,640]{2,1,0:T(8,128)S(1)} all-to-all(f32[4,40,640]{2,1,0:T(8,128)S(1)} %add.14), channel_id=1, replica_groups={{0,64,128,192},{32,96,160,224},{1,65,129,193},{33,97,161,225},{2,66,130..., dimensions={0} | all-to-all | bytes 819200 | tf_op jit(solution)/shard_map/all_to_all | solution.py:240
  63.6 1.2 %combine.1 = (f32[40,640]{1,0:T(8,128)S(1)}, f32[4,32,128]{2,1,0:T(8,128)}) custom-call(s32[3]{0:T(128)S(1)} %pad_add_fusion.pos, f32[4,40,640]{2,1,0:T(8,128)S(1)} %all_to_all.26.y, f32[8,8,512]{2,1,0:T(8,128)S(1)} %all-to-all-done.1.zz, f32[8,512]{1,0:T(8,128)S(1)} %reshape.15.mag), custom_call_target="tpu_custom_call" | custom-call | tf_op jit(solution)/shard_map/combine/pallas_call | solution.py:251
  64.8 4.5 %all-to-all-start.3 = ((f32[4,32,128]{2,1,0:T(8,128)}), f32[4,32,128]{2,1,0:T(8,128)S(1)}, u32[]{:S(2)}, u32[]{:S(2)}) async-start(f32[4,32,128]{2,1,0:T(8,128)} %get-tuple-element.24), calls=%async_computation.3 | async-start | bytes 131072 | tf_op jit(solution)/shard_map/all_to_all | solution.py:254
  69.3 4.8 %tokens_grad.1 = (f32[256,256]{1,0:T(8,128)S(1)}, f32[256,256]{1,0:T(8,128)S(1)}, f32[256,256]{1,0:T(8,128)S(1)}, f32[256,256]{1,0:T(8,128)S(1)}) custom-call(s32[3]{0:T(128)S(1)} %pad_add_fusion.pos, f32[8,8,512]{2,1,0:T(8,128)S(1)} %all-to-all-done.1.zz, f32[8,512]{1,0:T(8,128)S(1)} %reshape.15.mag, f32[32,256]{1,0:T(8,128)S(1)} %get-tuple-element.20.s_ref, ...), custom_call_target="tpu_custom_call" | custom-call | flops 3892314112 | bytes 10000000 | tf_op jit(solution)/shard_map/tokens_grad/pallas_call | solution.py:242
  74.1 0.8 all-to-all-done.3.gb4
  74.9 0.8 spread.1
  75.7 4.9 %all-to-all-start.4 = ((f32[4,40,640]{2,1,0:T(8,128)}), f32[4,40,640]{2,1,0:T(8,128)S(1)}, u32[]{:S(2)}, u32[]{:S(2)}) async-start(f32[4,40,640]{2,1,0:T(8,128)} %spread.1), calls=%async_computation.4 | async-start | bytes 819200 | tf_op jit(solution)/shard_map/all_to_all | solution.py:261
  80.6 1.3 %collective-permute-start.1 = (f32[256,256]{1,0:T(8,128)S(1)}, f32[256,256]{1,0:T(8,128)S(1)}, u32[]{:S(2)}, u32[]{:S(2)}) collective-permute-start(f32[256,256]{1,0:T(8,128)S(1)} %get-tuple-element.28), channel_id=1, source_target_pairs={{0,1},{1,2},{2,3},{3,0},{4,5},{5,6},{6,7},{7,4},{8,9},{9,10},{10,1... | collective-permute-start | bytes 786440 | tf_op jit(solution)/shard_map/ppermute | solution.py:257
  81.8 2.7 %collective-permute-start.2 = (f32[256,256]{1,0:T(8,128)S(1)}, f32[256,256]{1,0:T(8,128)S(1)}, u32[]{:S(2)}, u32[]{:S(2)}) collective-permute-start(f32[256,256]{1,0:T(8,128)S(1)} %get-tuple-element.29), channel_id=1, source_target_pairs={{0,2},{1,3},{2,0},{3,1},{4,6},{5,7},{6,4},{7,5},{8,10},{9,11},{10,... | collective-permute-start | bytes 786440 | tf_op jit(solution)/shard_map/ppermute | solution.py:257
  84.5 1.5 %collective-permute-start.3 = (f32[256,256]{1,0:T(8,128)S(1)}, f32[256,256]{1,0:T(8,128)S(1)}, u32[]{:S(2)}, u32[]{:S(2)}) collective-permute-start(f32[256,256]{1,0:T(8,128)S(1)} %get-tuple-element.30), channel_id=1, source_target_pairs={{0,3},{1,0},{2,1},{3,2},{4,7},{5,4},{6,5},{7,6},{8,11},{9,8},{10,9... | collective-permute-start | bytes 786440 | tf_op jit(solution)/shard_map/ppermute | solution.py:257
  86.0 0.6 all-to-all-done.4.own
  86.6 0.0 collective-permute-start.4
  86.6 3.8 %collective-permute-done.1 = f32[256,256]{1,0:T(8,128)S(1)} collective-permute-done((f32[256,256]{1,0:T(8,128)S(1)}, f32[256,256]{1,0:T(8,128)S(1)}, u32[]{:S(2)}, u32[]{:S(2)}) %collective-permute-start.1) | collective-permute-done | bytes 262176 | tf_op jit(solution)/shard_map/ppermute | solution.py:257
  90.4 4.1 %collective-permute-done.2 = f32[256,256]{1,0:T(8,128)S(1)} collective-permute-done((f32[256,256]{1,0:T(8,128)S(1)}, f32[256,256]{1,0:T(8,128)S(1)}, u32[]{:S(2)}, u32[]{:S(2)}) %collective-permute-start.2) | collective-permute-done | bytes 262176 | tf_op jit(solution)/shard_map/ppermute | solution.py:257
  94.4 0.0 collective-permute-done.3
  94.4 0.7 add_convert_fusion
  95.2 0.0 collective-permute-done.4.other
  95.2 1.5 %outputs.1 = (f32[32,3712]{1,0:T(8,128)}, f32[8,512]{1,0:T(8,128)S(1)}, f32[32,1024]{1,0:T(8,128)}) custom-call(s32[3]{0:T(128)S(1)} %pad_add_fusion.pos, f32[4,40,640]{2,1,0:T(8,128)S(1)} %all-to-all-done.4.own, f32[4,40,640]{2,1,0:T(8,128)S(1)} %collective-permute-done.4.other), custom_call_target="tpu_custom_call" | custom-call | tf_op jit(solution)/shard_map/outputs/pallas_call | solution.py:263
  96.6 0.6 copy.10
  (4 shorter events, 0.1 us)
Async XLA Ops:
  0.7 1.5 %copy-start = (bf16[256,3712]{1,0:T(8,128)(2,1)S(1)}, bf16[256,3712]{1,0:T(8,128)(2,1)}, u32[]{:S(2)}) copy-start(bf16[256,3712]{1,0:T(8,128)(2,1)} %u_hbm.5) | copy-start | bytes 5701636
  2.2 1.0 %copy-start.2 = (bf16[256,1024]{1,0:T(8,128)(2,1)S(1)}, bf16[256,1024]{1,0:T(8,128)(2,1)}, u32[]{:S(2)}) copy-start(bf16[256,1024]{1,0:T(8,128)(2,1)} %tok_ref.3) | copy-start | bytes 1572868
  3.3 0.9 copy-start.4
  4.2 0.8 copy-start.6
  5.1 29.8 %copy-start.8 = (f32[3712]{0:T(1024)S(1)}, f32[3712]{0:T(1024)}, u32[]{:S(2)}) copy-start(f32[3712]{0:T(1024)} %param.11) | copy-start | bytes 44548
  5.1 38.8 %copy-start.1 = (bf16[256,3712]{1,0:T(8,128)(2,1)S(1)}, bf16[256,3712]{1,0:T(8,128)(2,1)}, u32[]{:S(2)}) copy-start(bf16[256,3712]{1,0:T(8,128)(2,1)} %u_hbm.5) | copy-start | bytes 5701636
  5.1 38.8 %copy-start.3 = (bf16[256,1024]{1,0:T(8,128)(2,1)S(1)}, bf16[256,1024]{1,0:T(8,128)(2,1)}, u32[]{:S(2)}) copy-start(bf16[256,1024]{1,0:T(8,128)(2,1)} %tok_ref.3) | copy-start | bytes 1572868
  5.1 38.8 %copy-start.5 = (bf16[32,3712]{1,0:T(8,128)(2,1)S(1)}, bf16[32,3712]{1,0:T(8,128)(2,1)}, u32[]{:S(2)}) copy-start(bf16[32,3712]{1,0:T(8,128)(2,1)} %a_ref.3) | copy-start | bytes 712708
  5.1 38.8 %copy-start.7 = (bf16[1024,32]{0,1:T(8,128)(2,1)S(1)}, bf16[1024,32]{0,1:T(8,128)(2,1)}, u32[]{:S(2)}) copy-start(bf16[1024,32]{0,1:T(8,128)(2,1)} %param.9) | copy-start | bytes 196612
  31.5 12.4 %all-to-all-start.1 = ((f32[8,8,512]{2,1,0:T(8,128)}), f32[8,8,512]{2,1,0:T(8,128)S(1)}, u32[]{:S(2)}, u32[]{:S(2)}) async-start(f32[8,8,512]{2,1,0:T(8,128)} %broadcast_in_dim.2), calls=%async_computation.1 | async-start | bytes 262144 | tf_op jit(solution)/shard_map/all_to_all | solution.py:224
  50.0 1.8 %collective-permute-start = (f32[4,40,640]{2,1,0:T(8,128)S(1)}, f32[4,40,640]{2,1,0:T(8,128)S(1)}, u32[]{:S(2)}, u32[]{:S(2)}) collective-permute-start(f32[4,40,640]{2,1,0:T(8,128)S(1)} %get-tuple-element.23), channel_id=1, source_target_pairs={{0,32},{32,0},{64,96},{96,64},{128,160},{160,128},{192,224},{224,1... | collective-permute-start | bytes 1228808 | tf_op jit(solution)/shard_map/ppermute | solution.py:239
  64.8 10.1 %all-to-all-start.3 = ((f32[4,32,128]{2,1,0:T(8,128)}), f32[4,32,128]{2,1,0:T(8,128)S(1)}, u32[]{:S(2)}, u32[]{:S(2)}) async-start(f32[4,32,128]{2,1,0:T(8,128)} %get-tuple-element.24), calls=%async_computation.3 | async-start | bytes 131072 | tf_op jit(solution)/shard_map/all_to_all | solution.py:254
  75.7 10.9 %all-to-all-start.4 = ((f32[4,40,640]{2,1,0:T(8,128)}), f32[4,40,640]{2,1,0:T(8,128)S(1)}, u32[]{:S(2)}, u32[]{:S(2)}) async-start(f32[4,40,640]{2,1,0:T(8,128)} %spread.1), calls=%async_computation.4 | async-start | bytes 819200 | tf_op jit(solution)/shard_map/all_to_all | solution.py:261
  80.6 9.8 %collective-permute-start.1 = (f32[256,256]{1,0:T(8,128)S(1)}, f32[256,256]{1,0:T(8,128)S(1)}, u32[]{:S(2)}, u32[]{:S(2)}) collective-permute-start(f32[256,256]{1,0:T(8,128)S(1)} %get-tuple-element.28), channel_id=1, source_target_pairs={{0,1},{1,2},{2,3},{3,0},{4,5},{5,6},{6,7},{7,4},{8,9},{9,10},{10,1... | collective-permute-start | bytes 786440 | tf_op jit(solution)/shard_map/ppermute | solution.py:257
  81.8 12.6 %collective-permute-start.2 = (f32[256,256]{1,0:T(8,128)S(1)}, f32[256,256]{1,0:T(8,128)S(1)}, u32[]{:S(2)}, u32[]{:S(2)}) collective-permute-start(f32[256,256]{1,0:T(8,128)S(1)} %get-tuple-element.29), channel_id=1, source_target_pairs={{0,2},{1,3},{2,0},{3,1},{4,6},{5,7},{6,4},{7,5},{8,10},{9,11},{10,... | collective-permute-start | bytes 786440 | tf_op jit(solution)/shard_map/ppermute | solution.py:257
  84.5 9.9 %collective-permute-start.3 = (f32[256,256]{1,0:T(8,128)S(1)}, f32[256,256]{1,0:T(8,128)S(1)}, u32[]{:S(2)}, u32[]{:S(2)}) collective-permute-start(f32[256,256]{1,0:T(8,128)S(1)} %get-tuple-element.30), channel_id=1, source_target_pairs={{0,3},{1,0},{2,1},{3,2},{4,7},{5,4},{6,5},{7,6},{8,11},{9,8},{10,9... | collective-permute-start | bytes 786440 | tf_op jit(solution)/shard_map/ppermute | solution.py:257
  86.6 8.6 %collective-permute-start.4 = (f32[4,40,640]{2,1,0:T(8,128)S(1)}, f32[4,40,640]{2,1,0:T(8,128)S(1)}, u32[]{:S(2)}, u32[]{:S(2)}) collective-permute-start(f32[4,40,640]{2,1,0:T(8,128)S(1)} %all-to-all-done.4.own), channel_id=1, source_target_pairs={{0,32},{32,0},{64,96},{96,64},{128,160},{160,128},{192,224},{224,1... | collective-permute-start | bytes 1228808 | tf_op jit(solution)/shard_map/ppermute | solution.py:262

commit v2 on v1

v2 whole, which is shorter than its diff:
```python
import jax
import jax.numpy as jnp
from jax import lax
from jax.experimental import pallas as pl
from jax.experimental.pallas import tpu as pltpu
from jax.sharding import PartitionSpec as P

SCALE = 2.0
EPS = 1e-06

TOK, ROWS, COLS, RANK = 256, 1024, 3712, 32
CW = 512
NC = 8
LIMIT = 28
DEPTH = 2
UNITS = [512] * 7 + [128]
WIDTHS = [min(CW, COLS - CW * c) for c in range(NC)]
PW = CW + 128
PH = 40
X_GROUPS = [[0, 2, 4, 6], [1, 3, 5, 7]]
CORE_FLIP = [(i, i ^ 1) for i in range(8)]
F32, BF16 = jnp.float32, jnp.bfloat16
NN = (((1,), (0,)), ((), ()))
NT = (((1,), (1,)), ((), ()))
TN = (((0,), (0,)), ((), ()))

VMEM = pl.BlockSpec(memory_space=pltpu.VMEM)
HBM = pl.BlockSpec(memory_space=pl.ANY)


def mm(a, b, dims):
    return lax.dot_general(a, b, dims, preferred_element_type=F32)


def dp_place():
    return lax.axis_index("dp")


def span(c):
    return pl.ds(CW * c, WIDTHS[c])


def first_kernel(tok_h, bt_h, a_h, w_h, u_h, out, tok, bt, a, u, w, tok_t, b_v, sems, small):
    firsts = [
        pltpu.make_async_copy(src, dst, small.at[i])
        for i, (src, dst) in enumerate(((tok_h, tok), (bt_h, bt), (a_h, a)))
    ]
    for copy in firsts:
        copy.start()
    units = [(sum(UNITS[:i]), n) for i, n in enumerate(UNITS)]
    copies = [
        [
            pltpu.make_async_copy(src.at[:, pl.ds(at, n)], dst.at[:, pl.ds(at, n)], sems.at[j, i])
            for j, (src, dst) in enumerate(((u_h, u), (w_h, w)))
        ]
        for i, (at, n) in enumerate(units)
    ]

    def begin(i):
        if i < len(units):
            copies[i][0].start()
            copies[i][1].start()

    for i in range(DEPTH):
        begin(i)
    out[NC - 1] = jnp.zeros((8, CW), F32)
    for copy in firsts:
        copy.wait()
    b2t = bt[...] * BF16(SCALE)
    tok_t[...] = tok[...].T
    b_v[...] = b2t.T
    low = mm(bt[...], tok[...], NT)
    gram = mm(bt[...], b2t, NT).astype(BF16)
    for r in range(NC):
        for i in range(4):
            lane = TOK * (i % 2)
            out[r, 6 + i // 2 : 7 + i // 2, lane : lane + TOK] = low[4 * r + i : 4 * r + i + 1]
    for i, (at, n) in enumerate(units):
        copies[i][0].wait()
        copies[i][1].wait()
        begin(i + DEPTH)
        here = pl.ds(at, n)
        merged = w[:, here].astype(F32) + mm(b_v[...], a[:, here], NN)
        outer = mm(tok_t[...], u[:, here], NN)
        squares = jnp.sum((merged * merged).reshape(ROWS // 8, 8, n), 0)
        products = jnp.sum((merged * outer).reshape(ROWS // 8, 8, n), 0)
        lo = at % CW
        out[at // CW, 0:1, lo : lo + n] = jnp.sum(squares, 0, keepdims=True)
        out[at // CW, 1:2, lo : lo + n] = jnp.sum(products, 0, keepdims=True)
    last = NC - 1

    def store(q, n):
        for r in range(NC):
            out[r, 2:6, :n] = q[4 * r : 4 * r + 4]
            if n < CW:
                out[r, 2:6, n:] = jnp.zeros((4, CW - n), F32)

    place = dp_place()

    @pl.when(place < last)
    def _():
        mine = pl.ds(pl.multiple_of(place * CW, CW), CW)
        store(mm(bt[...], w[:, mine], NN) + mm(gram, a[:, mine], NN), CW)

    @pl.when(place == last)
    def _():
        store(mm(bt[...], w[:, span(last)], NN) + mm(gram, a[:, span(last)], NN), WIDTHS[last])


def columns(src, dst, sems):
    copies = [
        pltpu.make_async_copy(src.at[:, span(c)], dst.at[:, span(c)], sems.at[c])
        for c in range(NC)
    ]
    for copy in copies:
        copy.start()
    return copies


def second_kernel(zz, mag, tok, bt, a, u, w_h, keep, send, s_out, g_v, t_v, v_v, w, sems):
    copies = columns(w_h, w, sems)
    b2t = bt[...] * BF16(SCALE)
    for r in range(NC):
        for i in range(4):
            lane = TOK * (i % 2)
            t_v[4 * r + i : 4 * r + i + 1, :] = zz[r, 6 + i // 2 : 7 + i // 2, lane : lane + TOK]
    low = t_v[...]
    high = low.astype(BF16)
    pair = jnp.concatenate([high, (low - high.astype(F32)).astype(BF16)], 0)
    s_sum = jnp.zeros((RANK, TOK), F32)
    va_sum = jnp.zeros((RANK, RANK), F32)
    vm_sum = jnp.zeros((RANK, ROWS), F32)
    g_v[NC - 1] = jnp.zeros((PH, PW), F32)
    for c in range(NC):
        n = WIDTHS[c]
        uc, ac = u[:, span(c)], a[:, span(c)]
        normsq = zz[c, 0:1, :n] + EPS
        along = zz[c, 1:2, :n]
        ratio = mag[c : c + 1, :n] / jnp.sqrt(normsq)
        v = (ac.astype(F32) * (ratio * (along / normsq))).astype(BF16)
        scaled = (uc.astype(F32) * ratio).astype(BF16)
        s_sum = s_sum + mm(ac, scaled, NT)
        va_sum = va_sum + mm(v, ac, NT)
        v_v[:, span(c)] = v
        p = mm(pair, uc, NN)
        g_v[c, :RANK, :n] = (SCALE * ratio) * (p[:RANK] + p[RANK:])
        g_v[c, RANK : RANK + 1, :n] = along
        g_v[c, RANK + 1 :, :] = jnp.zeros((PH - RANK - 1, PW), F32)
        g_v[c, RANK : RANK + 1, CW:] = jnp.zeros((1, PW - CW), F32)
    s_out[...] = s_sum
    gb = mm(s_sum.astype(BF16), tok[...], NN) - mm(va_sum.astype(BF16), b2t, NN)
    for c in range(NC):
        copies[c].wait()
        vm_sum = vm_sum + mm(v_v[:, span(c)], w[:, span(c)], NT)
    gb = SCALE * (gb - vm_sum)
    for c in range(NC):
        g_v[c, :RANK, CW:] = gb[:, 128 * c : 128 * (c + 1)]
    core = lax.rem(dp_place(), 2)
    for x in range(4):
        keep[x] = g_v[2 * x + core]
        send[x] = g_v[2 * x + 1 - core]


def third_kernel(zz, mag, s_ref, bt, u, w_h, o0, o1, o2, o3, acc, w, sems):
    copies = columns(w_h, w, sems)
    acc[...] = mm(s_ref[...].astype(BF16), bt[...] * BF16(SCALE), TN)
    for c in range(NC):
        n = WIDTHS[c]
        ratio = mag[c : c + 1, :n] / jnp.sqrt(zz[c, 0:1, :n] + EPS)
        scaled = (u[:, span(c)].astype(F32) * ratio).astype(BF16)
        copies[c].wait()
        acc[...] += mm(scaled, w[:, span(c)], NT)
    for d, o in enumerate((o0, o1, o2, o3)):
        part = lax.rem(lax.axis_index("col") + d, 4)
        o[...] = acc[:, pl.ds(pl.multiple_of(part * 256, 256), 256)]


def combine_kernel(y, zz, mag, pack, gb4):
    s = dp_place()
    total = (y[0] + y[1]) + (y[2] + y[3])
    mine = zz[s]
    normsq = mine[0:1] + EPS
    root = jnp.sqrt(normsq)
    ratio = mag[pl.ds(s, 1), :] / root
    along = total[RANK : RANK + 1, :CW]
    factor = (SCALE * ratio) * (along / normsq)
    for r in range(NC):
        rows = slice(4 * r, 4 * r + 4)
        pack[rows, :CW] = total[rows, :CW] - factor * zz[r, 2:6, :]
    pack[RANK : RANK + 1, :CW] = along / root
    pack[RANK + 1 :, :CW] = jnp.zeros((PH - RANK - 1, CW), F32)
    pack[:, CW:] = jnp.zeros((PH, PW - CW), F32)
    gb = total[:RANK, CW:]
    for i in range(4):
        gb4[i] = gb


def spread_kernel(pack, gb4, out):
    gb = (gb4[0] + gb4[1]) + (gb4[2] + gb4[3])
    for i in range(4):
        out[i] = pack[...]
        out[i, :RANK, CW:] = gb


def last_kernel(own, other, ga, gm, gb):
    even = dp_place() % 2 == 0
    for c in range(NC):
        mine = own if c % 2 == 0 else other
        theirs = other if c % 2 == 0 else own
        chunk = jnp.where(even, mine[c // 2], theirs[c // 2])
        ga[:, span(c)] = chunk[:RANK, : WIDTHS[c]]
        gm[span(c)] = chunk[RANK, : WIDTHS[c]]
        gb[:, 128 * c : 128 * (c + 1)] = chunk[:RANK, CW:]


def call(kernel, name, ins, outs, scratch=(), cost=None, limit=32):
    shapes = [
        pltpu.VMEM(*o) if isinstance(o[0], tuple) else jax.ShapeDtypeStruct(o, F32) for o in outs
    ]
    return pl.pallas_call(
        kernel,
        name=name,
        out_shape=shapes if len(shapes) > 1 else shapes[0],
        in_specs=ins,
        out_specs=[VMEM] * len(outs) if len(outs) > 1 else VMEM,
        scratch_shapes=list(scratch),
        cost_estimate=cost,
        compiler_params=pltpu.CompilerParams(vmem_limit_bytes=int(limit * (1 << 20))),
    )


def in_hbm(x):
    return pltpu.with_memory_space_constraint(x, pltpu.HBM)


COST = pl.CostEstimate(
    flops=4 * TOK * ROWS * COLS, bytes_accessed=10_000_000, transcendentals=COLS
)


def norms(tokens, bt, factor_a, weight, upstream):
    return call(
        first_kernel,
        "norms",
        [HBM, HBM, HBM, HBM, HBM],
        [
            ((NC, 8, CW), F32),
            ((TOK, ROWS), BF16),
            ((RANK, ROWS), BF16),
            ((RANK, COLS), BF16),
            ((TOK, COLS), BF16),
        ],
        (
            pltpu.VMEM((ROWS, COLS), BF16),
            pltpu.VMEM((ROWS, TOK), BF16),
            pltpu.VMEM((ROWS, RANK), BF16),
            pltpu.SemaphoreType.DMA((2, len(UNITS))),
            pltpu.SemaphoreType.DMA((3,)),
        ),
        COST,
        LIMIT,
    )(*(in_hbm(x) for x in (tokens, bt, factor_a, weight, upstream)))


def factors(zz, mag, tok, bt, a, u, weight):
    return call(
        second_kernel,
        "factors",
        [VMEM] * 6 + [HBM],
        [(4, PH, PW), (4, PH, PW), (RANK, TOK)],
        (
            pltpu.VMEM((NC, PH, PW), F32),
            pltpu.VMEM((RANK, TOK), F32),
            pltpu.VMEM((RANK, COLS), BF16),
            pltpu.VMEM((ROWS, COLS), BF16),
            pltpu.SemaphoreType.DMA((NC,)),
        ),
        COST,
    )(zz, mag, tok, bt, a, u, in_hbm(weight))


def tokens_grad(zz, mag, s_part, bt, u, weight):
    return call(
        third_kernel,
        "tokens_grad",
        [VMEM] * 5 + [HBM],
        [(TOK, 256)] * 4,
        (
            pltpu.VMEM((TOK, ROWS), F32),
            pltpu.VMEM((ROWS, COLS), BF16),
            pltpu.SemaphoreType.DMA((NC,)),
        ),
        COST,
    )(zz, mag, s_part, bt, u, in_hbm(weight))


def shards(tokens, upstream, weight, factor_b, factor_a, magnitude):
    mag = jnp.pad(magnitude, (0, NC * CW - COLS)).reshape(NC, CW)
    bt = factor_b.T
    part, tok, bt, a, u = norms(tokens, bt, factor_a, weight, upstream)
    z = jnp.sum(lax.all_to_all(part, "row", 0, 0, tiled=True), 0)
    zz = lax.all_to_all(jnp.broadcast_to(z[None], part.shape), "row", 0, 0, tiled=True)

    keep, send, s_part = factors(zz, mag, tok, bt, a, u, weight)
    halves = keep + lax.ppermute(send, "dp", CORE_FLIP)
    halves, s_part = lax.optimization_barrier((halves, s_part))
    y = lax.all_to_all(halves, "dp", 0, 0, tiled=True, axis_index_groups=X_GROUPS)
    o0, o1, o2, o3 = tokens_grad(zz, mag, s_part, bt, u, weight)

    pack, gb4 = call(
        combine_kernel, "combine", [VMEM, VMEM, VMEM], [(PH, PW), (4, RANK, 128)]
    )(y, zz, mag)
    gb4, o1, o2, o3 = lax.optimization_barrier((gb4, o1, o2, o3))
    gb4 = lax.all_to_all(gb4, "col", 0, 0, tiled=True)
    arrived = [
        lax.ppermute(o, "col", [(i, (i + d) % 4) for i in range(4)])
        for d, o in ((1, o1), (2, o2), (3, o3))
    ]
    first, third, gb4 = lax.optimization_barrier((arrived[0], arrived[2], gb4))
    arrived = [first, arrived[1], third]
    packs = call(spread_kernel, "spread", [VMEM, VMEM], [(4, PH, PW)])(pack, gb4)
    own = lax.all_to_all(packs, "dp", 0, 0, tiled=True, axis_index_groups=X_GROUPS)
    other = lax.ppermute(own, "dp", CORE_FLIP)
    grad_a, gm, gbt = call(
        last_kernel, "outputs", [VMEM, VMEM], [(RANK, COLS), (COLS,), (RANK, ROWS)]
    )(own, other)
    grad_tokens = ((o0 + arrived[0]) + (arrived[1] + arrived[2])).astype(BF16)
    return grad_tokens, gm, grad_a, gbt.T


def solution(mesh):
    placed = (
        P("dp", "row"),
        P("dp", "col"),
        P("row", "col"),
        P("row", None),
        P(None, "col"),
        P("col"),
    )
    return jax.shard_map(
        shards,
        mesh=mesh,
        in_specs=placed,
        out_specs=(P("dp", ("row", "col")), P("col"), P(None, "col"), P("row", None)),
        check_vma=False,
    )
```

time: 97.8 us -> 89 us (0.910)
  the two profiles are of different devices: /device:TPU:2 before, /device:TPU:1 now
where the time goes in v2:
time: 89 us; the launch traced here: 88.5 us
  blocking collectives  24.1 us (27%)
  starting transfers between devices  22.6 us (25%)
  Pallas kernels  20.5 us (23%)
  waiting for transfers between devices  17.4 us (20%)
  other arithmetic  1.53 us (2%)
  local copies, waits for them, and re-layouts  1.52 us (2%)
    all_to_all x1, blocking collectives, shards(): z = jnp.sum(lax.all_to_all(part, 'row', 0, 0, tiled=True), 0)  16.6 us
    pallas_call x1, Pallas kernels, norms(): call(first_kernel, 'norms', [HBM, HBM, HBM, HBM, HBM], [((NC, 8, CW), F32...  8.05 us
    all_to_all x1, waiting for transfers between devices, shards(): lax.all_to_all(jnp.broadcast_to(z[None], part.shape), 'row', 0, 0, tiled=...  7.9 us
    all_to_all x1, blocking collectives, shards(): gb4 = lax.all_to_all(gb4, 'col', 0, 0, tiled=True)  7.5 us
    pallas_call x1, Pallas kernels, factors(): call(second_kernel, 'factors', [VMEM] * 6 + [HBM], [(4, PH, PW), (4, PH,...  6.37 us
    all_to_all x1, waiting for transfers between devices, shards(): lax.all_to_all(packs, 'dp', 0, 0, tiled=True, axis_index_groups=X_GROUPS)  5.36 us
    ppermute x1, starting transfers between devices, shards(): other = lax.ppermute(own, 'dp', CORE_FLIP)  4.54 us
    pallas_call x1, Pallas kernels, tokens_grad(): call(third_kernel, 'tokens_grad', [VMEM] * 5 + [HBM], [(TOK, 256)] * 4, (...  4.42 us
  transfers between devices with their start and end apart: 8, of which 5 were waited for; matrix products, arithmetic and copies ran while one was open for 1% of the time, Pallas kernels for 5%

profile of v2, /device:TPU:1, one launch (start us, length us, event | category | flops | bytes accessed | tf_op | source)
XLA Modules:
  0.0 88.5 jit_solution(8609204453139589381)
XLA Ops:
  0.6 0.0 copy-start.2
  0.6 8.1 %norms.1 = (f32[8,8,512]{2,1,0:T(8,128)S(1)}, bf16[256,1024]{1,0:T(8,128)(2,1)S(1)}, bf16[32,1024]{1,0:T(8,128)(2,1)S(1)}, bf16[32,3712]{1,0:T(8,128)(2,1)S(1)}, bf16[256,3712]{1,0:T(8,128)(2,1)S(1)}) custom-call(bf16[256,1024]{1,0:T(8,128)(2,1)} %tok_h.1, bf16[32,1024]{1,0:T(8,128)(2,1)} %bitcast.3, bf16[32,3712]{1,0:T(8,128)(2,1)} %a_h.1, ...), custom_call_target="tpu_custom_call" | custom-call | flops 3892314112 | bytes 10000000 | tf_op jit(solution)/shard_map/norms/pallas_call | solution.py:242
  8.7 0.0 copy-start
  8.7 16.6 %all_to_all.25 = f32[8,8,512]{2,1,0:T(8,128)S(1)} all-to-all(f32[8,8,512]{2,1,0:T(8,128)S(1)} %get-tuple-element.30), channel_id=1, replica_groups=mesh['dp'=8,'row'=8,'col'=4] {'row'}, dimensions={0} | all-to-all | bytes 262144 | tf_op jit(solution)/shard_map/all_to_all | solution.py:301
  25.3 0.7 broadcast_in_dim.2
  26.0 3.4 %all-to-all-start.1 = ((f32[8,8,512]{2,1,0:T(8,128)}), f32[8,8,512]{2,1,0:T(8,128)S(1)}, u32[]{:S(2)}, u32[]{:S(2)}) async-start(f32[8,8,512]{2,1,0:T(8,128)} %broadcast_in_dim.2), calls=%async_computation.1 | async-start | bytes 262144 | tf_op jit(solution)/shard_map/all_to_all | solution.py:302
  29.4 0.0 copy-done.2
  29.4 7.9 %all-to-all-done.1.zz = f32[8,8,512]{2,1,0:T(8,128)S(1)} async-done(((f32[8,8,512]{2,1,0:T(8,128)}), f32[8,8,512]{2,1,0:T(8,128)S(1)}, u32[]{:S(2)}, u32[]{:S(2)}) %all-to-all-start.1) | async-done | bytes 131104 | tf_op jit(solution)/shard_map/all_to_all | solution.py:302
  37.3 6.4 %factors.1 = (f32[4,40,640]{2,1,0:T(8,128)S(1)}, f32[4,40,640]{2,1,0:T(8,128)S(1)}, f32[32,256]{1,0:T(8,128)S(1)}) custom-call(f32[8,8,512]{2,1,0:T(8,128)S(1)} %all-to-all-done.1.zz, f32[8,512]{1,0:T(8,128)S(1)} %reshape.12.mag, bf16[256,1024]{1,0:T(8,128)(2,1)S(1)} %get-tuple-element.31.tok, bf16[32,1024]{1,0:T(8,128)(2,1)S(1)} %get-tuple-element.32.bt, ...), custom_call_target="tpu_custom_call" | custom-call | flops 3892314112 | bytes 10000000 | tf_op jit(solution)/shard_map/factors/pallas_call | solution.py:266
  43.7 0.0 copy-done
  43.7 3.4 %collective-permute-start = (f32[4,40,640]{2,1,0:T(8,128)S(1)}, f32[4,40,640]{2,1,0:T(8,128)S(1)}, u32[]{:S(2)}, u32[]{:S(2)}) collective-permute-start(f32[4,40,640]{2,1,0:T(8,128)S(1)} %get-tuple-element.36), channel_id=1, source_target_pairs={{0,32},{32,0},{64,96},{96,64},{128,160},{160,128},{192,224},{224,1... | collective-permute-start | bytes 1228808 | tf_op jit(solution)/shard_map/ppermute | solution.py:305
  47.1 1.4 %collective-permute-done = f32[4,40,640]{2,1,0:T(8,128)S(1)} collective-permute-done((f32[4,40,640]{2,1,0:T(8,128)S(1)}, f32[4,40,640]{2,1,0:T(8,128)S(1)}, u32[]{:S(2)}, u32[]{:S(2)}) %collective-permute-start) | collective-permute-done | bytes 409632 | tf_op jit(solution)/shard_map/ppermute | solution.py:305
  48.5 0.8 add.14
  49.3 4.0 %all-to-all-start.2 = ((f32[4,40,640]{2,1,0:T(8,128)}), f32[4,40,640]{2,1,0:T(8,128)S(1)}, u32[]{:S(2)}, u32[]{:S(2)}) async-start(f32[4,40,640]{2,1,0:T(8,128)} %add.14), calls=%async_computation.2 | async-start | bytes 819200 | tf_op jit(solution)/shard_map/all_to_all | solution.py:307
  53.3 0.0 copy-start.1
  53.3 0.8 copy-done.1
  54.1 4.4 %tokens_grad.1 = (f32[256,256]{1,0:T(8,128)S(1)}, f32[256,256]{1,0:T(8,128)S(1)}, f32[256,256]{1,0:T(8,128)S(1)}, f32[256,256]{1,0:T(8,128)S(1)}) custom-call(f32[8,8,512]{2,1,0:T(8,128)S(1)} %all-to-all-done.1.zz, f32[8,512]{1,0:T(8,128)S(1)} %reshape.12.mag, f32[32,256]{1,0:T(8,128)S(1)} %get-tuple-element.38.s_ref, bf16[32,1024]{1,0:T(8,128)(2,1)S(1)} %copy-done.1, ...), custom_call_target="tpu_custom_call" | custom-call | flops 3892314112 | bytes 10000000 | tf_op jit(solution)/shard_map/tokens_grad/pallas_call | solution.py:283
  58.6 2.1 %all-to-all-done.2.y = f32[4,40,640]{2,1,0:T(8,128)S(1)} async-done(((f32[4,40,640]{2,1,0:T(8,128)}), f32[4,40,640]{2,1,0:T(8,128)S(1)}, u32[]{:S(2)}, u32[]{:S(2)}) %all-to-all-start.2) | async-done | bytes 409632 | tf_op jit(solution)/shard_map/all_to_all | solution.py:307
  60.7 1.4 %collective-permute-start.1 = (f32[256,256]{1,0:T(8,128)S(1)}, f32[256,256]{1,0:T(8,128)S(1)}, u32[]{:S(2)}, u32[]{:S(2)}) collective-permute-start(f32[256,256]{1,0:T(8,128)S(1)} %get-tuple-element.45), channel_id=1, source_target_pairs={{0,1},{1,2},{2,3},{3,0},{4,5},{5,6},{6,7},{7,4},{8,9},{9,10},{10,1... | collective-permute-start | bytes 786440 | tf_op jit(solution)/shard_map/ppermute | solution.py:316
  62.1 1.5 %collective-permute-start.2 = (f32[256,256]{1,0:T(8,128)S(1)}, f32[256,256]{1,0:T(8,128)S(1)}, u32[]{:S(2)}, u32[]{:S(2)}) collective-permute-start(f32[256,256]{1,0:T(8,128)S(1)} %get-tuple-element.46), channel_id=1, source_target_pairs={{0,3},{1,0},{2,1},{3,2},{4,7},{5,4},{6,5},{7,6},{8,11},{9,8},{10,9... | collective-permute-start | bytes 786440 | tf_op jit(solution)/shard_map/ppermute | solution.py:316
  63.6 7.5 %all_to_all.26.gb4 = f32[4,32,128]{2,1,0:T(8,128)S(1)} all-to-all(f32[4,32,128]{2,1,0:T(8,128)S(1)} %get-tuple-element.47), channel_id=1, replica_groups=mesh['dp'=8,'row'=8,'col'=4] {'col'}, dimensions={0} | all-to-all | bytes 131072 | tf_op jit(solution)/shard_map/all_to_all | solution.py:314
  71.1 0.0 collective-permute-done.1
  71.1 0.0 collective-permute-done.2
  71.1 0.8 spread.1
  71.9 3.5 %all-to-all-start.4 = ((f32[4,40,640]{2,1,0:T(8,128)}), f32[4,40,640]{2,1,0:T(8,128)S(1)}, u32[]{:S(2)}, u32[]{:S(2)}) async-start(f32[4,40,640]{2,1,0:T(8,128)} %spread.1), calls=%async_computation.4 | async-start | bytes 819200 | tf_op jit(solution)/shard_map/all_to_all | solution.py:322
  75.4 0.9 %collective-permute-start.3 = (f32[256,256]{1,0:T(8,128)S(1)}, f32[256,256]{1,0:T(8,128)S(1)}, u32[]{:S(2)}, u32[]{:S(2)}) collective-permute-start(f32[256,256]{1,0:T(8,128)S(1)} %get-tuple-element.49), channel_id=1, source_target_pairs={{0,2},{1,3},{2,0},{3,1},{4,6},{5,7},{6,4},{7,5},{8,10},{9,11},{10,... | collective-permute-start | bytes 786440 | tf_op jit(solution)/shard_map/ppermute | solution.py:316
  76.3 5.4 %all-to-all-done.4.own = f32[4,40,640]{2,1,0:T(8,128)S(1)} async-done(((f32[4,40,640]{2,1,0:T(8,128)}), f32[4,40,640]{2,1,0:T(8,128)S(1)}, u32[]{:S(2)}, u32[]{:S(2)}) %all-to-all-start.4) | async-done | bytes 409632 | tf_op jit(solution)/shard_map/all_to_all | solution.py:322
  81.7 4.5 %collective-permute-start.4 = (f32[4,40,640]{2,1,0:T(8,128)S(1)}, f32[4,40,640]{2,1,0:T(8,128)S(1)}, u32[]{:S(2)}, u32[]{:S(2)}) collective-permute-start(f32[4,40,640]{2,1,0:T(8,128)S(1)} %all-to-all-done.4.own), channel_id=1, source_target_pairs={{0,32},{32,0},{64,96},{96,64},{128,160},{160,128},{192,224},{224,1... | collective-permute-start | bytes 1228808 | tf_op jit(solution)/shard_map/ppermute | solution.py:323
  86.2 0.0 collective-permute-done.3
  86.2 0.7 add_convert_fusion
  86.9 0.7 collective-permute-done.4.other
  87.6 0.9 outputs.1
  (4 shorter events, 0.1 us)
Async XLA Ops:
  0.6 28.7 %copy-start.2 = (f32[3712]{0:T(1024)S(1)}, f32[3712]{0:T(1024)}, u32[]{:S(2)}) copy-start(f32[3712]{0:T(1024)} %param.11) | copy-start | bytes 44548
  8.7 35.0 %copy-start = (bf16[32,1024]{1,0:T(8,128)(2,1)}, bf16[32,1024]{1,0:T(8,128)(2,1)S(1)}, u32[]{:S(2)}) copy-start(bf16[32,1024]{1,0:T(8,128)(2,1)S(1)} %get-tuple-element.32.bt) | copy-start | bytes 196612
  26.0 11.3 %all-to-all-start.1 = ((f32[8,8,512]{2,1,0:T(8,128)}), f32[8,8,512]{2,1,0:T(8,128)S(1)}, u32[]{:S(2)}, u32[]{:S(2)}) async-start(f32[8,8,512]{2,1,0:T(8,128)} %broadcast_in_dim.2), calls=%async_computation.1 | async-start | bytes 262144 | tf_op jit(solution)/shard_map/all_to_all | solution.py:302
  43.7 4.8 %collective-permute-start = (f32[4,40,640]{2,1,0:T(8,128)S(1)}, f32[4,40,640]{2,1,0:T(8,128)S(1)}, u32[]{:S(2)}, u32[]{:S(2)}) collective-permute-start(f32[4,40,640]{2,1,0:T(8,128)S(1)} %get-tuple-element.36), channel_id=1, source_target_pairs={{0,32},{32,0},{64,96},{96,64},{128,160},{160,128},{192,224},{224,1... | collective-permute-start | bytes 1228808 | tf_op jit(solution)/shard_map/ppermute | solution.py:305
  49.3 11.4 %all-to-all-start.2 = ((f32[4,40,640]{2,1,0:T(8,128)}), f32[4,40,640]{2,1,0:T(8,128)S(1)}, u32[]{:S(2)}, u32[]{:S(2)}) async-start(f32[4,40,640]{2,1,0:T(8,128)} %add.14), calls=%async_computation.2 | async-start | bytes 819200 | tf_op jit(solution)/shard_map/all_to_all | solution.py:307
  53.3 0.8 copy-start.1
  60.7 10.4 %collective-permute-start.1 = (f32[256,256]{1,0:T(8,128)S(1)}, f32[256,256]{1,0:T(8,128)S(1)}, u32[]{:S(2)}, u32[]{:S(2)}) collective-permute-start(f32[256,256]{1,0:T(8,128)S(1)} %get-tuple-element.45), channel_id=1, source_target_pairs={{0,1},{1,2},{2,3},{3,0},{4,5},{5,6},{6,7},{7,4},{8,9},{9,10},{10,1... | collective-permute-start | bytes 786440 | tf_op jit(solution)/shard_map/ppermute | solution.py:316
  62.1 9.0 %collective-permute-start.2 = (f32[256,256]{1,0:T(8,128)S(1)}, f32[256,256]{1,0:T(8,128)S(1)}, u32[]{:S(2)}, u32[]{:S(2)}) collective-permute-start(f32[256,256]{1,0:T(8,128)S(1)} %get-tuple-element.46), channel_id=1, source_target_pairs={{0,3},{1,0},{2,1},{3,2},{4,7},{5,4},{6,5},{7,6},{8,11},{9,8},{10,9... | collective-permute-start | bytes 786440 | tf_op jit(solution)/shard_map/ppermute | solution.py:316
  71.9 9.8 %all-to-all-start.4 = ((f32[4,40,640]{2,1,0:T(8,128)}), f32[4,40,640]{2,1,0:T(8,128)S(1)}, u32[]{:S(2)}, u32[]{:S(2)}) async-start(f32[4,40,640]{2,1,0:T(8,128)} %spread.1), calls=%async_computation.4 | async-start | bytes 819200 | tf_op jit(solution)/shard_map/all_to_all | solution.py:322
  75.4 10.8 %collective-permute-start.3 = (f32[256,256]{1,0:T(8,128)S(1)}, f32[256,256]{1,0:T(8,128)S(1)}, u32[]{:S(2)}, u32[]{:S(2)}) collective-permute-start(f32[256,256]{1,0:T(8,128)S(1)} %get-tuple-element.49), channel_id=1, source_target_pairs={{0,2},{1,3},{2,0},{3,1},{4,6},{5,7},{6,4},{7,5},{8,10},{9,11},{10,... | collective-permute-start | bytes 786440 | tf_op jit(solution)/shard_map/ppermute | solution.py:316
  81.7 5.9 %collective-permute-start.4 = (f32[4,40,640]{2,1,0:T(8,128)S(1)}, f32[4,40,640]{2,1,0:T(8,128)S(1)}, u32[]{:S(2)}, u32[]{:S(2)}) collective-permute-start(f32[4,40,640]{2,1,0:T(8,128)S(1)} %all-to-all-done.4.own), channel_id=1, source_target_pairs={{0,32},{32,0},{64,96},{96,64},{128,160},{160,128},{192,224},{224,1... | collective-permute-start | bytes 1228808 | tf_op jit(solution)/shard_map/ppermute | solution.py:323

commit v3 on v2

--- a/solution.py
+++ b/solution.py
@@ -117,7 +117,17 @@
     return copies
 
 
-def second_kernel(zz, mag, tok, bt, a, u, w_h, keep, send, s_out, g_v, t_v, v_v, w, sems):
+def sum_kernel(parts, out):
+    total = jnp.sum(parts[...], 0)
+    for r in range(NC):
+        out[r] = total
+
+
+def add_kernel(a, b, out):
+    out[...] = a[...] + b[...]
+
+
+def second_kernel(zz, mag, tok, bt, a, u, w_h, keep, send, s_out, g_v, t_v, w, sems):
     copies = columns(w_h, w, sems)
     b2t = bt[...] * BF16(SCALE)
     for r in range(NC):
@@ -141,7 +151,8 @@
         scaled = (uc.astype(F32) * ratio).astype(BF16)
         s_sum = s_sum + mm(ac, scaled, NT)
         va_sum = va_sum + mm(v, ac, NT)
-        v_v[:, span(c)] = v
+        copies[c].wait()
+        vm_sum = vm_sum + mm(v, w[:, span(c)], NT)
         p = mm(pair, uc, NN)
         g_v[c, :RANK, :n] = (SCALE * ratio) * (p[:RANK] + p[RANK:])
         g_v[c, RANK : RANK + 1, :n] = along
@@ -149,9 +160,6 @@
         g_v[c, RANK : RANK + 1, CW:] = jnp.zeros((1, PW - CW), F32)
     s_out[...] = s_sum
     gb = mm(s_sum.astype(BF16), tok[...], NN) - mm(va_sum.astype(BF16), b2t, NN)
-    for c in range(NC):
-        copies[c].wait()
-        vm_sum = vm_sum + mm(v_v[:, span(c)], w[:, span(c)], NT)
     gb = SCALE * (gb - vm_sum)
     for c in range(NC):
         g_v[c, :RANK, CW:] = gb[:, 128 * c : 128 * (c + 1)]
@@ -175,7 +183,7 @@
         o[...] = acc[:, pl.ds(pl.multiple_of(part * 256, 256), 256)]
 
 
-def combine_kernel(y, zz, mag, pack, gb4):
+def combine_kernel(y, zz, mag, pack, gb):
     s = dp_place()
     total = (y[0] + y[1]) + (y[2] + y[3])
     mine = zz[s]
@@ -190,13 +198,11 @@
     pack[RANK : RANK + 1, :CW] = along / root
     pack[RANK + 1 :, :CW] = jnp.zeros((PH - RANK - 1, CW), F32)
     pack[:, CW:] = jnp.zeros((PH, PW - CW), F32)
-    gb = total[:RANK, CW:]
-    for i in range(4):
-        gb4[i] = gb
-
-
-def spread_kernel(pack, gb4, out):
-    gb = (gb4[0] + gb4[1]) + (gb4[2] + gb4[3])
+    gb[...] = total[:RANK, CW:]
+
+
+def spread_kernel(pack, g0, g1, g2, g3, out):
+    gb = (g0[...] + g1[...]) + (g2[...] + g3[...])
     for i in range(4):
         out[i] = pack[...]
         out[i, :RANK, CW:] = gb
@@ -271,7 +277,6 @@
         (
             pltpu.VMEM((NC, PH, PW), F32),
             pltpu.VMEM((RANK, TOK), F32),
-            pltpu.VMEM((RANK, COLS), BF16),
             pltpu.VMEM((ROWS, COLS), BF16),
             pltpu.SemaphoreType.DMA((NC,)),
         ),
@@ -294,31 +299,34 @@
     )(zz, mag, s_part, bt, u, in_hbm(weight))
 
 
+def from_col(x, d):
+    return lax.ppermute(x, "col", [(i, (i + d) % 4) for i in range(4)])
+
+
 def shards(tokens, upstream, weight, factor_b, factor_a, magnitude):
     mag = jnp.pad(magnitude, (0, NC * CW - COLS)).reshape(NC, CW)
     bt = factor_b.T
     part, tok, bt, a, u = norms(tokens, bt, factor_a, weight, upstream)
-    z = jnp.sum(lax.all_to_all(part, "row", 0, 0, tiled=True), 0)
-    zz = lax.all_to_all(jnp.broadcast_to(z[None], part.shape), "row", 0, 0, tiled=True)
+    parts = lax.all_to_all(part, "row", 0, 0, tiled=True)
+    sums = call(sum_kernel, "sum", [VMEM], [((NC, 8, CW), F32)])(parts)
+    zz = lax.all_to_all(sums, "row", 0, 0, tiled=True)
 
     keep, send, s_part = factors(zz, mag, tok, bt, a, u, weight)
-    halves = keep + lax.ppermute(send, "dp", CORE_FLIP)
+    other = lax.ppermute(send, "dp", CORE_FLIP)
+    halves = call(add_kernel, "add", [VMEM, VMEM], [((4, PH, PW), F32)])(keep, other)
     halves, s_part = lax.optimization_barrier((halves, s_part))
     y = lax.all_to_all(halves, "dp", 0, 0, tiled=True, axis_index_groups=X_GROUPS)
     o0, o1, o2, o3 = tokens_grad(zz, mag, s_part, bt, u, weight)
 
-    pack, gb4 = call(
-        combine_kernel, "combine", [VMEM, VMEM, VMEM], [(PH, PW), (4, RANK, 128)]
+    pack, gb = call(
+        combine_kernel, "combine", [VMEM, VMEM, VMEM], [(PH, PW), (RANK, 128)]
     )(y, zz, mag)
-    gb4, o1, o2, o3 = lax.optimization_barrier((gb4, o1, o2, o3))
-    gb4 = lax.all_to_all(gb4, "col", 0, 0, tiled=True)
-    arrived = [
-        lax.ppermute(o, "col", [(i, (i + d) % 4) for i in range(4)])
-        for d, o in ((1, o1), (2, o2), (3, o3))
-    ]
-    first, third, gb4 = lax.optimization_barrier((arrived[0], arrived[2], gb4))
+    gb, o1, o2, o3 = lax.optimization_barrier((gb, o1, o2, o3))
+    gbs = [gb] + [from_col(gb, d) for d in (1, 2, 3)]
+    arrived = [from_col(o, d) for d, o in ((1, o1), (2, o2), (3, o3))]
+    first, third, gbs[0] = lax.optimization_barrier((arrived[0], arrived[2], gbs[0]))
     arrived = [first, arrived[1], third]
-    packs = call(spread_kernel, "spread", [VMEM, VMEM], [(4, PH, PW)])(pack, gb4)
+    packs = call(spread_kernel, "spread", [VMEM] * 5, [((4, PH, PW), F32)])(pack, *gbs)
     own = lax.all_to_all(packs, "dp", 0, 0, tiled=True, axis_index_groups=X_GROUPS)
     other = lax.ppermute(own, "dp", CORE_FLIP)
     grad_a, gm, gbt = call(

time: 89 us -> 86.8 us (0.975)
  blocking collectives: 24.1 us -> 16.6 us
  waiting for transfers between devices: 17.4 us -> 20.8 us
  starting transfers between devices: 22.6 us -> 25.6 us
    all_to_all x2 -> x1, blocking collectives: 24.1 us -> 16.6 us  [shards(): parts = lax.all_to_all(part, 'row', 0, 0, tiled=True)]
    ppermute x4 -> x7, waiting for transfers between devices: 1.38 us -> 5.18 us  [the longest x6 3.8 us: from_col(): return lax.ppermute(x, 'col', [(i, (i + d) % 4) for i in range(4)])]
    ppermute x4 -> x7, starting transfers between devices: 7.24 us -> 10.2 us  [the longest x6 6.83 us: from_col(): return lax.ppermute(x, 'col', [(i, (i + d) % 4) for i in range(4)])]
    pallas_call x2 -> x4, Pallas kernels: 0.83 us -> 2.3 us  [the longest x1 0.8 us: shards(): call(add_kernel, 'add', [VMEM, VMEM], [((4, PH, PW), F32)])(keep, other)]
    pallas_call x1, Pallas kernels: 6.37 us -> 5.33 us  [factors(): call(second_kernel, 'factors', [VMEM] * 6 + [HBM], [(4, PH, PW), (4, PH,...]
  transfers between devices with their start and end apart: 8 -> 11, of which waited for: 5 -> 8; matrix products, arithmetic and copies ran while one was open for 1% -> 1% of each run, Pallas kernels for 5% -> 5%
where the time goes in v3:
time: 86.8 us; the launch traced here: 86.3 us
  starting transfers between devices  25.6 us (29%)
  Pallas kernels  21 us (24%)
  waiting for transfers between devices  20.8 us (24%)
  blocking collectives  16.6 us (19%)
    all_to_all x1, blocking collectives, shards(): parts = lax.all_to_all(part, 'row', 0, 0, tiled=True)  16.6 us
    pallas_call x1, Pallas kernels, norms(): call(first_kernel, 'norms', [HBM, HBM, HBM, HBM, HBM], [((NC, 8, CW), F32...  8.05 us
    all_to_all x1, waiting for transfers between devices, shards(): zz = lax.all_to_all(sums, 'row', 0, 0, tiled=True)  7.91 us
    ppermute x6, starting transfers between devices, from_col(): return lax.ppermute(x, 'col', [(i, (i + d) % 4) for i in range(4)])  6.83 us
    pallas_call x1, Pallas kernels, factors(): call(second_kernel, 'factors', [VMEM] * 6 + [HBM], [(4, PH, PW), (4, PH,...  5.33 us
    all_to_all x1, waiting for transfers between devices, shards(): lax.all_to_all(packs, 'dp', 0, 0, tiled=True, axis_index_groups=X_GROUPS)  4.95 us
    ppermute x1, starting transfers between devices, shards(): other = lax.ppermute(own, 'dp', CORE_FLIP)  4.55 us
    pallas_call x1, Pallas kernels, tokens_grad(): call(third_kernel, 'tokens_grad', [VMEM] * 5 + [HBM], [(TOK, 256)] * 4, (...  4.42 us
  transfers between devices with their start and end apart: 11, of which 8 were waited for; matrix products, arithmetic and copies ran while one was open for 1% of the time, Pallas kernels for 5%

profile of v3, /device:TPU:1, one launch (start us, length us, event | category | flops | bytes accessed | tf_op | source)
XLA Modules:
  0.0 86.3 jit_solution(17387641002251083203)
XLA Ops:
  0.6 0.0 copy-start.2
  0.6 8.1 %norms.1 = (f32[8,8,512]{2,1,0:T(8,128)S(1)}, bf16[256,1024]{1,0:T(8,128)(2,1)S(1)}, bf16[32,1024]{1,0:T(8,128)(2,1)S(1)}, bf16[32,3712]{1,0:T(8,128)(2,1)S(1)}, bf16[256,3712]{1,0:T(8,128)(2,1)S(1)}) custom-call(bf16[256,1024]{1,0:T(8,128)(2,1)} %tok_h.1, bf16[32,1024]{1,0:T(8,128)(2,1)} %bitcast.3, bf16[32,3712]{1,0:T(8,128)(2,1)} %a_h.1, ...), custom_call_target="tpu_custom_call" | custom-call | flops 3892314112 | bytes 10000000 | tf_op jit(solution)/shard_map/norms/pallas_call | solution.py:248
  8.7 0.0 copy-start
  8.7 16.6 %all_to_all.20.parts = f32[8,8,512]{2,1,0:T(8,128)S(1)} all-to-all(f32[8,8,512]{2,1,0:T(8,128)S(1)} %get-tuple-element.30), channel_id=1, replica_groups=mesh['dp'=8,'row'=8,'col'=4] {'row'}, dimensions={0} | all-to-all | bytes 262144 | tf_op jit(solution)/shard_map/all_to_all | solution.py:310
  25.3 0.7 sum.1
  26.0 3.4 %all-to-all-start.1 = ((f32[8,8,512]{2,1,0:T(8,128)}), f32[8,8,512]{2,1,0:T(8,128)S(1)}, u32[]{:S(2)}, u32[]{:S(2)}) async-start(f32[8,8,512]{2,1,0:T(8,128)} %sum.1), calls=%async_computation.1 | async-start | bytes 262144 | tf_op jit(solution)/shard_map/all_to_all | solution.py:312
  29.3 0.0 copy-done.2
  29.4 7.9 %all-to-all-done.1.zz = f32[8,8,512]{2,1,0:T(8,128)S(1)} async-done(((f32[8,8,512]{2,1,0:T(8,128)}), f32[8,8,512]{2,1,0:T(8,128)S(1)}, u32[]{:S(2)}, u32[]{:S(2)}) %all-to-all-start.1) | async-done | bytes 131104 | tf_op jit(solution)/shard_map/all_to_all | solution.py:312
  37.3 5.3 %factors.1 = (f32[4,40,640]{2,1,0:T(8,128)S(1)}, f32[4,40,640]{2,1,0:T(8,128)S(1)}, f32[32,256]{1,0:T(8,128)S(1)}) custom-call(f32[8,8,512]{2,1,0:T(8,128)S(1)} %all-to-all-done.1.zz, f32[8,512]{1,0:T(8,128)S(1)} %reshape.11.mag, bf16[256,1024]{1,0:T(8,128)(2,1)S(1)} %get-tuple-element.31.tok, bf16[32,1024]{1,0:T(8,128)(2,1)S(1)} %get-tuple-element.32.bt, ...), custom_call_target="tpu_custom_call" | custom-call | flops 3892314112 | bytes 10000000 | tf_op jit(solution)/shard_map/factors/pallas_call | solution.py:272
  42.6 0.0 copy-done
  42.6 3.4 %collective-permute-start = (f32[4,40,640]{2,1,0:T(8,128)S(1)}, f32[4,40,640]{2,1,0:T(8,128)S(1)}, u32[]{:S(2)}, u32[]{:S(2)}) collective-permute-start(f32[4,40,640]{2,1,0:T(8,128)S(1)} %get-tuple-element.36), channel_id=1, source_target_pairs={{0,32},{32,0},{64,96},{96,64},{128,160},{160,128},{192,224},{224,1... | collective-permute-start | bytes 1228808 | tf_op jit(solution)/shard_map/ppermute | solution.py:315
  46.1 1.4 %collective-permute-done.b = f32[4,40,640]{2,1,0:T(8,128)S(1)} collective-permute-done((f32[4,40,640]{2,1,0:T(8,128)S(1)}, f32[4,40,640]{2,1,0:T(8,128)S(1)}, u32[]{:S(2)}, u32[]{:S(2)}) %collective-permute-start) | collective-permute-done | bytes 409632 | tf_op jit(solution)/shard_map/ppermute | solution.py:315
  47.4 0.8 add.18
  48.2 4.0 %all-to-all-start.2 = ((f32[4,40,640]{2,1,0:T(8,128)}), f32[4,40,640]{2,1,0:T(8,128)S(1)}, u32[]{:S(2)}, u32[]{:S(2)}) async-start(f32[4,40,640]{2,1,0:T(8,128)} %add.18), calls=%async_computation.2 | async-start | bytes 819200 | tf_op jit(solution)/shard_map/all_to_all | solution.py:318
  52.2 0.0 copy-start.1
  52.2 0.8 copy-done.1
  53.1 4.4 %tokens_grad.1 = (f32[256,256]{1,0:T(8,128)S(1)}, f32[256,256]{1,0:T(8,128)S(1)}, f32[256,256]{1,0:T(8,128)S(1)}, f32[256,256]{1,0:T(8,128)S(1)}) custom-call(f32[8,8,512]{2,1,0:T(8,128)S(1)} %all-to-all-done.1.zz, f32[8,512]{1,0:T(8,128)S(1)} %reshape.11.mag, f32[32,256]{1,0:T(8,128)S(1)} %get-tuple-element.38.s_ref, bf16[32,1024]{1,0:T(8,128)(2,1)S(1)} %copy-done.1, ...), custom_call_target="tpu_custom_call" | custom-call | flops 3892314112 | bytes 10000000 | tf_op jit(solution)/shard_map/tokens_grad/pallas_call | solution.py:288
  57.5 2.1 %all-to-all-done.2.y = f32[4,40,640]{2,1,0:T(8,128)S(1)} async-done(((f32[4,40,640]{2,1,0:T(8,128)}), f32[4,40,640]{2,1,0:T(8,128)S(1)}, u32[]{:S(2)}, u32[]{:S(2)}) %all-to-all-start.2) | async-done | bytes 409632 | tf_op jit(solution)/shard_map/all_to_all | solution.py:318
  59.7 1.6 %collective-permute-start.1 = (f32[256,256]{1,0:T(8,128)S(1)}, f32[256,256]{1,0:T(8,128)S(1)}, u32[]{:S(2)}, u32[]{:S(2)}) collective-permute-start(f32[256,256]{1,0:T(8,128)S(1)} %get-tuple-element.45), channel_id=1, source_target_pairs={{0,1},{1,2},{2,3},{3,0},{4,5},{5,6},{6,7},{7,4},{8,9},{9,10},{10,1... | collective-permute-start | bytes 786440 | tf_op jit(solution)/shard_map/ppermute | solution.py:303
  61.2 1.5 %collective-permute-start.2 = (f32[256,256]{1,0:T(8,128)S(1)}, f32[256,256]{1,0:T(8,128)S(1)}, u32[]{:S(2)}, u32[]{:S(2)}) collective-permute-start(f32[256,256]{1,0:T(8,128)S(1)} %get-tuple-element.46), channel_id=1, source_target_pairs={{0,3},{1,0},{2,1},{3,2},{4,7},{5,4},{6,5},{7,6},{8,11},{9,8},{10,9... | collective-permute-start | bytes 786440 | tf_op jit(solution)/shard_map/ppermute | solution.py:303
  62.8 1.4 %collective-permute-start.6 = (f32[32,128]{1,0:T(8,128)S(1)}, f32[32,128]{1,0:T(8,128)S(1)}, u32[]{:S(2)}, u32[]{:S(2)}) collective-permute-start(f32[32,128]{1,0:T(8,128)S(1)} %get-tuple-element.52.g0), channel_id=1, source_target_pairs={{0,3},{1,0},{2,1},{3,2},{4,7},{5,4},{6,5},{7,6},{8,11},{9,8},{10,9... | collective-permute-start | bytes 49160 | tf_op jit(solution)/shard_map/ppermute | solution.py:303
  64.1 0.4 collective-permute-start.5
  64.5 0.7 collective-permute-start.4
  65.2 2.1 %collective-permute-done.1 = f32[256,256]{1,0:T(8,128)S(1)} collective-permute-done((f32[256,256]{1,0:T(8,128)S(1)}, f32[256,256]{1,0:T(8,128)S(1)}, u32[]{:S(2)}, u32[]{:S(2)}) %collective-permute-start.1) | collective-permute-done | bytes 262176 | tf_op jit(solution)/shard_map/ppermute | solution.py:303
  67.2 0.0 collective-permute-done.2
  67.2 0.0 collective-permute-done.6.g3
  67.3 1.1 %collective-permute-done.5.g2 = f32[32,128]{1,0:T(8,128)S(1)} collective-permute-done((f32[32,128]{1,0:T(8,128)S(1)}, f32[32,128]{1,0:T(8,128)S(1)}, u32[]{:S(2)}, u32[]{:S(2)}) %collective-permute-start.5) | collective-permute-done | bytes 16416 | tf_op jit(solution)/shard_map/ppermute | solution.py:303
  68.4 0.6 collective-permute-done.4.g1
  69.0 0.8 spread.1
  69.8 3.5 %all-to-all-start.3 = ((f32[4,40,640]{2,1,0:T(8,128)}), f32[4,40,640]{2,1,0:T(8,128)S(1)}, u32[]{:S(2)}, u32[]{:S(2)}) async-start(f32[4,40,640]{2,1,0:T(8,128)} %spread.1), calls=%async_computation.3 | async-start | bytes 819200 | tf_op jit(solution)/shard_map/all_to_all | solution.py:330
  73.2 1.3 %collective-permute-start.3 = (f32[256,256]{1,0:T(8,128)S(1)}, f32[256,256]{1,0:T(8,128)S(1)}, u32[]{:S(2)}, u32[]{:S(2)}) collective-permute-start(f32[256,256]{1,0:T(8,128)S(1)} %get-tuple-element.49), channel_id=1, source_target_pairs={{0,2},{1,3},{2,0},{3,1},{4,6},{5,7},{6,4},{7,5},{8,10},{9,11},{10,... | collective-permute-start | bytes 786440 | tf_op jit(solution)/shard_map/ppermute | solution.py:303
  74.6 4.9 %all-to-all-done.3.own = f32[4,40,640]{2,1,0:T(8,128)S(1)} async-done(((f32[4,40,640]{2,1,0:T(8,128)}), f32[4,40,640]{2,1,0:T(8,128)S(1)}, u32[]{:S(2)}, u32[]{:S(2)}) %all-to-all-start.3) | async-done | bytes 409632 | tf_op jit(solution)/shard_map/all_to_all | solution.py:330
  79.5 4.6 %collective-permute-start.7 = (f32[4,40,640]{2,1,0:T(8,128)S(1)}, f32[4,40,640]{2,1,0:T(8,128)S(1)}, u32[]{:S(2)}, u32[]{:S(2)}) collective-permute-start(f32[4,40,640]{2,1,0:T(8,128)S(1)} %all-to-all-done.3.own), channel_id=1, source_target_pairs={{0,32},{32,0},{64,96},{96,64},{128,160},{160,128},{192,224},{224,1... | collective-permute-start | bytes 1228808 | tf_op jit(solution)/shard_map/ppermute | solution.py:331
  84.1 0.0 collective-permute-done.3
  84.1 0.7 add_convert_fusion
  84.8 0.7 collective-permute-done.7.other
  85.4 0.9 %outputs.1 = (f32[32,3712]{1,0:T(8,128)}, f32[3712]{0:T(1024)}, f32[32,1024]{1,0:T(8,128)}) custom-call(f32[4,40,640]{2,1,0:T(8,128)S(1)} %all-to-all-done.3.own, f32[4,40,640]{2,1,0:T(8,128)S(1)} %collective-permute-done.7.other), custom_call_target="tpu_custom_call" | custom-call | tf_op jit(solution)/shard_map/outputs/pallas_call | solution.py:332
  (3 shorter events, 0.1 us)
Async XLA Ops:
  0.6 28.7 %copy-start.2 = (f32[3712]{0:T(1024)S(1)}, f32[3712]{0:T(1024)}, u32[]{:S(2)}) copy-start(f32[3712]{0:T(1024)} %param.11) | copy-start | bytes 44548
  8.7 33.9 %copy-start = (bf16[32,1024]{1,0:T(8,128)(2,1)}, bf16[32,1024]{1,0:T(8,128)(2,1)S(1)}, u32[]{:S(2)}) copy-start(bf16[32,1024]{1,0:T(8,128)(2,1)S(1)} %get-tuple-element.32.bt) | copy-start | bytes 196612
  26.0 11.3 %all-to-all-start.1 = ((f32[8,8,512]{2,1,0:T(8,128)}), f32[8,8,512]{2,1,0:T(8,128)S(1)}, u32[]{:S(2)}, u32[]{:S(2)}) async-start(f32[8,8,512]{2,1,0:T(8,128)} %sum.1), calls=%async_computation.1 | async-start | bytes 262144 | tf_op jit(solution)/shard_map/all_to_all | solution.py:312
  42.6 4.8 %collective-permute-start = (f32[4,40,640]{2,1,0:T(8,128)S(1)}, f32[4,40,640]{2,1,0:T(8,128)S(1)}, u32[]{:S(2)}, u32[]{:S(2)}) collective-permute-start(f32[4,40,640]{2,1,0:T(8,128)S(1)} %get-tuple-element.36), channel_id=1, source_target_pairs={{0,32},{32,0},{64,96},{96,64},{128,160},{160,128},{192,224},{224,1... | collective-permute-start | bytes 1228808 | tf_op jit(solution)/shard_map/ppermute | solution.py:315
  48.2 11.4 %all-to-all-start.2 = ((f32[4,40,640]{2,1,0:T(8,128)}), f32[4,40,640]{2,1,0:T(8,128)S(1)}, u32[]{:S(2)}, u32[]{:S(2)}) async-start(f32[4,40,640]{2,1,0:T(8,128)} %add.18), calls=%async_computation.2 | async-start | bytes 819200 | tf_op jit(solution)/shard_map/all_to_all | solution.py:318
  52.2 0.8 copy-start.1
  59.7 7.6 %collective-permute-start.1 = (f32[256,256]{1,0:T(8,128)S(1)}, f32[256,256]{1,0:T(8,128)S(1)}, u32[]{:S(2)}, u32[]{:S(2)}) collective-permute-start(f32[256,256]{1,0:T(8,128)S(1)} %get-tuple-element.45), channel_id=1, source_target_pairs={{0,1},{1,2},{2,3},{3,0},{4,5},{5,6},{6,7},{7,4},{8,9},{9,10},{10,1... | collective-permute-start | bytes 786440 | tf_op jit(solution)/shard_map/ppermute | solution.py:303
  61.2 6.0 %collective-permute-start.2 = (f32[256,256]{1,0:T(8,128)S(1)}, f32[256,256]{1,0:T(8,128)S(1)}, u32[]{:S(2)}, u32[]{:S(2)}) collective-permute-start(f32[256,256]{1,0:T(8,128)S(1)} %get-tuple-element.46), channel_id=1, source_target_pairs={{0,3},{1,0},{2,1},{3,2},{4,7},{5,4},{6,5},{7,6},{8,11},{9,8},{10,9... | collective-permute-start | bytes 786440 | tf_op jit(solution)/shard_map/ppermute | solution.py:303
  62.8 4.5 %collective-permute-start.6 = (f32[32,128]{1,0:T(8,128)S(1)}, f32[32,128]{1,0:T(8,128)S(1)}, u32[]{:S(2)}, u32[]{:S(2)}) collective-permute-start(f32[32,128]{1,0:T(8,128)S(1)} %get-tuple-element.52.g0), channel_id=1, source_target_pairs={{0,3},{1,0},{2,1},{3,2},{4,7},{5,4},{6,5},{7,6},{8,11},{9,8},{10,9... | collective-permute-start | bytes 49160 | tf_op jit(solution)/shard_map/ppermute | solution.py:303
  64.1 4.3 %collective-permute-start.5 = (f32[32,128]{1,0:T(8,128)S(1)}, f32[32,128]{1,0:T(8,128)S(1)}, u32[]{:S(2)}, u32[]{:S(2)}) collective-permute-start(f32[32,128]{1,0:T(8,128)S(1)} %get-tuple-element.52.g0), channel_id=1, source_target_pairs={{0,2},{1,3},{2,0},{3,1},{4,6},{5,7},{6,4},{7,5},{8,10},{9,11},{10,... | collective-permute-start | bytes 49160 | tf_op jit(solution)/shard_map/ppermute | solution.py:303
  64.5 4.5 %collective-permute-start.4 = (f32[32,128]{1,0:T(8,128)S(1)}, f32[32,128]{1,0:T(8,128)S(1)}, u32[]{:S(2)}, u32[]{:S(2)}) collective-permute-start(f32[32,128]{1,0:T(8,128)S(1)} %get-tuple-element.52.g0), channel_id=1, source_target_pairs={{0,1},{1,2},{2,3},{3,0},{4,5},{5,6},{6,7},{7,4},{8,9},{9,10},{10,1... | collective-permute-start | bytes 49160 | tf_op jit(solution)/shard_map/ppermute | solution.py:303
  69.8 9.8 %all-to-all-start.3 = ((f32[4,40,640]{2,1,0:T(8,128)}), f32[4,40,640]{2,1,0:T(8,128)S(1)}, u32[]{:S(2)}, u32[]{:S(2)}) async-start(f32[4,40,640]{2,1,0:T(8,128)} %spread.1), calls=%async_computation.3 | async-start | bytes 819200 | tf_op jit(solution)/shard_map/all_to_all | solution.py:330
  73.2 10.8 %collective-permute-start.3 = (f32[256,256]{1,0:T(8,128)S(1)}, f32[256,256]{1,0:T(8,128)S(1)}, u32[]{:S(2)}, u32[]{:S(2)}) collective-permute-start(f32[256,256]{1,0:T(8,128)S(1)} %get-tuple-element.49), channel_id=1, source_target_pairs={{0,2},{1,3},{2,0},{3,1},{4,6},{5,7},{6,4},{7,5},{8,10},{9,11},{10,... | collective-permute-start | bytes 786440 | tf_op jit(solution)/shard_map/ppermute | solution.py:303
  79.5 5.9 %collective-permute-start.7 = (f32[4,40,640]{2,1,0:T(8,128)S(1)}, f32[4,40,640]{2,1,0:T(8,128)S(1)}, u32[]{:S(2)}, u32[]{:S(2)}) collective-permute-start(f32[4,40,640]{2,1,0:T(8,128)S(1)} %all-to-all-done.3.own), channel_id=1, source_target_pairs={{0,32},{32,0},{64,96},{96,64},{128,160},{160,128},{192,224},{224,1... | collective-permute-start | bytes 1228808 | tf_op jit(solution)/shard_map/ppermute | solution.py:331

commit v4 on v3

--- a/solution.py
+++ b/solution.py
@@ -17,7 +17,6 @@
 WIDTHS = [min(CW, COLS - CW * c) for c in range(NC)]
 PW = CW + 128
 PH = 40
-X_GROUPS = [[0, 2, 4, 6], [1, 3, 5, 7]]
 CORE_FLIP = [(i, i ^ 1) for i in range(8)]
 F32, BF16 = jnp.float32, jnp.bfloat16
 NN = (((1,), (0,)), ((), ()))
@@ -123,8 +122,11 @@
         out[r] = total
 
 
-def add_kernel(a, b, out):
-    out[...] = a[...] + b[...]
+def add_kernel(a, b, *outs):
+    x = dp_place() // 2
+    for d, out in enumerate(outs):
+        part = lax.rem(x + d, 4)
+        out[...] = a[part] + b[part]
 
 
 def second_kernel(zz, mag, tok, bt, a, u, w_h, keep, send, s_out, g_v, t_v, w, sems):
@@ -169,23 +171,27 @@
         send[x] = g_v[2 * x + 1 - core]
 
 
-def third_kernel(zz, mag, s_ref, bt, u, w_h, o0, o1, o2, o3, acc, w, sems):
+def third_kernel(zz, mag, s_ref, bt_h, u, w_h, o0, o1, o2, o3, acc, w, bt, sems, small):
     copies = columns(w_h, w, sems)
-    acc[...] = mm(s_ref[...].astype(BF16), bt[...] * BF16(SCALE), TN)
+    last = pltpu.make_async_copy(bt_h, bt, small.at[0])
+    last.start()
+    acc[...] = jnp.zeros((TOK, ROWS), F32)
     for c in range(NC):
         n = WIDTHS[c]
         ratio = mag[c : c + 1, :n] / jnp.sqrt(zz[c, 0:1, :n] + EPS)
         scaled = (u[:, span(c)].astype(F32) * ratio).astype(BF16)
         copies[c].wait()
         acc[...] += mm(scaled, w[:, span(c)], NT)
+    last.wait()
+    acc[...] += mm(s_ref[...].astype(BF16), bt[...] * BF16(SCALE), TN)
     for d, o in enumerate((o0, o1, o2, o3)):
         part = lax.rem(lax.axis_index("col") + d, 4)
         o[...] = acc[:, pl.ds(pl.multiple_of(part * 256, 256), 256)]
 
 
-def combine_kernel(y, zz, mag, pack, gb):
+def combine_kernel(y0, y1, y2, y3, zz, mag, pack, gb):
     s = dp_place()
-    total = (y[0] + y[1]) + (y[2] + y[3])
+    total = (y0[...] + y1[...]) + (y2[...] + y3[...])
     mine = zz[s]
     normsq = mine[0:1] + EPS
     root = jnp.sqrt(normsq)
@@ -201,22 +207,22 @@
     gb[...] = total[:RANK, CW:]
 
 
-def spread_kernel(pack, g0, g1, g2, g3, out):
-    gb = (g0[...] + g1[...]) + (g2[...] + g3[...])
-    for i in range(4):
-        out[i] = pack[...]
-        out[i, :RANK, CW:] = gb
-
-
-def last_kernel(own, other, ga, gm, gb):
-    even = dp_place() % 2 == 0
+def finish_kernel(pack, g0, g1, g2, g3, out):
+    out[...] = pack[...]
+    out[:RANK, CW:] = (g0[...] + g1[...]) + (g2[...] + g3[...])
+
+
+def last_kernel(p0, p1, p2, p3, f0, f1, f2, f3, ga, gm, gb, both):
+    place = dp_place()
+    core = lax.rem(place, 2)
+    for d, (own, other) in enumerate(((p0, f0), (p1, f1), (p2, f2), (p3, f3))):
+        x = lax.rem(place // 2 + 4 - d, 4)
+        both[2 * x + core] = own[...]
+        both[2 * x + 1 - core] = other[...]
     for c in range(NC):
-        mine = own if c % 2 == 0 else other
-        theirs = other if c % 2 == 0 else own
-        chunk = jnp.where(even, mine[c // 2], theirs[c // 2])
-        ga[:, span(c)] = chunk[:RANK, : WIDTHS[c]]
-        gm[span(c)] = chunk[RANK, : WIDTHS[c]]
-        gb[:, 128 * c : 128 * (c + 1)] = chunk[:RANK, CW:]
+        ga[:, span(c)] = both[c, :RANK, : WIDTHS[c]]
+        gm[span(c)] = both[c, RANK, : WIDTHS[c]]
+        gb[:, 128 * c : 128 * (c + 1)] = both[c, :RANK, CW:]
 
 
 def call(kernel, name, ins, outs, scratch=(), cost=None, limit=32):
@@ -288,15 +294,21 @@
     return call(
         third_kernel,
         "tokens_grad",
-        [VMEM] * 5 + [HBM],
+        [VMEM] * 3 + [HBM, VMEM, HBM],
         [(TOK, 256)] * 4,
         (
             pltpu.VMEM((TOK, ROWS), F32),
             pltpu.VMEM((ROWS, COLS), BF16),
+            pltpu.VMEM((RANK, ROWS), BF16),
             pltpu.SemaphoreType.DMA((NC,)),
+            pltpu.SemaphoreType.DMA((1,)),
         ),
         COST,
-    )(zz, mag, s_part, bt, u, in_hbm(weight))
+    )(zz, mag, s_part, in_hbm(bt), u, in_hbm(weight))
+
+
+def along_x(x, d):
+    return lax.ppermute(x, "dp", [(i, (i + 2 * d) % 8) for i in range(8)])
 
 
 def from_col(x, d):
@@ -306,32 +318,36 @@
 def shards(tokens, upstream, weight, factor_b, factor_a, magnitude):
     mag = jnp.pad(magnitude, (0, NC * CW - COLS)).reshape(NC, CW)
     bt = factor_b.T
-    part, tok, bt, a, u = norms(tokens, bt, factor_a, weight, upstream)
+    part, tok, bt_near, a, u = norms(tokens, bt, factor_a, weight, upstream)
     parts = lax.all_to_all(part, "row", 0, 0, tiled=True)
     sums = call(sum_kernel, "sum", [VMEM], [((NC, 8, CW), F32)])(parts)
     zz = lax.all_to_all(sums, "row", 0, 0, tiled=True)
 
-    keep, send, s_part = factors(zz, mag, tok, bt, a, u, weight)
+    keep, send, s_part = factors(zz, mag, tok, bt_near, a, u, weight)
     other = lax.ppermute(send, "dp", CORE_FLIP)
-    halves = call(add_kernel, "add", [VMEM, VMEM], [((4, PH, PW), F32)])(keep, other)
+    halves = call(add_kernel, "add", [VMEM, VMEM], [(PH, PW)] * 4)(keep, other)
     halves, s_part = lax.optimization_barrier((halves, s_part))
-    y = lax.all_to_all(halves, "dp", 0, 0, tiled=True, axis_index_groups=X_GROUPS)
+    y = [halves[0]] + [along_x(halves[d], d) for d in (1, 2, 3)]
     o0, o1, o2, o3 = tokens_grad(zz, mag, s_part, bt, u, weight)
 
     pack, gb = call(
-        combine_kernel, "combine", [VMEM, VMEM, VMEM], [(PH, PW), (RANK, 128)]
-    )(y, zz, mag)
+        combine_kernel, "combine", [VMEM] * 6, [(PH, PW), (RANK, 128)]
+    )(*y, zz, mag)
     gb, o1, o2, o3 = lax.optimization_barrier((gb, o1, o2, o3))
     gbs = [gb] + [from_col(gb, d) for d in (1, 2, 3)]
-    arrived = [from_col(o, d) for d, o in ((1, o1), (2, o2), (3, o3))]
-    first, third, gbs[0] = lax.optimization_barrier((arrived[0], arrived[2], gbs[0]))
-    arrived = [first, arrived[1], third]
-    packs = call(spread_kernel, "spread", [VMEM] * 5, [((4, PH, PW), F32)])(pack, *gbs)
-    own = lax.all_to_all(packs, "dp", 0, 0, tiled=True, axis_index_groups=X_GROUPS)
-    other = lax.ppermute(own, "dp", CORE_FLIP)
+    first, third, gbs[0] = lax.optimization_barrier((from_col(o1, 1), from_col(o3, 3), gbs[0]))
+    pack = call(finish_kernel, "finish", [VMEM] * 5, [(PH, PW)])(pack, *gbs)
+    pack, o2 = lax.optimization_barrier((pack, o2))
+    arrived = [first, from_col(o2, 2), third]
+    own = [pack] + [along_x(pack, d) for d in (1, 2, 3)]
+    other = [lax.ppermute(p, "dp", CORE_FLIP) for p in own]
     grad_a, gm, gbt = call(
-        last_kernel, "outputs", [VMEM, VMEM], [(RANK, COLS), (COLS,), (RANK, ROWS)]
-    )(own, other)
+        last_kernel,
+        "outputs",
+        [VMEM] * 8,
+        [(RANK, COLS), (COLS,), (RANK, ROWS)],
+        (pltpu.VMEM((NC, PH, PW), F32),),
+    )(*own, *other)
     grad_tokens = ((o0 + arrived[0]) + (arrived[1] + arrived[2])).astype(BF16)
     return grad_tokens, gm, grad_a, gbt.T
 

time: 86.8 us -> 82.2 us (0.947)
  waiting for transfers between devices: 20.8 us -> 14.1 us
  starting transfers between devices: 25.6 us -> 30 us
  Pallas kernels: 21 us -> 19.8 us
    ppermute x1 -> x10, starting transfers between devices: 4.55 us -> 16.4 us  [the longest x4 9.36 us: shards(): other = [lax.ppermute(p, 'dp', CORE_FLIP) for p in own]]
    all_to_all x2 -> x0, starting transfers between devices: 7.47 us -> none  [the longest x1 4.01 us: shards(): lax.all_to_all(halves, 'dp', 0, 0, tiled=True, axis_index_groups=X_GROUPS)]
    all_to_all x2 -> x0, waiting for transfers between devices: 7.06 us -> none  [the longest x1 4.95 us: shards(): lax.all_to_all(packs, 'dp', 0, 0, tiled=True, axis_index_groups=X_GROUPS)]
    pallas_call x5, Pallas kernels: 6.92 us -> 5.71 us  [the longest x1 4.65 us: tokens_grad(): call(third_kernel, 'tokens_grad', [VMEM] * 3 + [HBM, VMEM, HBM], [(TOK, 2...]
  transfers between devices with their start and end apart: 11 -> 18, of which waited for: 8 -> 6; matrix products, arithmetic and copies ran while one was open for 1% -> 0% of each run, Pallas kernels for 5% -> 7%
where the time goes in v4:
time: 82.2 us; the launch traced here: 81.9 us
  starting transfers between devices  30 us (36%)
  Pallas kernels  19.8 us (24%)
  blocking collectives  16.6 us (20%)
  waiting for transfers between devices  14.1 us (17%)
    all_to_all x1, blocking collectives, shards(): parts = lax.all_to_all(part, 'row', 0, 0, tiled=True)  16.6 us
    ppermute x4, starting transfers between devices, shards(): other = [lax.ppermute(p, 'dp', CORE_FLIP) for p in own]  9.36 us
    pallas_call x1, Pallas kernels, norms(): call(first_kernel, 'norms', [HBM, HBM, HBM, HBM, HBM], [((NC, 8, CW), F32...  8.05 us
    all_to_all x1, waiting for transfers between devices, shards(): zz = lax.all_to_all(sums, 'row', 0, 0, tiled=True)  7.91 us
    ppermute x6, starting transfers between devices, along_x(): return lax.ppermute(x, 'dp', [(i, (i + 2 * d) % 8) for i in range(8)])  7.01 us
    ppermute x6, starting transfers between devices, from_col(): return lax.ppermute(x, 'col', [(i, (i + d) % 4) for i in range(4)])  6.87 us
    pallas_call x1, Pallas kernels, factors(): call(second_kernel, 'factors', [VMEM] * 6 + [HBM], [(4, PH, PW), (4, PH,...  5.33 us
    pallas_call x1, Pallas kernels, tokens_grad(): call(third_kernel, 'tokens_grad', [VMEM] * 3 + [HBM, VMEM, HBM], [(TOK, 2...  4.65 us
  transfers between devices with their start and end apart: 18, of which 6 were waited for; matrix products, arithmetic and copies ran while one was open for 0% of the time, Pallas kernels for 7%

profile of v4, /device:TPU:1, one launch (start us, length us, event | category | flops | bytes accessed | tf_op | source)
XLA Modules:
  0.0 81.9 jit_solution(18296098169802779002)
XLA Ops:
  0.6 0.0 copy-start
  0.6 8.1 %norms.1 = (f32[8,8,512]{2,1,0:T(8,128)S(1)}, bf16[256,1024]{1,0:T(8,128)(2,1)S(1)}, bf16[32,1024]{1,0:T(8,128)(2,1)S(1)}, bf16[32,3712]{1,0:T(8,128)(2,1)S(1)}, bf16[256,3712]{1,0:T(8,128)(2,1)S(1)}) custom-call(bf16[256,1024]{1,0:T(8,128)(2,1)} %tok_h.1, bf16[32,1024]{1,0:T(8,128)(2,1)} %bitcast.3, bf16[32,3712]{1,0:T(8,128)(2,1)} %a_h.1, ...), custom_call_target="tpu_custom_call" | custom-call | flops 3892314112 | bytes 10000000 | tf_op jit(solution)/shard_map/norms/pallas_call | solution.py:254
  8.7 16.6 %all_to_all.10.parts = f32[8,8,512]{2,1,0:T(8,128)S(1)} all-to-all(f32[8,8,512]{2,1,0:T(8,128)S(1)} %get-tuple-element.39), channel_id=1, replica_groups=mesh['dp'=8,'row'=8,'col'=4] {'row'}, dimensions={0} | all-to-all | bytes 262144 | tf_op jit(solution)/shard_map/all_to_all | solution.py:322
  25.3 0.7 sum.1
  26.0 3.4 %all-to-all-start.1 = ((f32[8,8,512]{2,1,0:T(8,128)}), f32[8,8,512]{2,1,0:T(8,128)S(1)}, u32[]{:S(2)}, u32[]{:S(2)}) async-start(f32[8,8,512]{2,1,0:T(8,128)} %sum.1), calls=%async_computation.1 | async-start | bytes 262144 | tf_op jit(solution)/shard_map/all_to_all | solution.py:324
  29.3 0.0 copy-done
  29.4 7.9 %all-to-all-done.1.zz = f32[8,8,512]{2,1,0:T(8,128)S(1)} async-done(((f32[8,8,512]{2,1,0:T(8,128)}), f32[8,8,512]{2,1,0:T(8,128)S(1)}, u32[]{:S(2)}, u32[]{:S(2)}) %all-to-all-start.1) | async-done | bytes 131104 | tf_op jit(solution)/shard_map/all_to_all | solution.py:324
  37.3 5.3 %factors.1 = (f32[4,40,640]{2,1,0:T(8,128)S(1)}, f32[4,40,640]{2,1,0:T(8,128)S(1)}, f32[32,256]{1,0:T(8,128)S(1)}) custom-call(f32[8,8,512]{2,1,0:T(8,128)S(1)} %all-to-all-done.1.zz, f32[8,512]{1,0:T(8,128)S(1)} %reshape.11.mag, bf16[256,1024]{1,0:T(8,128)(2,1)S(1)} %get-tuple-element.40.tok, bf16[32,1024]{1,0:T(8,128)(2,1)S(1)} %get-tuple-element.41.bt, ...), custom_call_target="tpu_custom_call" | custom-call | flops 3892314112 | bytes 10000000 | tf_op jit(solution)/shard_map/factors/pallas_call | solution.py:278
  42.6 3.4 %collective-permute-start = (f32[4,40,640]{2,1,0:T(8,128)S(1)}, f32[4,40,640]{2,1,0:T(8,128)S(1)}, u32[]{:S(2)}, u32[]{:S(2)}) collective-permute-start(f32[4,40,640]{2,1,0:T(8,128)S(1)} %get-tuple-element.45), channel_id=1, source_target_pairs={{0,32},{32,0},{64,96},{96,64},{128,160},{160,128},{192,224},{224,1... | collective-permute-start | bytes 1228808 | tf_op jit(solution)/shard_map/ppermute | solution.py:327
  46.0 1.4 %collective-permute-done.b = f32[4,40,640]{2,1,0:T(8,128)S(1)} collective-permute-done((f32[4,40,640]{2,1,0:T(8,128)S(1)}, f32[4,40,640]{2,1,0:T(8,128)S(1)}, u32[]{:S(2)}, u32[]{:S(2)}) %collective-permute-start) | collective-permute-done | bytes 409632 | tf_op jit(solution)/shard_map/ppermute | solution.py:327
  47.4 0.1 add.18
  47.5 1.3 %collective-permute-start.1 = (f32[40,640]{1,0:T(8,128)S(1)}, f32[40,640]{1,0:T(8,128)S(1)}, u32[]{:S(2)}, u32[]{:S(2)}) collective-permute-start(f32[40,640]{1,0:T(8,128)S(1)} %get-tuple-element.54), channel_id=1, source_target_pairs={{0,64},{32,96},{64,128},{96,160},{128,192},{160,224},{192,0},{224,... | collective-permute-start | bytes 307208 | tf_op jit(solution)/shard_map/ppermute | solution.py:311
  48.7 2.5 %collective-permute-start.2 = (f32[40,640]{1,0:T(8,128)S(1)}, f32[40,640]{1,0:T(8,128)S(1)}, u32[]{:S(2)}, u32[]{:S(2)}) collective-permute-start(f32[40,640]{1,0:T(8,128)S(1)} %get-tuple-element.55), channel_id=1, source_target_pairs={{0,128},{32,160},{64,192},{96,224},{128,0},{160,32},{192,64},{224,... | collective-permute-start | bytes 307208 | tf_op jit(solution)/shard_map/ppermute | solution.py:311
  51.2 1.2 %collective-permute-start.3 = (f32[40,640]{1,0:T(8,128)S(1)}, f32[40,640]{1,0:T(8,128)S(1)}, u32[]{:S(2)}, u32[]{:S(2)}) collective-permute-start(f32[40,640]{1,0:T(8,128)S(1)} %get-tuple-element.56), channel_id=1, source_target_pairs={{0,192},{32,224},{64,0},{96,32},{128,64},{160,96},{192,128},{224,1... | collective-permute-start | bytes 307208 | tf_op jit(solution)/shard_map/ppermute | solution.py:311
  52.4 4.6 %tokens_grad.1 = (f32[256,256]{1,0:T(8,128)S(1)}, f32[256,256]{1,0:T(8,128)S(1)}, f32[256,256]{1,0:T(8,128)S(1)}, f32[256,256]{1,0:T(8,128)S(1)}) custom-call(f32[8,8,512]{2,1,0:T(8,128)S(1)} %all-to-all-done.1.zz, f32[8,512]{1,0:T(8,128)S(1)} %reshape.11.mag, f32[32,256]{1,0:T(8,128)S(1)} %get-tuple-element.51.s_ref, bf16[32,1024]{1,0:T(8,128)(2,1)} %bitcast.4, ...), custom_call_target="tpu_custom_call" | custom-call | flops 3892314112 | bytes 10000000 | tf_op jit(solution)/shard_map/tokens_grad/pallas_call | solution.py:294
  57.0 0.0 collective-permute-done.1.y1
  57.0 0.0 collective-permute-done.2.y2
  57.0 0.0 collective-permute-done.3.y3
  57.0 0.1 combine.1
  57.1 1.4 %collective-permute-start.4 = (f32[256,256]{1,0:T(8,128)S(1)}, f32[256,256]{1,0:T(8,128)S(1)}, u32[]{:S(2)}, u32[]{:S(2)}) collective-permute-start(f32[256,256]{1,0:T(8,128)S(1)} %get-tuple-element.61), channel_id=1, source_target_pairs={{0,1},{1,2},{2,3},{3,0},{4,5},{5,6},{6,7},{7,4},{8,9},{9,10},{10,1... | collective-permute-start | bytes 786440 | tf_op jit(solution)/shard_map/ppermute | solution.py:315
  58.5 1.5 %collective-permute-start.5 = (f32[256,256]{1,0:T(8,128)S(1)}, f32[256,256]{1,0:T(8,128)S(1)}, u32[]{:S(2)}, u32[]{:S(2)}) collective-permute-start(f32[256,256]{1,0:T(8,128)S(1)} %get-tuple-element.62), channel_id=1, source_target_pairs={{0,3},{1,0},{2,1},{3,2},{4,7},{5,4},{6,5},{7,6},{8,11},{9,8},{10,9... | collective-permute-start | bytes 786440 | tf_op jit(solution)/shard_map/ppermute | solution.py:315
  60.0 1.4 %collective-permute-start.8 = (f32[32,128]{1,0:T(8,128)S(1)}, f32[32,128]{1,0:T(8,128)S(1)}, u32[]{:S(2)}, u32[]{:S(2)}) collective-permute-start(f32[32,128]{1,0:T(8,128)S(1)} %get-tuple-element.66.g0), channel_id=1, source_target_pairs={{0,3},{1,0},{2,1},{3,2},{4,7},{5,4},{6,5},{7,6},{8,11},{9,8},{10,9... | collective-permute-start | bytes 49160 | tf_op jit(solution)/shard_map/ppermute | solution.py:315
  61.4 0.4 collective-permute-start.7
  61.7 0.7 collective-permute-start.6
  62.4 2.7 %collective-permute-done.4 = f32[256,256]{1,0:T(8,128)S(1)} collective-permute-done((f32[256,256]{1,0:T(8,128)S(1)}, f32[256,256]{1,0:T(8,128)S(1)}, u32[]{:S(2)}, u32[]{:S(2)}) %collective-permute-start.4) | collective-permute-done | bytes 262176 | tf_op jit(solution)/shard_map/ppermute | solution.py:315
  65.1 0.0 collective-permute-done.5
  65.1 0.1 collective-permute-done.8.g3
  65.1 1.1 %collective-permute-done.7.g2 = f32[32,128]{1,0:T(8,128)S(1)} collective-permute-done((f32[32,128]{1,0:T(8,128)S(1)}, f32[32,128]{1,0:T(8,128)S(1)}, u32[]{:S(2)}, u32[]{:S(2)}) %collective-permute-start.7) | collective-permute-done | bytes 16416 | tf_op jit(solution)/shard_map/ppermute | solution.py:315
  66.3 0.0 collective-permute-done.6.g1
  66.3 1.6 %collective-permute-start.9 = (f32[256,256]{1,0:T(8,128)S(1)}, f32[256,256]{1,0:T(8,128)S(1)}, u32[]{:S(2)}, u32[]{:S(2)}) collective-permute-start(f32[256,256]{1,0:T(8,128)S(1)} %get-tuple-element.68), channel_id=1, source_target_pairs={{0,2},{1,3},{2,0},{3,1},{4,6},{5,7},{6,4},{7,5},{8,10},{9,11},{10,... | collective-permute-start | bytes 786440 | tf_op jit(solution)/shard_map/ppermute | solution.py:315
  67.8 0.5 collective-permute-start.12
  68.3 1.7 %collective-permute-start.11 = (f32[40,640]{1,0:T(8,128)S(1)}, f32[40,640]{1,0:T(8,128)S(1)}, u32[]{:S(2)}, u32[]{:S(2)}) collective-permute-start(f32[40,640]{1,0:T(8,128)S(1)} %finish.1.p0), channel_id=1, source_target_pairs={{0,128},{32,160},{64,192},{96,224},{128,0},{160,32},{192,64},{224,... | collective-permute-start | bytes 307208 | tf_op jit(solution)/shard_map/ppermute | solution.py:311
  70.0 0.0 collective-permute-start.10
  70.0 3.9 %collective-permute-start.13 = (f32[40,640]{1,0:T(8,128)S(1)}, f32[40,640]{1,0:T(8,128)S(1)}, u32[]{:S(2)}, u32[]{:S(2)}) collective-permute-start(f32[40,640]{1,0:T(8,128)S(1)} %finish.1.p0), channel_id=1, source_target_pairs={{0,32},{32,0},{64,96},{96,64},{128,160},{160,128},{192,224},{224,1... | collective-permute-start | bytes 307208 | tf_op jit(solution)/shard_map/ppermute | solution.py:343
  73.9 0.0 collective-permute-done.12.p3
  73.9 1.6 %collective-permute-start.16 = (f32[40,640]{1,0:T(8,128)S(1)}, f32[40,640]{1,0:T(8,128)S(1)}, u32[]{:S(2)}, u32[]{:S(2)}) collective-permute-start(f32[40,640]{1,0:T(8,128)S(1)} %collective-permute-done.12.p3), channel_id=1, source_target_pairs={{0,32},{32,0},{64,96},{96,64},{128,160},{160,128},{192,224},{224,1... | collective-permute-start | bytes 307208 | tf_op jit(solution)/shard_map/ppermute | solution.py:343
  75.4 0.0 collective-permute-done.11.p2
  75.5 2.8 %collective-permute-start.15 = (f32[40,640]{1,0:T(8,128)S(1)}, f32[40,640]{1,0:T(8,128)S(1)}, u32[]{:S(2)}, u32[]{:S(2)}) collective-permute-start(f32[40,640]{1,0:T(8,128)S(1)} %collective-permute-done.11.p2), channel_id=1, source_target_pairs={{0,32},{32,0},{64,96},{96,64},{128,160},{160,128},{192,224},{224,1... | collective-permute-start | bytes 307208 | tf_op jit(solution)/shard_map/ppermute | solution.py:343
  78.2 0.0 collective-permute-done.10.p1
  78.2 1.1 %collective-permute-start.14 = (f32[40,640]{1,0:T(8,128)S(1)}, f32[40,640]{1,0:T(8,128)S(1)}, u32[]{:S(2)}, u32[]{:S(2)}) collective-permute-start(f32[40,640]{1,0:T(8,128)S(1)} %collective-permute-done.10.p1), channel_id=1, source_target_pairs={{0,32},{32,0},{64,96},{96,64},{128,160},{160,128},{192,224},{224,1... | collective-permute-start | bytes 307208 | tf_op jit(solution)/shard_map/ppermute | solution.py:343
  79.3 0.0 collective-permute-done.13.f0
  79.3 0.0 collective-permute-done.16.f3
  79.3 0.0 collective-permute-done.15.f2
  79.4 0.9 %collective-permute-done.14.f1 = f32[40,640]{1,0:T(8,128)S(1)} collective-permute-done((f32[40,640]{1,0:T(8,128)S(1)}, f32[40,640]{1,0:T(8,128)S(1)}, u32[]{:S(2)}, u32[]{:S(2)}) %collective-permute-start.14) | collective-permute-done | bytes 102432 | tf_op jit(solution)/shard_map/ppermute | solution.py:343
  80.3 0.9 %outputs.1 = (f32[32,3712]{1,0:T(8,128)}, f32[3712]{0:T(1024)}, f32[32,1024]{1,0:T(8,128)}) custom-call(f32[40,640]{1,0:T(8,128)S(1)} %finish.1.p0, f32[40,640]{1,0:T(8,128)S(1)} %collective-permute-done.10.p1, f32[40,640]{1,0:T(8,128)S(1)} %collective-permute-done.11.p2, f32[40,640]{1,0:T(8,128)S(1)} %collective-permute-done.12.p3, ...), custom_call_target="tpu_custom_call" | custom-call | tf_op jit(solution)/shard_map/outputs/pallas_call | solution.py:344
  81.2 0.0 collective-permute-done.9
  81.2 0.7 add_convert_fusion
  (3 shorter events, 0.0 us)
Async XLA Ops:
  0.6 28.7 %copy-start = (f32[3712]{0:T(1024)S(1)}, f32[3712]{0:T(1024)}, u32[]{:S(2)}) copy-start(f32[3712]{0:T(1024)} %param.11) | copy-start | bytes 44548
  26.0 11.3 %all-to-all-start.1 = ((f32[8,8,512]{2,1,0:T(8,128)}), f32[8,8,512]{2,1,0:T(8,128)S(1)}, u32[]{:S(2)}, u32[]{:S(2)}) async-start(f32[8,8,512]{2,1,0:T(8,128)} %sum.1), calls=%async_computation.1 | async-start | bytes 262144 | tf_op jit(solution)/shard_map/all_to_all | solution.py:324
  42.6 4.8 %collective-permute-start = (f32[4,40,640]{2,1,0:T(8,128)S(1)}, f32[4,40,640]{2,1,0:T(8,128)S(1)}, u32[]{:S(2)}, u32[]{:S(2)}) collective-permute-start(f32[4,40,640]{2,1,0:T(8,128)S(1)} %get-tuple-element.45), channel_id=1, source_target_pairs={{0,32},{32,0},{64,96},{96,64},{128,160},{160,128},{192,224},{224,1... | collective-permute-start | bytes 1228808 | tf_op jit(solution)/shard_map/ppermute | solution.py:327
  47.5 9.5 %collective-permute-start.1 = (f32[40,640]{1,0:T(8,128)S(1)}, f32[40,640]{1,0:T(8,128)S(1)}, u32[]{:S(2)}, u32[]{:S(2)}) collective-permute-start(f32[40,640]{1,0:T(8,128)S(1)} %get-tuple-element.54), channel_id=1, source_target_pairs={{0,64},{32,96},{64,128},{96,160},{128,192},{160,224},{192,0},{224,... | collective-permute-start | bytes 307208 | tf_op jit(solution)/shard_map/ppermute | solution.py:311
  48.7 8.3 %collective-permute-start.2 = (f32[40,640]{1,0:T(8,128)S(1)}, f32[40,640]{1,0:T(8,128)S(1)}, u32[]{:S(2)}, u32[]{:S(2)}) collective-permute-start(f32[40,640]{1,0:T(8,128)S(1)} %get-tuple-element.55), channel_id=1, source_target_pairs={{0,128},{32,160},{64,192},{96,224},{128,0},{160,32},{192,64},{224,... | collective-permute-start | bytes 307208 | tf_op jit(solution)/shard_map/ppermute | solution.py:311
  51.2 5.8 %collective-permute-start.3 = (f32[40,640]{1,0:T(8,128)S(1)}, f32[40,640]{1,0:T(8,128)S(1)}, u32[]{:S(2)}, u32[]{:S(2)}) collective-permute-start(f32[40,640]{1,0:T(8,128)S(1)} %get-tuple-element.56), channel_id=1, source_target_pairs={{0,192},{32,224},{64,0},{96,32},{128,64},{160,96},{192,128},{224,1... | collective-permute-start | bytes 307208 | tf_op jit(solution)/shard_map/ppermute | solution.py:311
  57.1 8.0 %collective-permute-start.4 = (f32[256,256]{1,0:T(8,128)S(1)}, f32[256,256]{1,0:T(8,128)S(1)}, u32[]{:S(2)}, u32[]{:S(2)}) collective-permute-start(f32[256,256]{1,0:T(8,128)S(1)} %get-tuple-element.61), channel_id=1, source_target_pairs={{0,1},{1,2},{2,3},{3,0},{4,5},{5,6},{6,7},{7,4},{8,9},{9,10},{10,1... | collective-permute-start | bytes 786440 | tf_op jit(solution)/shard_map/ppermute | solution.py:315
  58.5 6.6 %collective-permute-start.5 = (f32[256,256]{1,0:T(8,128)S(1)}, f32[256,256]{1,0:T(8,128)S(1)}, u32[]{:S(2)}, u32[]{:S(2)}) collective-permute-start(f32[256,256]{1,0:T(8,128)S(1)} %get-tuple-element.62), channel_id=1, source_target_pairs={{0,3},{1,0},{2,1},{3,2},{4,7},{5,4},{6,5},{7,6},{8,11},{9,8},{10,9... | collective-permute-start | bytes 786440 | tf_op jit(solution)/shard_map/ppermute | solution.py:315
  60.0 5.2 %collective-permute-start.8 = (f32[32,128]{1,0:T(8,128)S(1)}, f32[32,128]{1,0:T(8,128)S(1)}, u32[]{:S(2)}, u32[]{:S(2)}) collective-permute-start(f32[32,128]{1,0:T(8,128)S(1)} %get-tuple-element.66.g0), channel_id=1, source_target_pairs={{0,3},{1,0},{2,1},{3,2},{4,7},{5,4},{6,5},{7,6},{8,11},{9,8},{10,9... | collective-permute-start | bytes 49160 | tf_op jit(solution)/shard_map/ppermute | solution.py:315
  61.4 4.9 %collective-permute-start.7 = (f32[32,128]{1,0:T(8,128)S(1)}, f32[32,128]{1,0:T(8,128)S(1)}, u32[]{:S(2)}, u32[]{:S(2)}) collective-permute-start(f32[32,128]{1,0:T(8,128)S(1)} %get-tuple-element.66.g0), channel_id=1, source_target_pairs={{0,2},{1,3},{2,0},{3,1},{4,6},{5,7},{6,4},{7,5},{8,10},{9,11},{10,... | collective-permute-start | bytes 49160 | tf_op jit(solution)/shard_map/ppermute | solution.py:315
  61.7 4.5 %collective-permute-start.6 = (f32[32,128]{1,0:T(8,128)S(1)}, f32[32,128]{1,0:T(8,128)S(1)}, u32[]{:S(2)}, u32[]{:S(2)}) collective-permute-start(f32[32,128]{1,0:T(8,128)S(1)} %get-tuple-element.66.g0), channel_id=1, source_target_pairs={{0,1},{1,2},{2,3},{3,0},{4,5},{5,6},{6,7},{7,4},{8,9},{9,10},{10,1... | collective-permute-start | bytes 49160 | tf_op jit(solution)/shard_map/ppermute | solution.py:315
  66.3 14.9 %collective-permute-start.9 = (f32[256,256]{1,0:T(8,128)S(1)}, f32[256,256]{1,0:T(8,128)S(1)}, u32[]{:S(2)}, u32[]{:S(2)}) collective-permute-start(f32[256,256]{1,0:T(8,128)S(1)} %get-tuple-element.68), channel_id=1, source_target_pairs={{0,2},{1,3},{2,0},{3,1},{4,6},{5,7},{6,4},{7,5},{8,10},{9,11},{10,... | collective-permute-start | bytes 786440 | tf_op jit(solution)/shard_map/ppermute | solution.py:315
  67.8 6.0 %collective-permute-start.12 = (f32[40,640]{1,0:T(8,128)S(1)}, f32[40,640]{1,0:T(8,128)S(1)}, u32[]{:S(2)}, u32[]{:S(2)}) collective-permute-start(f32[40,640]{1,0:T(8,128)S(1)} %finish.1.p0), channel_id=1, source_target_pairs={{0,192},{32,224},{64,0},{96,32},{128,64},{160,96},{192,128},{224,1... | collective-permute-start | bytes 307208 | tf_op jit(solution)/shard_map/ppermute | solution.py:311
  68.3 7.1 %collective-permute-start.11 = (f32[40,640]{1,0:T(8,128)S(1)}, f32[40,640]{1,0:T(8,128)S(1)}, u32[]{:S(2)}, u32[]{:S(2)}) collective-permute-start(f32[40,640]{1,0:T(8,128)S(1)} %finish.1.p0), channel_id=1, source_target_pairs={{0,128},{32,160},{64,192},{96,224},{128,0},{160,32},{192,64},{224,... | collective-permute-start | bytes 307208 | tf_op jit(solution)/shard_map/ppermute | solution.py:311
  70.0 8.3 %collective-permute-start.10 = (f32[40,640]{1,0:T(8,128)S(1)}, f32[40,640]{1,0:T(8,128)S(1)}, u32[]{:S(2)}, u32[]{:S(2)}) collective-permute-start(f32[40,640]{1,0:T(8,128)S(1)} %finish.1.p0), channel_id=1, source_target_pairs={{0,64},{32,96},{64,128},{96,160},{128,192},{160,224},{192,0},{224,... | collective-permute-start | bytes 307208 | tf_op jit(solution)/shard_map/ppermute | solution.py:311
  70.0 9.4 %collective-permute-start.13 = (f32[40,640]{1,0:T(8,128)S(1)}, f32[40,640]{1,0:T(8,128)S(1)}, u32[]{:S(2)}, u32[]{:S(2)}) collective-permute-start(f32[40,640]{1,0:T(8,128)S(1)} %finish.1.p0), channel_id=1, source_target_pairs={{0,32},{32,0},{64,96},{96,64},{128,160},{160,128},{192,224},{224,1... | collective-permute-start | bytes 307208 | tf_op jit(solution)/shard_map/ppermute | solution.py:343
  73.9 5.5 %collective-permute-start.16 = (f32[40,640]{1,0:T(8,128)S(1)}, f32[40,640]{1,0:T(8,128)S(1)}, u32[]{:S(2)}, u32[]{:S(2)}) collective-permute-start(f32[40,640]{1,0:T(8,128)S(1)} %collective-permute-done.12.p3), channel_id=1, source_target_pairs={{0,32},{32,0},{64,96},{96,64},{128,160},{160,128},{192,224},{224,1... | collective-permute-start | bytes 307208 | tf_op jit(solution)/shard_map/ppermute | solution.py:343
  75.5 3.9 %collective-permute-start.15 = (f32[40,640]{1,0:T(8,128)S(1)}, f32[40,640]{1,0:T(8,128)S(1)}, u32[]{:S(2)}, u32[]{:S(2)}) collective-permute-start(f32[40,640]{1,0:T(8,128)S(1)} %collective-permute-done.11.p2), channel_id=1, source_target_pairs={{0,32},{32,0},{64,96},{96,64},{128,160},{160,128},{192,224},{224,1... | collective-permute-start | bytes 307208 | tf_op jit(solution)/shard_map/ppermute | solution.py:343
  78.2 2.1 %collective-permute-start.14 = (f32[40,640]{1,0:T(8,128)S(1)}, f32[40,640]{1,0:T(8,128)S(1)}, u32[]{:S(2)}, u32[]{:S(2)}) collective-permute-start(f32[40,640]{1,0:T(8,128)S(1)} %collective-permute-done.10.p1), channel_id=1, source_target_pairs={{0,32},{32,0},{64,96},{96,64},{128,160},{160,128},{192,224},{224,1... | collective-permute-start | bytes 307208 | tf_op jit(solution)/shard_map/ppermute | solution.py:343

commit v5 on v4

--- a/solution.py
+++ b/solution.py
@@ -171,7 +171,7 @@
         send[x] = g_v[2 * x + 1 - core]
 
 
-def third_kernel(zz, mag, s_ref, bt_h, u, w_h, o0, o1, o2, o3, acc, w, bt, sems, small):
+def third_kernel(zz, mag, s_ref, bt_h, u, w_h, o0, o1, o3, o2a, o2b, acc, w, bt, sems, small):
     copies = columns(w_h, w, sems)
     last = pltpu.make_async_copy(bt_h, bt, small.at[0])
     last.start()
@@ -184,9 +184,16 @@
         acc[...] += mm(scaled, w[:, span(c)], NT)
     last.wait()
     acc[...] += mm(s_ref[...].astype(BF16), bt[...] * BF16(SCALE), TN)
-    for d, o in enumerate((o0, o1, o2, o3)):
+    half = TOK // 2
+    for d, rows, o in (
+        (0, slice(0, TOK), o0),
+        (1, slice(0, TOK), o1),
+        (3, slice(0, TOK), o3),
+        (2, slice(0, half), o2a),
+        (2, slice(half, TOK), o2b),
+    ):
         part = lax.rem(lax.axis_index("col") + d, 4)
-        o[...] = acc[:, pl.ds(pl.multiple_of(part * 256, 256), 256)]
+        o[...] = acc[rows, pl.ds(pl.multiple_of(part * 256, 256), 256)]
 
 
 def combine_kernel(y0, y1, y2, y3, zz, mag, pack, gb):
@@ -207,7 +214,12 @@
     gb[...] = total[:RANK, CW:]
 
 
-def finish_kernel(pack, g0, g1, g2, g3, out):
+def finish_kernel(pack, g0, g1, g2, g3, o1, o3, ra, rb, out, s1, s3):
+    half = TOK // 2
+    s1[:half] = o1[:half] + ra[...]
+    s1[half:] = o1[half:]
+    s3[:half] = o3[:half]
+    s3[half:] = o3[half:] + rb[...]
     out[...] = pack[...]
     out[:RANK, CW:] = (g0[...] + g1[...]) + (g2[...] + g3[...])
 
@@ -295,7 +307,7 @@
         third_kernel,
         "tokens_grad",
         [VMEM] * 3 + [HBM, VMEM, HBM],
-        [(TOK, 256)] * 4,
+        [(TOK, 256)] * 3 + [(TOK // 2, 256)] * 2,
         (
             pltpu.VMEM((TOK, ROWS), F32),
             pltpu.VMEM((ROWS, COLS), BF16),
@@ -328,17 +340,18 @@
     halves = call(add_kernel, "add", [VMEM, VMEM], [(PH, PW)] * 4)(keep, other)
     halves, s_part = lax.optimization_barrier((halves, s_part))
     y = [halves[0]] + [along_x(halves[d], d) for d in (1, 2, 3)]
-    o0, o1, o2, o3 = tokens_grad(zz, mag, s_part, bt, u, weight)
+    o0, o1, o3, o2a, o2b = tokens_grad(zz, mag, s_part, bt, u, weight)
 
     pack, gb = call(
         combine_kernel, "combine", [VMEM] * 6, [(PH, PW), (RANK, 128)]
     )(*y, zz, mag)
-    gb, o1, o2, o3 = lax.optimization_barrier((gb, o1, o2, o3))
+    gb, o2a, o2b = lax.optimization_barrier((gb, o2a, o2b))
     gbs = [gb] + [from_col(gb, d) for d in (1, 2, 3)]
-    first, third, gbs[0] = lax.optimization_barrier((from_col(o1, 1), from_col(o3, 3), gbs[0]))
-    pack = call(finish_kernel, "finish", [VMEM] * 5, [(PH, PW)])(pack, *gbs)
-    pack, o2 = lax.optimization_barrier((pack, o2))
-    arrived = [first, from_col(o2, 2), third]
+    ra, rb = from_col(o2a, 1), from_col(o2b, 3)
+    pack, s1, s3 = call(
+        finish_kernel, "finish", [VMEM] * 9, [(PH, PW), (TOK, 256), (TOK, 256)]
+    )(pack, *gbs, o1, o3, ra, rb)
+    arrived = from_col(s1, 1), from_col(s3, 3)
     own = [pack] + [along_x(pack, d) for d in (1, 2, 3)]
     other = [lax.ppermute(p, "dp", CORE_FLIP) for p in own]
     grad_a, gm, gbt = call(
@@ -348,7 +361,7 @@
         [(RANK, COLS), (COLS,), (RANK, ROWS)],
         (pltpu.VMEM((NC, PH, PW), F32),),
     )(*own, *other)
-    grad_tokens = ((o0 + arrived[0]) + (arrived[1] + arrived[2])).astype(BF16)
+    grad_tokens = (o0 + (arrived[0] + arrived[1])).astype(BF16)
     return grad_tokens, gm, grad_a, gbt.T
 
 

time: 82.2 us -> 84.7 us (1.030)
  starting transfers between devices: 30 us -> 31.5 us
  waiting for transfers between devices: 14.1 us -> 15.1 us
    ppermute x6, waiting for transfers between devices: 0.02 us -> 1.6 us  [along_x(): return lax.ppermute(x, 'dp', [(i, (i + 2 * d) % 8) for i in range(8)])]
    ppermute x6 -> x7, starting transfers between devices: 6.87 us -> 7.99 us  [from_col(): return lax.ppermute(x, 'col', [(i, (i + d) % 4) for i in range(4)])]
    ppermute x6 -> x7, waiting for transfers between devices: 3.85 us -> 3.24 us  [from_col(): return lax.ppermute(x, 'col', [(i, (i + d) % 4) for i in range(4)])]
  transfers between devices with their start and end apart: 18 -> 19, of which waited for: 6 -> 7; matrix products, arithmetic and copies ran while one was open for 0% -> 0% of each run, Pallas kernels for 7% -> 7%
where the time goes in v5:
time: 84.7 us; the launch traced here: 84.5 us
  starting transfers between devices  31.5 us (37%)
  Pallas kernels  19.8 us (23%)
  blocking collectives  16.6 us (20%)
  waiting for transfers between devices  15.1 us (18%)
    all_to_all x1, blocking collectives, shards(): parts = lax.all_to_all(part, 'row', 0, 0, tiled=True)  16.6 us
    ppermute x4, starting transfers between devices, shards(): other = [lax.ppermute(p, 'dp', CORE_FLIP) for p in own]  9.63 us
    pallas_call x1, Pallas kernels, norms(): call(first_kernel, 'norms', [HBM, HBM, HBM, HBM, HBM], [((NC, 8, CW), F32...  8.05 us
    ppermute x7, starting transfers between devices, from_col(): return lax.ppermute(x, 'col', [(i, (i + d) % 4) for i in range(4)])  7.99 us
    all_to_all x1, waiting for transfers between devices, shards(): zz = lax.all_to_all(sums, 'row', 0, 0, tiled=True)  7.91 us
    ppermute x6, starting transfers between devices, along_x(): return lax.ppermute(x, 'dp', [(i, (i + 2 * d) % 8) for i in range(8)])  7.1 us
    pallas_call x1, Pallas kernels, factors(): call(second_kernel, 'factors', [VMEM] * 6 + [HBM], [(4, PH, PW), (4, PH,...  5.33 us
    pallas_call x1, Pallas kernels, tokens_grad(): call(third_kernel, 'tokens_grad', [VMEM] * 3 + [HBM, VMEM, HBM], [(TOK, 2...  4.64 us
  transfers between devices with their start and end apart: 19, of which 7 were waited for; matrix products, arithmetic and copies ran while one was open for 0% of the time, Pallas kernels for 7%

profile of v5, /device:TPU:1, one launch (start us, length us, event | category | flops | bytes accessed | tf_op | source)
XLA Modules:
  0.0 84.5 jit_solution(8561061951886605843)
XLA Ops:
  0.6 8.1 %norms.1 = (f32[8,8,512]{2,1,0:T(8,128)S(1)}, bf16[256,1024]{1,0:T(8,128)(2,1)S(1)}, bf16[32,1024]{1,0:T(8,128)(2,1)S(1)}, bf16[32,3712]{1,0:T(8,128)(2,1)S(1)}, bf16[256,3712]{1,0:T(8,128)(2,1)S(1)}) custom-call(bf16[256,1024]{1,0:T(8,128)(2,1)} %tok_h.1, bf16[32,1024]{1,0:T(8,128)(2,1)} %bitcast.3, bf16[32,3712]{1,0:T(8,128)(2,1)} %a_h.1, ...), custom_call_target="tpu_custom_call" | custom-call | flops 3892314112 | bytes 10000000 | tf_op jit(solution)/shard_map/norms/pallas_call | solution.py:266
  8.7 16.6 %all_to_all.10.parts = f32[8,8,512]{2,1,0:T(8,128)S(1)} all-to-all(f32[8,8,512]{2,1,0:T(8,128)S(1)} %get-tuple-element.37), channel_id=1, replica_groups=mesh['dp'=8,'row'=8,'col'=4] {'row'}, dimensions={0} | all-to-all | bytes 262144 | tf_op jit(solution)/shard_map/all_to_all | solution.py:334
  25.3 0.7 sum.1
  26.0 3.4 %all-to-all-start.1 = ((f32[8,8,512]{2,1,0:T(8,128)}), f32[8,8,512]{2,1,0:T(8,128)S(1)}, u32[]{:S(2)}, u32[]{:S(2)}) async-start(f32[8,8,512]{2,1,0:T(8,128)} %sum.1), calls=%async_computation.1 | async-start | bytes 262144 | tf_op jit(solution)/shard_map/all_to_all | solution.py:336
  29.4 7.9 %all-to-all-done.1.zz = f32[8,8,512]{2,1,0:T(8,128)S(1)} async-done(((f32[8,8,512]{2,1,0:T(8,128)}), f32[8,8,512]{2,1,0:T(8,128)S(1)}, u32[]{:S(2)}, u32[]{:S(2)}) %all-to-all-start.1) | async-done | bytes 131104 | tf_op jit(solution)/shard_map/all_to_all | solution.py:336
  37.3 5.3 %factors.1 = (f32[4,40,640]{2,1,0:T(8,128)S(1)}, f32[4,40,640]{2,1,0:T(8,128)S(1)}, f32[32,256]{1,0:T(8,128)S(1)}) custom-call(f32[8,8,512]{2,1,0:T(8,128)S(1)} %all-to-all-done.1.zz, f32[8,512]{1,0:T(8,128)S(1)} %reshape.11.mag, bf16[256,1024]{1,0:T(8,128)(2,1)S(1)} %get-tuple-element.38.tok, bf16[32,1024]{1,0:T(8,128)(2,1)S(1)} %get-tuple-element.39.bt, ...), custom_call_target="tpu_custom_call" | custom-call | flops 3892314112 | bytes 10000000 | tf_op jit(solution)/shard_map/factors/pallas_call | solution.py:290
  42.6 3.4 %collective-permute-start = (f32[4,40,640]{2,1,0:T(8,128)S(1)}, f32[4,40,640]{2,1,0:T(8,128)S(1)}, u32[]{:S(2)}, u32[]{:S(2)}) collective-permute-start(f32[4,40,640]{2,1,0:T(8,128)S(1)} %get-tuple-element.43), channel_id=1, source_target_pairs={{0,32},{32,0},{64,96},{96,64},{128,160},{160,128},{192,224},{224,1... | collective-permute-start | bytes 1228808 | tf_op jit(solution)/shard_map/ppermute | solution.py:339
  46.0 1.4 %collective-permute-done.b = f32[4,40,640]{2,1,0:T(8,128)S(1)} collective-permute-done((f32[4,40,640]{2,1,0:T(8,128)S(1)}, f32[4,40,640]{2,1,0:T(8,128)S(1)}, u32[]{:S(2)}, u32[]{:S(2)}) %collective-permute-start) | collective-permute-done | bytes 409632 | tf_op jit(solution)/shard_map/ppermute | solution.py:339
  47.4 0.1 add.13
  47.5 1.3 %collective-permute-start.1 = (f32[40,640]{1,0:T(8,128)S(1)}, f32[40,640]{1,0:T(8,128)S(1)}, u32[]{:S(2)}, u32[]{:S(2)}) collective-permute-start(f32[40,640]{1,0:T(8,128)S(1)} %get-tuple-element.52), channel_id=1, source_target_pairs={{0,64},{32,96},{64,128},{96,160},{128,192},{160,224},{192,0},{224,... | collective-permute-start | bytes 307208 | tf_op jit(solution)/shard_map/ppermute | solution.py:323
  48.7 2.5 %collective-permute-start.2 = (f32[40,640]{1,0:T(8,128)S(1)}, f32[40,640]{1,0:T(8,128)S(1)}, u32[]{:S(2)}, u32[]{:S(2)}) collective-permute-start(f32[40,640]{1,0:T(8,128)S(1)} %get-tuple-element.53), channel_id=1, source_target_pairs={{0,128},{32,160},{64,192},{96,224},{128,0},{160,32},{192,64},{224,... | collective-permute-start | bytes 307208 | tf_op jit(solution)/shard_map/ppermute | solution.py:323
  51.2 1.2 %collective-permute-start.3 = (f32[40,640]{1,0:T(8,128)S(1)}, f32[40,640]{1,0:T(8,128)S(1)}, u32[]{:S(2)}, u32[]{:S(2)}) collective-permute-start(f32[40,640]{1,0:T(8,128)S(1)} %get-tuple-element.54), channel_id=1, source_target_pairs={{0,192},{32,224},{64,0},{96,32},{128,64},{160,96},{192,128},{224,1... | collective-permute-start | bytes 307208 | tf_op jit(solution)/shard_map/ppermute | solution.py:323
  52.4 4.6 %tokens_grad.1 = (f32[256,256]{1,0:T(8,128)S(1)}, f32[256,256]{1,0:T(8,128)S(1)}, f32[256,256]{1,0:T(8,128)S(1)}, f32[128,256]{1,0:T(8,128)S(1)}, f32[128,256]{1,0:T(8,128)S(1)}) custom-call(f32[8,8,512]{2,1,0:T(8,128)S(1)} %all-to-all-done.1.zz, f32[8,512]{1,0:T(8,128)S(1)} %reshape.11.mag, f32[32,256]{1,0:T(8,128)S(1)} %get-tuple-element.49.s_ref, ...), custom_call_target="tpu_custom_call" | custom-call | flops 3892314112 | bytes 10000000 | tf_op jit(solution)/shard_map/tokens_grad/pallas_call | solution.py:306
  57.0 0.0 collective-permute-done.1.y1
  57.0 0.0 collective-permute-done.2.y2
  57.0 0.0 collective-permute-done.3.y3
  57.0 0.1 combine.1
  57.1 1.4 %collective-permute-start.7 = (f32[128,256]{1,0:T(8,128)S(1)}, f32[128,256]{1,0:T(8,128)S(1)}, u32[]{:S(2)}, u32[]{:S(2)}) collective-permute-start(f32[128,256]{1,0:T(8,128)S(1)} %get-tuple-element.62), channel_id=1, source_target_pairs={{0,1},{1,2},{2,3},{3,0},{4,5},{5,6},{6,7},{7,4},{8,9},{9,10},{10,1... | collective-permute-start | bytes 393224 | tf_op jit(solution)/shard_map/ppermute | solution.py:327
  58.5 1.5 %collective-permute-start.8 = (f32[128,256]{1,0:T(8,128)S(1)}, f32[128,256]{1,0:T(8,128)S(1)}, u32[]{:S(2)}, u32[]{:S(2)}) collective-permute-start(f32[128,256]{1,0:T(8,128)S(1)} %get-tuple-element.63), channel_id=1, source_target_pairs={{0,3},{1,0},{2,1},{3,2},{4,7},{5,4},{6,5},{7,6},{8,11},{9,8},{10,9... | collective-permute-start | bytes 393224 | tf_op jit(solution)/shard_map/ppermute | solution.py:327
  60.0 1.4 %collective-permute-start.6 = (f32[32,128]{1,0:T(8,128)S(1)}, f32[32,128]{1,0:T(8,128)S(1)}, u32[]{:S(2)}, u32[]{:S(2)}) collective-permute-start(f32[32,128]{1,0:T(8,128)S(1)} %get-tuple-element.59.g0), channel_id=1, source_target_pairs={{0,3},{1,0},{2,1},{3,2},{4,7},{5,4},{6,5},{7,6},{8,11},{9,8},{10,9... | collective-permute-start | bytes 49160 | tf_op jit(solution)/shard_map/ppermute | solution.py:327
  61.4 0.4 collective-permute-start.5
  61.7 0.7 collective-permute-start.4
  62.4 0.5 collective-permute-done.6.g3
  62.9 2.6 %collective-permute-done.5.g2 = f32[32,128]{1,0:T(8,128)S(1)} collective-permute-done((f32[32,128]{1,0:T(8,128)S(1)}, f32[32,128]{1,0:T(8,128)S(1)}, u32[]{:S(2)}, u32[]{:S(2)}) %collective-permute-start.5) | collective-permute-done | bytes 16416 | tf_op jit(solution)/shard_map/ppermute | solution.py:327
  65.5 0.2 collective-permute-done.4.g1
  65.6 0.0 collective-permute-done.7.ra
  65.6 0.0 collective-permute-done.8.rb
  65.6 0.1 finish.1
  65.7 3.5 %collective-permute-start.14 = (f32[40,640]{1,0:T(8,128)S(1)}, f32[40,640]{1,0:T(8,128)S(1)}, u32[]{:S(2)}, u32[]{:S(2)}) collective-permute-start(f32[40,640]{1,0:T(8,128)S(1)} %get-tuple-element.66.p0), channel_id=1, source_target_pairs={{0,32},{32,0},{64,96},{96,64},{128,160},{160,128},{192,224},{224,1... | collective-permute-start | bytes 307208 | tf_op jit(solution)/shard_map/ppermute | solution.py:356
  69.2 0.0 collective-permute-start.9
  69.2 2.7 %collective-permute-start.10 = (f32[256,256]{1,0:T(8,128)S(1)}, f32[256,256]{1,0:T(8,128)S(1)}, u32[]{:S(2)}, u32[]{:S(2)}) collective-permute-start(f32[256,256]{1,0:T(8,128)S(1)} %get-tuple-element.65), channel_id=1, source_target_pairs={{0,3},{1,0},{2,1},{3,2},{4,7},{5,4},{6,5},{7,6},{8,11},{9,8},{10,9... | collective-permute-start | bytes 786440 | tf_op jit(solution)/shard_map/ppermute | solution.py:327
  71.9 1.0 %collective-permute-start.13 = (f32[40,640]{1,0:T(8,128)S(1)}, f32[40,640]{1,0:T(8,128)S(1)}, u32[]{:S(2)}, u32[]{:S(2)}) collective-permute-start(f32[40,640]{1,0:T(8,128)S(1)} %get-tuple-element.66.p0), channel_id=1, source_target_pairs={{0,192},{32,224},{64,0},{96,32},{128,64},{160,96},{192,128},{224,1... | collective-permute-start | bytes 307208 | tf_op jit(solution)/shard_map/ppermute | solution.py:323
  72.9 1.1 %collective-permute-start.12 = (f32[40,640]{1,0:T(8,128)S(1)}, f32[40,640]{1,0:T(8,128)S(1)}, u32[]{:S(2)}, u32[]{:S(2)}) collective-permute-start(f32[40,640]{1,0:T(8,128)S(1)} %get-tuple-element.66.p0), channel_id=1, source_target_pairs={{0,128},{32,160},{64,192},{96,224},{128,0},{160,32},{192,64},{224,... | collective-permute-start | bytes 307208 | tf_op jit(solution)/shard_map/ppermute | solution.py:323
  74.0 0.0 collective-permute-done.14.f0
  74.0 0.1 collective-permute-start.11
  74.1 1.6 %collective-permute-done.13.p3 = f32[40,640]{1,0:T(8,128)S(1)} collective-permute-done((f32[40,640]{1,0:T(8,128)S(1)}, f32[40,640]{1,0:T(8,128)S(1)}, u32[]{:S(2)}, u32[]{:S(2)}) %collective-permute-start.13) | collective-permute-done | bytes 102432 | tf_op jit(solution)/shard_map/ppermute | solution.py:323
  75.7 2.6 %collective-permute-start.17 = (f32[40,640]{1,0:T(8,128)S(1)}, f32[40,640]{1,0:T(8,128)S(1)}, u32[]{:S(2)}, u32[]{:S(2)}) collective-permute-start(f32[40,640]{1,0:T(8,128)S(1)} %collective-permute-done.13.p3), channel_id=1, source_target_pairs={{0,32},{32,0},{64,96},{96,64},{128,160},{160,128},{192,224},{224,1... | collective-permute-start | bytes 307208 | tf_op jit(solution)/shard_map/ppermute | solution.py:356
  78.3 0.0 collective-permute-done.12.p2
  78.3 2.5 %collective-permute-start.16 = (f32[40,640]{1,0:T(8,128)S(1)}, f32[40,640]{1,0:T(8,128)S(1)}, u32[]{:S(2)}, u32[]{:S(2)}) collective-permute-start(f32[40,640]{1,0:T(8,128)S(1)} %collective-permute-done.12.p2), channel_id=1, source_target_pairs={{0,32},{32,0},{64,96},{96,64},{128,160},{160,128},{192,224},{224,1... | collective-permute-start | bytes 307208 | tf_op jit(solution)/shard_map/ppermute | solution.py:356
  80.8 0.0 collective-permute-done.11.p1
  80.8 1.1 %collective-permute-start.15 = (f32[40,640]{1,0:T(8,128)S(1)}, f32[40,640]{1,0:T(8,128)S(1)}, u32[]{:S(2)}, u32[]{:S(2)}) collective-permute-start(f32[40,640]{1,0:T(8,128)S(1)} %collective-permute-done.11.p1), channel_id=1, source_target_pairs={{0,32},{32,0},{64,96},{96,64},{128,160},{160,128},{192,224},{224,1... | collective-permute-start | bytes 307208 | tf_op jit(solution)/shard_map/ppermute | solution.py:356
  81.8 0.0 collective-permute-done.17.f3
  81.9 0.0 collective-permute-done.16.f2
  81.9 0.9 %collective-permute-done.15.f1 = f32[40,640]{1,0:T(8,128)S(1)} collective-permute-done((f32[40,640]{1,0:T(8,128)S(1)}, f32[40,640]{1,0:T(8,128)S(1)}, u32[]{:S(2)}, u32[]{:S(2)}) %collective-permute-start.15) | collective-permute-done | bytes 102432 | tf_op jit(solution)/shard_map/ppermute | solution.py:356
  82.8 0.9 %outputs.1 = (f32[32,3712]{1,0:T(8,128)}, f32[3712]{0:T(1024)}, f32[32,1024]{1,0:T(8,128)}) custom-call(f32[40,640]{1,0:T(8,128)S(1)} %get-tuple-element.66.p0, f32[40,640]{1,0:T(8,128)S(1)} %collective-permute-done.11.p1, f32[40,640]{1,0:T(8,128)S(1)} %collective-permute-done.12.p2, f32[40,640]{1,0:T(8,128)S(1)} %collective-permute-done.13.p3, ...), custom_call_target="tpu_custom_call" | custom-call | tf_op jit(solution)/shard_map/outputs/pallas_call | solution.py:357
  83.7 0.0 collective-permute-done.9
  83.7 0.0 collective-permute-done.10
  83.7 0.7 add_convert_fusion
  (4 shorter events, 0.0 us)
Async XLA Ops:
  0.6 28.7 %copy-start = (f32[3712]{0:T(1024)S(1)}, f32[3712]{0:T(1024)}, u32[]{:S(2)}) copy-start(f32[3712]{0:T(1024)} %param.11) | copy-start | bytes 44548
  26.0 11.3 %all-to-all-start.1 = ((f32[8,8,512]{2,1,0:T(8,128)}), f32[8,8,512]{2,1,0:T(8,128)S(1)}, u32[]{:S(2)}, u32[]{:S(2)}) async-start(f32[8,8,512]{2,1,0:T(8,128)} %sum.1), calls=%async_computation.1 | async-start | bytes 262144 | tf_op jit(solution)/shard_map/all_to_all | solution.py:336
  42.6 4.8 %collective-permute-start = (f32[4,40,640]{2,1,0:T(8,128)S(1)}, f32[4,40,640]{2,1,0:T(8,128)S(1)}, u32[]{:S(2)}, u32[]{:S(2)}) collective-permute-start(f32[4,40,640]{2,1,0:T(8,128)S(1)} %get-tuple-element.43), channel_id=1, source_target_pairs={{0,32},{32,0},{64,96},{96,64},{128,160},{160,128},{192,224},{224,1... | collective-permute-start | bytes 1228808 | tf_op jit(solution)/shard_map/ppermute | solution.py:339
  47.5 9.5 %collective-permute-start.1 = (f32[40,640]{1,0:T(8,128)S(1)}, f32[40,640]{1,0:T(8,128)S(1)}, u32[]{:S(2)}, u32[]{:S(2)}) collective-permute-start(f32[40,640]{1,0:T(8,128)S(1)} %get-tuple-element.52), channel_id=1, source_target_pairs={{0,64},{32,96},{64,128},{96,160},{128,192},{160,224},{192,0},{224,... | collective-permute-start | bytes 307208 | tf_op jit(solution)/shard_map/ppermute | solution.py:323
  48.7 8.3 %collective-permute-start.2 = (f32[40,640]{1,0:T(8,128)S(1)}, f32[40,640]{1,0:T(8,128)S(1)}, u32[]{:S(2)}, u32[]{:S(2)}) collective-permute-start(f32[40,640]{1,0:T(8,128)S(1)} %get-tuple-element.53), channel_id=1, source_target_pairs={{0,128},{32,160},{64,192},{96,224},{128,0},{160,32},{192,64},{224,... | collective-permute-start | bytes 307208 | tf_op jit(solution)/shard_map/ppermute | solution.py:323
  51.2 5.8 %collective-permute-start.3 = (f32[40,640]{1,0:T(8,128)S(1)}, f32[40,640]{1,0:T(8,128)S(1)}, u32[]{:S(2)}, u32[]{:S(2)}) collective-permute-start(f32[40,640]{1,0:T(8,128)S(1)} %get-tuple-element.54), channel_id=1, source_target_pairs={{0,192},{32,224},{64,0},{96,32},{128,64},{160,96},{192,128},{224,1... | collective-permute-start | bytes 307208 | tf_op jit(solution)/shard_map/ppermute | solution.py:323
  57.1 8.5 %collective-permute-start.7 = (f32[128,256]{1,0:T(8,128)S(1)}, f32[128,256]{1,0:T(8,128)S(1)}, u32[]{:S(2)}, u32[]{:S(2)}) collective-permute-start(f32[128,256]{1,0:T(8,128)S(1)} %get-tuple-element.62), channel_id=1, source_target_pairs={{0,1},{1,2},{2,3},{3,0},{4,5},{5,6},{6,7},{7,4},{8,9},{9,10},{10,1... | collective-permute-start | bytes 393224 | tf_op jit(solution)/shard_map/ppermute | solution.py:327
  58.5 7.2 %collective-permute-start.8 = (f32[128,256]{1,0:T(8,128)S(1)}, f32[128,256]{1,0:T(8,128)S(1)}, u32[]{:S(2)}, u32[]{:S(2)}) collective-permute-start(f32[128,256]{1,0:T(8,128)S(1)} %get-tuple-element.63), channel_id=1, source_target_pairs={{0,3},{1,0},{2,1},{3,2},{4,7},{5,4},{6,5},{7,6},{8,11},{9,8},{10,9... | collective-permute-start | bytes 393224 | tf_op jit(solution)/shard_map/ppermute | solution.py:327
  60.0 2.9 %collective-permute-start.6 = (f32[32,128]{1,0:T(8,128)S(1)}, f32[32,128]{1,0:T(8,128)S(1)}, u32[]{:S(2)}, u32[]{:S(2)}) collective-permute-start(f32[32,128]{1,0:T(8,128)S(1)} %get-tuple-element.59.g0), channel_id=1, source_target_pairs={{0,3},{1,0},{2,1},{3,2},{4,7},{5,4},{6,5},{7,6},{8,11},{9,8},{10,9... | collective-permute-start | bytes 49160 | tf_op jit(solution)/shard_map/ppermute | solution.py:327
  61.4 4.1 %collective-permute-start.5 = (f32[32,128]{1,0:T(8,128)S(1)}, f32[32,128]{1,0:T(8,128)S(1)}, u32[]{:S(2)}, u32[]{:S(2)}) collective-permute-start(f32[32,128]{1,0:T(8,128)S(1)} %get-tuple-element.59.g0), channel_id=1, source_target_pairs={{0,2},{1,3},{2,0},{3,1},{4,6},{5,7},{6,4},{7,5},{8,10},{9,11},{10,... | collective-permute-start | bytes 49160 | tf_op jit(solution)/shard_map/ppermute | solution.py:327
  61.7 3.9 %collective-permute-start.4 = (f32[32,128]{1,0:T(8,128)S(1)}, f32[32,128]{1,0:T(8,128)S(1)}, u32[]{:S(2)}, u32[]{:S(2)}) collective-permute-start(f32[32,128]{1,0:T(8,128)S(1)} %get-tuple-element.59.g0), channel_id=1, source_target_pairs={{0,1},{1,2},{2,3},{3,0},{4,5},{5,6},{6,7},{7,4},{8,9},{9,10},{10,1... | collective-permute-start | bytes 49160 | tf_op jit(solution)/shard_map/ppermute | solution.py:327
  65.7 8.3 %collective-permute-start.14 = (f32[40,640]{1,0:T(8,128)S(1)}, f32[40,640]{1,0:T(8,128)S(1)}, u32[]{:S(2)}, u32[]{:S(2)}) collective-permute-start(f32[40,640]{1,0:T(8,128)S(1)} %get-tuple-element.66.p0), channel_id=1, source_target_pairs={{0,32},{32,0},{64,96},{96,64},{128,160},{160,128},{192,224},{224,1... | collective-permute-start | bytes 307208 | tf_op jit(solution)/shard_map/ppermute | solution.py:356
  69.2 14.5 %collective-permute-start.9 = (f32[256,256]{1,0:T(8,128)S(1)}, f32[256,256]{1,0:T(8,128)S(1)}, u32[]{:S(2)}, u32[]{:S(2)}) collective-permute-start(f32[256,256]{1,0:T(8,128)S(1)} %get-tuple-element.64), channel_id=1, source_target_pairs={{0,1},{1,2},{2,3},{3,0},{4,5},{5,6},{6,7},{7,4},{8,9},{9,10},{10,1... | collective-permute-start | bytes 786440 | tf_op jit(solution)/shard_map/ppermute | solution.py:327
  69.2 14.5 %collective-permute-start.10 = (f32[256,256]{1,0:T(8,128)S(1)}, f32[256,256]{1,0:T(8,128)S(1)}, u32[]{:S(2)}, u32[]{:S(2)}) collective-permute-start(f32[256,256]{1,0:T(8,128)S(1)} %get-tuple-element.65), channel_id=1, source_target_pairs={{0,3},{1,0},{2,1},{3,2},{4,7},{5,4},{6,5},{7,6},{8,11},{9,8},{10,9... | collective-permute-start | bytes 786440 | tf_op jit(solution)/shard_map/ppermute | solution.py:327
  71.9 3.8 %collective-permute-start.13 = (f32[40,640]{1,0:T(8,128)S(1)}, f32[40,640]{1,0:T(8,128)S(1)}, u32[]{:S(2)}, u32[]{:S(2)}) collective-permute-start(f32[40,640]{1,0:T(8,128)S(1)} %get-tuple-element.66.p0), channel_id=1, source_target_pairs={{0,192},{32,224},{64,0},{96,32},{128,64},{160,96},{192,128},{224,1... | collective-permute-start | bytes 307208 | tf_op jit(solution)/shard_map/ppermute | solution.py:323
  72.9 5.4 %collective-permute-start.12 = (f32[40,640]{1,0:T(8,128)S(1)}, f32[40,640]{1,0:T(8,128)S(1)}, u32[]{:S(2)}, u32[]{:S(2)}) collective-permute-start(f32[40,640]{1,0:T(8,128)S(1)} %get-tuple-element.66.p0), channel_id=1, source_target_pairs={{0,128},{32,160},{64,192},{96,224},{128,0},{160,32},{192,64},{224,... | collective-permute-start | bytes 307208 | tf_op jit(solution)/shard_map/ppermute | solution.py:323
  74.0 6.8 %collective-permute-start.11 = (f32[40,640]{1,0:T(8,128)S(1)}, f32[40,640]{1,0:T(8,128)S(1)}, u32[]{:S(2)}, u32[]{:S(2)}) collective-permute-start(f32[40,640]{1,0:T(8,128)S(1)} %get-tuple-element.66.p0), channel_id=1, source_target_pairs={{0,64},{32,96},{64,128},{96,160},{128,192},{160,224},{192,0},{224,... | collective-permute-start | bytes 307208 | tf_op jit(solution)/shard_map/ppermute | solution.py:323
  75.7 6.2 %collective-permute-start.17 = (f32[40,640]{1,0:T(8,128)S(1)}, f32[40,640]{1,0:T(8,128)S(1)}, u32[]{:S(2)}, u32[]{:S(2)}) collective-permute-start(f32[40,640]{1,0:T(8,128)S(1)} %collective-permute-done.13.p3), channel_id=1, source_target_pairs={{0,32},{32,0},{64,96},{96,64},{128,160},{160,128},{192,224},{224,1... | collective-permute-start | bytes 307208 | tf_op jit(solution)/shard_map/ppermute | solution.py:356
  78.3 3.6 %collective-permute-start.16 = (f32[40,640]{1,0:T(8,128)S(1)}, f32[40,640]{1,0:T(8,128)S(1)}, u32[]{:S(2)}, u32[]{:S(2)}) collective-permute-start(f32[40,640]{1,0:T(8,128)S(1)} %collective-permute-done.12.p2), channel_id=1, source_target_pairs={{0,32},{32,0},{64,96},{96,64},{128,160},{160,128},{192,224},{224,1... | collective-permute-start | bytes 307208 | tf_op jit(solution)/shard_map/ppermute | solution.py:356
  80.8 2.0 %collective-permute-start.15 = (f32[40,640]{1,0:T(8,128)S(1)}, f32[40,640]{1,0:T(8,128)S(1)}, u32[]{:S(2)}, u32[]{:S(2)}) collective-permute-start(f32[40,640]{1,0:T(8,128)S(1)} %collective-permute-done.11.p1), channel_id=1, source_target_pairs={{0,32},{32,0},{64,96},{96,64},{128,160},{160,128},{192,224},{224,1... | collective-permute-start | bytes 307208 | tf_op jit(solution)/shard_map/ppermute | solution.py:356

commit v6 on v5

--- a/solution.py
+++ b/solution.py
@@ -351,8 +351,9 @@
     pack, s1, s3 = call(
         finish_kernel, "finish", [VMEM] * 9, [(PH, PW), (TOK, 256), (TOK, 256)]
     )(pack, *gbs, o1, o3, ra, rb)
+    own = [pack] + [along_x(pack, d) for d in (1, 2, 3)]
+    own, s1, s3 = lax.optimization_barrier((own, s1, s3))
     arrived = from_col(s1, 1), from_col(s3, 3)
-    own = [pack] + [along_x(pack, d) for d in (1, 2, 3)]
     other = [lax.ppermute(p, "dp", CORE_FLIP) for p in own]
     grad_a, gm, gbt = call(
         last_kernel,

time: 84.7 us -> 85.1 us (level)
  waiting for transfers between devices: 15.1 us -> 18.7 us
  starting transfers between devices: 31.5 us -> 28.3 us
    ppermute x4, starting transfers between devices: 9.63 us -> 6.45 us  [shards(): other = [lax.ppermute(p, 'dp', CORE_FLIP) for p in own]]
    ppermute x6, waiting for transfers between devices: 1.6 us -> 4.77 us  [along_x(): return lax.ppermute(x, 'dp', [(i, (i + 2 * d) % 8) for i in range(8)])]
  transfers between devices with their start and end apart: 19 -> 19, of which waited for: 7 -> 11; matrix products, arithmetic and copies ran while one was open for 0% -> 0% of each run, Pallas kernels for 7% -> 7%
where the time goes in v6:
time: 85.1 us; the launch traced here: 84.9 us
  starting transfers between devices  28.3 us (33%)
  Pallas kernels  19.8 us (23%)
  waiting for transfers between devices  18.7 us (22%)
  blocking collectives  16.6 us (20%)
    all_to_all x1, blocking collectives, shards(): parts = lax.all_to_all(part, 'row', 0, 0, tiled=True)  16.6 us
    pallas_call x1, Pallas kernels, norms(): call(first_kernel, 'norms', [HBM, HBM, HBM, HBM, HBM], [((NC, 8, CW), F32...  8.05 us
    ppermute x7, starting transfers between devices, from_col(): return lax.ppermute(x, 'col', [(i, (i + d) % 4) for i in range(4)])  7.97 us
    all_to_all x1, waiting for transfers between devices, shards(): zz = lax.all_to_all(sums, 'row', 0, 0, tiled=True)  7.91 us
    ppermute x6, starting transfers between devices, along_x(): return lax.ppermute(x, 'dp', [(i, (i + 2 * d) % 8) for i in range(8)])  7.09 us
    ppermute x4, starting transfers between devices, shards(): other = [lax.ppermute(p, 'dp', CORE_FLIP) for p in own]  6.45 us
    pallas_call x1, Pallas kernels, factors(): call(second_kernel, 'factors', [VMEM] * 6 + [HBM], [(4, PH, PW), (4, PH,...  5.33 us
    ppermute x6, waiting for transfers between devices, along_x(): return lax.ppermute(x, 'dp', [(i, (i + 2 * d) % 8) for i in range(8)])  4.77 us
  transfers between devices with their start and end apart: 19, of which 11 were waited for; matrix products, arithmetic and copies ran while one was open for 0% of the time, Pallas kernels for 7%

profile of v6, /device:TPU:1, one launch (start us, length us, event | category | flops | bytes accessed | tf_op | source)
XLA Modules:
  0.0 84.9 jit_solution(2380059493177018269)
XLA Ops:
  0.6 8.1 %norms.1 = (f32[8,8,512]{2,1,0:T(8,128)S(1)}, bf16[256,1024]{1,0:T(8,128)(2,1)S(1)}, bf16[32,1024]{1,0:T(8,128)(2,1)S(1)}, bf16[32,3712]{1,0:T(8,128)(2,1)S(1)}, bf16[256,3712]{1,0:T(8,128)(2,1)S(1)}) custom-call(bf16[256,1024]{1,0:T(8,128)(2,1)} %tok_h.1, bf16[32,1024]{1,0:T(8,128)(2,1)} %bitcast.3, bf16[32,3712]{1,0:T(8,128)(2,1)} %a_h.1, ...), custom_call_target="tpu_custom_call" | custom-call | flops 3892314112 | bytes 10000000 | tf_op jit(solution)/shard_map/norms/pallas_call | solution.py:266
  8.7 16.6 %all_to_all.10.parts = f32[8,8,512]{2,1,0:T(8,128)S(1)} all-to-all(f32[8,8,512]{2,1,0:T(8,128)S(1)} %get-tuple-element.43), channel_id=1, replica_groups=mesh['dp'=8,'row'=8,'col'=4] {'row'}, dimensions={0} | all-to-all | bytes 262144 | tf_op jit(solution)/shard_map/all_to_all | solution.py:334
  25.3 0.7 sum.1
  26.0 3.4 %all-to-all-start.1 = ((f32[8,8,512]{2,1,0:T(8,128)}), f32[8,8,512]{2,1,0:T(8,128)S(1)}, u32[]{:S(2)}, u32[]{:S(2)}) async-start(f32[8,8,512]{2,1,0:T(8,128)} %sum.1), calls=%async_computation.1 | async-start | bytes 262144 | tf_op jit(solution)/shard_map/all_to_all | solution.py:336
  29.4 7.9 %all-to-all-done.1.zz = f32[8,8,512]{2,1,0:T(8,128)S(1)} async-done(((f32[8,8,512]{2,1,0:T(8,128)}), f32[8,8,512]{2,1,0:T(8,128)S(1)}, u32[]{:S(2)}, u32[]{:S(2)}) %all-to-all-start.1) | async-done | bytes 131104 | tf_op jit(solution)/shard_map/all_to_all | solution.py:336
  37.3 5.3 %factors.1 = (f32[4,40,640]{2,1,0:T(8,128)S(1)}, f32[4,40,640]{2,1,0:T(8,128)S(1)}, f32[32,256]{1,0:T(8,128)S(1)}) custom-call(f32[8,8,512]{2,1,0:T(8,128)S(1)} %all-to-all-done.1.zz, f32[8,512]{1,0:T(8,128)S(1)} %reshape.11.mag, bf16[256,1024]{1,0:T(8,128)(2,1)S(1)} %get-tuple-element.44.tok, bf16[32,1024]{1,0:T(8,128)(2,1)S(1)} %get-tuple-element.45.bt, ...), custom_call_target="tpu_custom_call" | custom-call | flops 3892314112 | bytes 10000000 | tf_op jit(solution)/shard_map/factors/pallas_call | solution.py:290
  42.6 3.4 %collective-permute-start = (f32[4,40,640]{2,1,0:T(8,128)S(1)}, f32[4,40,640]{2,1,0:T(8,128)S(1)}, u32[]{:S(2)}, u32[]{:S(2)}) collective-permute-start(f32[4,40,640]{2,1,0:T(8,128)S(1)} %get-tuple-element.49), channel_id=1, source_target_pairs={{0,32},{32,0},{64,96},{96,64},{128,160},{160,128},{192,224},{224,1... | collective-permute-start | bytes 1228808 | tf_op jit(solution)/shard_map/ppermute | solution.py:339
  46.0 1.4 %collective-permute-done.b = f32[4,40,640]{2,1,0:T(8,128)S(1)} collective-permute-done((f32[4,40,640]{2,1,0:T(8,128)S(1)}, f32[4,40,640]{2,1,0:T(8,128)S(1)}, u32[]{:S(2)}, u32[]{:S(2)}) %collective-permute-start) | collective-permute-done | bytes 409632 | tf_op jit(solution)/shard_map/ppermute | solution.py:339
  47.4 0.1 add.13
  47.5 1.3 %collective-permute-start.1 = (f32[40,640]{1,0:T(8,128)S(1)}, f32[40,640]{1,0:T(8,128)S(1)}, u32[]{:S(2)}, u32[]{:S(2)}) collective-permute-start(f32[40,640]{1,0:T(8,128)S(1)} %get-tuple-element.58), channel_id=1, source_target_pairs={{0,64},{32,96},{64,128},{96,160},{128,192},{160,224},{192,0},{224,... | collective-permute-start | bytes 307208 | tf_op jit(solution)/shard_map/ppermute | solution.py:323
  48.7 2.5 %collective-permute-start.2 = (f32[40,640]{1,0:T(8,128)S(1)}, f32[40,640]{1,0:T(8,128)S(1)}, u32[]{:S(2)}, u32[]{:S(2)}) collective-permute-start(f32[40,640]{1,0:T(8,128)S(1)} %get-tuple-element.59), channel_id=1, source_target_pairs={{0,128},{32,160},{64,192},{96,224},{128,0},{160,32},{192,64},{224,... | collective-permute-start | bytes 307208 | tf_op jit(solution)/shard_map/ppermute | solution.py:323
  51.2 1.2 %collective-permute-start.3 = (f32[40,640]{1,0:T(8,128)S(1)}, f32[40,640]{1,0:T(8,128)S(1)}, u32[]{:S(2)}, u32[]{:S(2)}) collective-permute-start(f32[40,640]{1,0:T(8,128)S(1)} %get-tuple-element.60), channel_id=1, source_target_pairs={{0,192},{32,224},{64,0},{96,32},{128,64},{160,96},{192,128},{224,1... | collective-permute-start | bytes 307208 | tf_op jit(solution)/shard_map/ppermute | solution.py:323
  52.4 4.6 %tokens_grad.1 = (f32[256,256]{1,0:T(8,128)S(1)}, f32[256,256]{1,0:T(8,128)S(1)}, f32[256,256]{1,0:T(8,128)S(1)}, f32[128,256]{1,0:T(8,128)S(1)}, f32[128,256]{1,0:T(8,128)S(1)}) custom-call(f32[8,8,512]{2,1,0:T(8,128)S(1)} %all-to-all-done.1.zz, f32[8,512]{1,0:T(8,128)S(1)} %reshape.11.mag, f32[32,256]{1,0:T(8,128)S(1)} %get-tuple-element.55.s_ref, ...), custom_call_target="tpu_custom_call" | custom-call | flops 3892314112 | bytes 10000000 | tf_op jit(solution)/shard_map/tokens_grad/pallas_call | solution.py:306
  57.0 0.0 collective-permute-done.1.y1
  57.0 0.0 collective-permute-done.2.y2
  57.0 0.0 collective-permute-done.3.y3
  57.0 0.1 combine.1
  57.1 1.4 %collective-permute-start.7 = (f32[128,256]{1,0:T(8,128)S(1)}, f32[128,256]{1,0:T(8,128)S(1)}, u32[]{:S(2)}, u32[]{:S(2)}) collective-permute-start(f32[128,256]{1,0:T(8,128)S(1)} %get-tuple-element.68), channel_id=1, source_target_pairs={{0,1},{1,2},{2,3},{3,0},{4,5},{5,6},{6,7},{7,4},{8,9},{9,10},{10,1... | collective-permute-start | bytes 393224 | tf_op jit(solution)/shard_map/ppermute | solution.py:327
  58.5 1.5 %collective-permute-start.8 = (f32[128,256]{1,0:T(8,128)S(1)}, f32[128,256]{1,0:T(8,128)S(1)}, u32[]{:S(2)}, u32[]{:S(2)}) collective-permute-start(f32[128,256]{1,0:T(8,128)S(1)} %get-tuple-element.69), channel_id=1, source_target_pairs={{0,3},{1,0},{2,1},{3,2},{4,7},{5,4},{6,5},{7,6},{8,11},{9,8},{10,9... | collective-permute-start | bytes 393224 | tf_op jit(solution)/shard_map/ppermute | solution.py:327
  60.0 1.4 %collective-permute-start.6 = (f32[32,128]{1,0:T(8,128)S(1)}, f32[32,128]{1,0:T(8,128)S(1)}, u32[]{:S(2)}, u32[]{:S(2)}) collective-permute-start(f32[32,128]{1,0:T(8,128)S(1)} %get-tuple-element.65.g0), channel_id=1, source_target_pairs={{0,3},{1,0},{2,1},{3,2},{4,7},{5,4},{6,5},{7,6},{8,11},{9,8},{10,9... | collective-permute-start | bytes 49160 | tf_op jit(solution)/shard_map/ppermute | solution.py:327
  61.4 0.4 collective-permute-start.5
  61.7 0.7 collective-permute-start.4
  62.4 0.5 collective-permute-done.6.g3
  62.9 2.6 %collective-permute-done.5.g2 = f32[32,128]{1,0:T(8,128)S(1)} collective-permute-done((f32[32,128]{1,0:T(8,128)S(1)}, f32[32,128]{1,0:T(8,128)S(1)}, u32[]{:S(2)}, u32[]{:S(2)}) %collective-permute-start.5) | collective-permute-done | bytes 16416 | tf_op jit(solution)/shard_map/ppermute | solution.py:327
  65.5 0.2 collective-permute-done.4.g1
  65.6 0.0 collective-permute-done.7.ra
  65.6 0.0 collective-permute-done.8.rb
  65.6 0.1 finish.1
  65.7 0.9 %collective-permute-start.11 = (f32[40,640]{1,0:T(8,128)S(1)}, f32[40,640]{1,0:T(8,128)S(1)}, u32[]{:S(2)}, u32[]{:S(2)}) collective-permute-start(f32[40,640]{1,0:T(8,128)S(1)} %get-tuple-element.75.p0), channel_id=1, source_target_pairs={{0,192},{32,224},{64,0},{96,32},{128,64},{160,96},{192,128},{224,1... | collective-permute-start | bytes 307208 | tf_op jit(solution)/shard_map/ppermute | solution.py:323
  66.6 1.3 %collective-permute-start.10 = (f32[40,640]{1,0:T(8,128)S(1)}, f32[40,640]{1,0:T(8,128)S(1)}, u32[]{:S(2)}, u32[]{:S(2)}) collective-permute-start(f32[40,640]{1,0:T(8,128)S(1)} %get-tuple-element.75.p0), channel_id=1, source_target_pairs={{0,128},{32,160},{64,192},{96,224},{128,0},{160,32},{192,64},{224,... | collective-permute-start | bytes 307208 | tf_op jit(solution)/shard_map/ppermute | solution.py:323
  67.9 0.0 collective-permute-start.9
  67.9 1.4 %collective-permute-done.11.p3 = f32[40,640]{1,0:T(8,128)S(1)} collective-permute-done((f32[40,640]{1,0:T(8,128)S(1)}, f32[40,640]{1,0:T(8,128)S(1)}, u32[]{:S(2)}, u32[]{:S(2)}) %collective-permute-start.11) | collective-permute-done | bytes 102432 | tf_op jit(solution)/shard_map/ppermute | solution.py:323
  69.3 2.3 %collective-permute-done.10.p2 = f32[40,640]{1,0:T(8,128)S(1)} collective-permute-done((f32[40,640]{1,0:T(8,128)S(1)}, f32[40,640]{1,0:T(8,128)S(1)}, u32[]{:S(2)}, u32[]{:S(2)}) %collective-permute-start.10) | collective-permute-done | bytes 102432 | tf_op jit(solution)/shard_map/ppermute | solution.py:323
  71.6 1.1 %collective-permute-done.9.p1 = f32[40,640]{1,0:T(8,128)S(1)} collective-permute-done((f32[40,640]{1,0:T(8,128)S(1)}, f32[40,640]{1,0:T(8,128)S(1)}, u32[]{:S(2)}, u32[]{:S(2)}) %collective-permute-start.9) | collective-permute-done | bytes 102432 | tf_op jit(solution)/shard_map/ppermute | solution.py:323
  72.7 0.0 collective-permute-start.12
  72.7 2.6 %collective-permute-start.13 = (f32[256,256]{1,0:T(8,128)S(1)}, f32[256,256]{1,0:T(8,128)S(1)}, u32[]{:S(2)}, u32[]{:S(2)}) collective-permute-start(f32[256,256]{1,0:T(8,128)S(1)} %get-tuple-element.74), channel_id=1, source_target_pairs={{0,3},{1,0},{2,1},{3,2},{4,7},{5,4},{6,5},{7,6},{8,11},{9,8},{10,9... | collective-permute-start | bytes 786440 | tf_op jit(solution)/shard_map/ppermute | solution.py:327
  75.4 5.6 %collective-permute-start.14 = (f32[40,640]{1,0:T(8,128)S(1)}, f32[40,640]{1,0:T(8,128)S(1)}, u32[]{:S(2)}, u32[]{:S(2)}) collective-permute-start(f32[40,640]{1,0:T(8,128)S(1)} %get-tuple-element.75.p0), channel_id=1, source_target_pairs={{0,32},{32,0},{64,96},{96,64},{128,160},{160,128},{192,224},{224,1... | collective-permute-start | bytes 307208 | tf_op jit(solution)/shard_map/ppermute | solution.py:357
  80.9 0.0 collective-permute-start.15
  80.9 0.5 collective-permute-start.16
  81.5 0.4 collective-permute-done.14.f0
  81.9 0.4 collective-permute-start.17
  82.2 0.0 collective-permute-done.15.f1
  82.3 0.1 collective-permute-done.16.f2
  82.4 0.8 collective-permute-done.17.f3
  83.2 0.9 %outputs.1 = (f32[32,3712]{1,0:T(8,128)}, f32[3712]{0:T(1024)}, f32[32,1024]{1,0:T(8,128)}) custom-call(f32[40,640]{1,0:T(8,128)S(1)} %get-tuple-element.75.p0, f32[40,640]{1,0:T(8,128)S(1)} %collective-permute-done.9.p1, f32[40,640]{1,0:T(8,128)S(1)} %collective-permute-done.10.p2, f32[40,640]{1,0:T(8,128)S(1)} %collective-permute-done.11.p3, ...), custom_call_target="tpu_custom_call" | custom-call | tf_op jit(solution)/shard_map/outputs/pallas_call | solution.py:358
  84.1 0.0 collective-permute-done.12
  84.1 0.0 collective-permute-done.13
  84.1 0.7 add_convert_fusion
  (4 shorter events, 0.0 us)
Async XLA Ops:
  0.6 28.7 %copy-start = (f32[3712]{0:T(1024)S(1)}, f32[3712]{0:T(1024)}, u32[]{:S(2)}) copy-start(f32[3712]{0:T(1024)} %param.11) | copy-start | bytes 44548
  26.0 11.3 %all-to-all-start.1 = ((f32[8,8,512]{2,1,0:T(8,128)}), f32[8,8,512]{2,1,0:T(8,128)S(1)}, u32[]{:S(2)}, u32[]{:S(2)}) async-start(f32[8,8,512]{2,1,0:T(8,128)} %sum.1), calls=%async_computation.1 | async-start | bytes 262144 | tf_op jit(solution)/shard_map/all_to_all | solution.py:336
  42.6 4.8 %collective-permute-start = (f32[4,40,640]{2,1,0:T(8,128)S(1)}, f32[4,40,640]{2,1,0:T(8,128)S(1)}, u32[]{:S(2)}, u32[]{:S(2)}) collective-permute-start(f32[4,40,640]{2,1,0:T(8,128)S(1)} %get-tuple-element.49), channel_id=1, source_target_pairs={{0,32},{32,0},{64,96},{96,64},{128,160},{160,128},{192,224},{224,1... | collective-permute-start | bytes 1228808 | tf_op jit(solution)/shard_map/ppermute | solution.py:339
  47.5 9.5 %collective-permute-start.1 = (f32[40,640]{1,0:T(8,128)S(1)}, f32[40,640]{1,0:T(8,128)S(1)}, u32[]{:S(2)}, u32[]{:S(2)}) collective-permute-start(f32[40,640]{1,0:T(8,128)S(1)} %get-tuple-element.58), channel_id=1, source_target_pairs={{0,64},{32,96},{64,128},{96,160},{128,192},{160,224},{192,0},{224,... | collective-permute-start | bytes 307208 | tf_op jit(solution)/shard_map/ppermute | solution.py:323
  48.7 8.3 %collective-permute-start.2 = (f32[40,640]{1,0:T(8,128)S(1)}, f32[40,640]{1,0:T(8,128)S(1)}, u32[]{:S(2)}, u32[]{:S(2)}) collective-permute-start(f32[40,640]{1,0:T(8,128)S(1)} %get-tuple-element.59), channel_id=1, source_target_pairs={{0,128},{32,160},{64,192},{96,224},{128,0},{160,32},{192,64},{224,... | collective-permute-start | bytes 307208 | tf_op jit(solution)/shard_map/ppermute | solution.py:323
  51.2 5.8 %collective-permute-start.3 = (f32[40,640]{1,0:T(8,128)S(1)}, f32[40,640]{1,0:T(8,128)S(1)}, u32[]{:S(2)}, u32[]{:S(2)}) collective-permute-start(f32[40,640]{1,0:T(8,128)S(1)} %get-tuple-element.60), channel_id=1, source_target_pairs={{0,192},{32,224},{64,0},{96,32},{128,64},{160,96},{192,128},{224,1... | collective-permute-start | bytes 307208 | tf_op jit(solution)/shard_map/ppermute | solution.py:323
  57.1 8.5 %collective-permute-start.7 = (f32[128,256]{1,0:T(8,128)S(1)}, f32[128,256]{1,0:T(8,128)S(1)}, u32[]{:S(2)}, u32[]{:S(2)}) collective-permute-start(f32[128,256]{1,0:T(8,128)S(1)} %get-tuple-element.68), channel_id=1, source_target_pairs={{0,1},{1,2},{2,3},{3,0},{4,5},{5,6},{6,7},{7,4},{8,9},{9,10},{10,1... | collective-permute-start | bytes 393224 | tf_op jit(solution)/shard_map/ppermute | solution.py:327
  58.5 7.2 %collective-permute-start.8 = (f32[128,256]{1,0:T(8,128)S(1)}, f32[128,256]{1,0:T(8,128)S(1)}, u32[]{:S(2)}, u32[]{:S(2)}) collective-permute-start(f32[128,256]{1,0:T(8,128)S(1)} %get-tuple-element.69), channel_id=1, source_target_pairs={{0,3},{1,0},{2,1},{3,2},{4,7},{5,4},{6,5},{7,6},{8,11},{9,8},{10,9... | collective-permute-start | bytes 393224 | tf_op jit(solution)/shard_map/ppermute | solution.py:327
  60.0 2.9 %collective-permute-start.6 = (f32[32,128]{1,0:T(8,128)S(1)}, f32[32,128]{1,0:T(8,128)S(1)}, u32[]{:S(2)}, u32[]{:S(2)}) collective-permute-start(f32[32,128]{1,0:T(8,128)S(1)} %get-tuple-element.65.g0), channel_id=1, source_target_pairs={{0,3},{1,0},{2,1},{3,2},{4,7},{5,4},{6,5},{7,6},{8,11},{9,8},{10,9... | collective-permute-start | bytes 49160 | tf_op jit(solution)/shard_map/ppermute | solution.py:327
  61.4 4.1 %collective-permute-start.5 = (f32[32,128]{1,0:T(8,128)S(1)}, f32[32,128]{1,0:T(8,128)S(1)}, u32[]{:S(2)}, u32[]{:S(2)}) collective-permute-start(f32[32,128]{1,0:T(8,128)S(1)} %get-tuple-element.65.g0), channel_id=1, source_target_pairs={{0,2},{1,3},{2,0},{3,1},{4,6},{5,7},{6,4},{7,5},{8,10},{9,11},{10,... | collective-permute-start | bytes 49160 | tf_op jit(solution)/shard_map/ppermute | solution.py:327
  61.7 3.9 %collective-permute-start.4 = (f32[32,128]{1,0:T(8,128)S(1)}, f32[32,128]{1,0:T(8,128)S(1)}, u32[]{:S(2)}, u32[]{:S(2)}) collective-permute-start(f32[32,128]{1,0:T(8,128)S(1)} %get-tuple-element.65.g0), channel_id=1, source_target_pairs={{0,1},{1,2},{2,3},{3,0},{4,5},{5,6},{6,7},{7,4},{8,9},{9,10},{10,1... | collective-permute-start | bytes 49160 | tf_op jit(solution)/shard_map/ppermute | solution.py:327
  65.7 3.6 %collective-permute-start.11 = (f32[40,640]{1,0:T(8,128)S(1)}, f32[40,640]{1,0:T(8,128)S(1)}, u32[]{:S(2)}, u32[]{:S(2)}) collective-permute-start(f32[40,640]{1,0:T(8,128)S(1)} %get-tuple-element.75.p0), channel_id=1, source_target_pairs={{0,192},{32,224},{64,0},{96,32},{128,64},{160,96},{192,128},{224,1... | collective-permute-start | bytes 307208 | tf_op jit(solution)/shard_map/ppermute | solution.py:323
  66.6 5.0 %collective-permute-start.10 = (f32[40,640]{1,0:T(8,128)S(1)}, f32[40,640]{1,0:T(8,128)S(1)}, u32[]{:S(2)}, u32[]{:S(2)}) collective-permute-start(f32[40,640]{1,0:T(8,128)S(1)} %get-tuple-element.75.p0), channel_id=1, source_target_pairs={{0,128},{32,160},{64,192},{96,224},{128,0},{160,32},{192,64},{224,... | collective-permute-start | bytes 307208 | tf_op jit(solution)/shard_map/ppermute | solution.py:323
  67.9 4.8 %collective-permute-start.9 = (f32[40,640]{1,0:T(8,128)S(1)}, f32[40,640]{1,0:T(8,128)S(1)}, u32[]{:S(2)}, u32[]{:S(2)}) collective-permute-start(f32[40,640]{1,0:T(8,128)S(1)} %get-tuple-element.75.p0), channel_id=1, source_target_pairs={{0,64},{32,96},{64,128},{96,160},{128,192},{160,224},{192,0},{224,... | collective-permute-start | bytes 307208 | tf_op jit(solution)/shard_map/ppermute | solution.py:323
  72.7 11.5 %collective-permute-start.12 = (f32[256,256]{1,0:T(8,128)S(1)}, f32[256,256]{1,0:T(8,128)S(1)}, u32[]{:S(2)}, u32[]{:S(2)}) collective-permute-start(f32[256,256]{1,0:T(8,128)S(1)} %get-tuple-element.73), channel_id=1, source_target_pairs={{0,1},{1,2},{2,3},{3,0},{4,5},{5,6},{6,7},{7,4},{8,9},{9,10},{10,1... | collective-permute-start | bytes 786440 | tf_op jit(solution)/shard_map/ppermute | solution.py:327
  72.7 11.4 %collective-permute-start.13 = (f32[256,256]{1,0:T(8,128)S(1)}, f32[256,256]{1,0:T(8,128)S(1)}, u32[]{:S(2)}, u32[]{:S(2)}) collective-permute-start(f32[256,256]{1,0:T(8,128)S(1)} %get-tuple-element.74), channel_id=1, source_target_pairs={{0,3},{1,0},{2,1},{3,2},{4,7},{5,4},{6,5},{7,6},{8,11},{9,8},{10,9... | collective-permute-start | bytes 786440 | tf_op jit(solution)/shard_map/ppermute | solution.py:327
  75.4 6.5 %collective-permute-start.14 = (f32[40,640]{1,0:T(8,128)S(1)}, f32[40,640]{1,0:T(8,128)S(1)}, u32[]{:S(2)}, u32[]{:S(2)}) collective-permute-start(f32[40,640]{1,0:T(8,128)S(1)} %get-tuple-element.75.p0), channel_id=1, source_target_pairs={{0,32},{32,0},{64,96},{96,64},{128,160},{160,128},{192,224},{224,1... | collective-permute-start | bytes 307208 | tf_op jit(solution)/shard_map/ppermute | solution.py:357
  80.9 1.3 %collective-permute-start.15 = (f32[40,640]{1,0:T(8,128)S(1)}, f32[40,640]{1,0:T(8,128)S(1)}, u32[]{:S(2)}, u32[]{:S(2)}) collective-permute-start(f32[40,640]{1,0:T(8,128)S(1)} %collective-permute-done.9.p1), channel_id=1, source_target_pairs={{0,32},{32,0},{64,96},{96,64},{128,160},{160,128},{192,224},{224,1... | collective-permute-start | bytes 307208 | tf_op jit(solution)/shard_map/ppermute | solution.py:357
  80.9 1.5 %collective-permute-start.16 = (f32[40,640]{1,0:T(8,128)S(1)}, f32[40,640]{1,0:T(8,128)S(1)}, u32[]{:S(2)}, u32[]{:S(2)}) collective-permute-start(f32[40,640]{1,0:T(8,128)S(1)} %collective-permute-done.10.p2), channel_id=1, source_target_pairs={{0,32},{32,0},{64,96},{96,64},{128,160},{160,128},{192,224},{224,1... | collective-permute-start | bytes 307208 | tf_op jit(solution)/shard_map/ppermute | solution.py:357
  81.9 1.3 %collective-permute-start.17 = (f32[40,640]{1,0:T(8,128)S(1)}, f32[40,640]{1,0:T(8,128)S(1)}, u32[]{:S(2)}, u32[]{:S(2)}) collective-permute-start(f32[40,640]{1,0:T(8,128)S(1)} %collective-permute-done.11.p3), channel_id=1, source_target_pairs={{0,32},{32,0},{64,96},{96,64},{128,160},{160,128},{192,224},{224,1... | collective-permute-start | bytes 307208 | tf_op jit(solution)/shard_map/ppermute | solution.py:357
